TPU v7x, 512 devices: a whole 4x4x16 slice. The times are simulated.
512 devices in a mesh: dp: 8 (over z_lo), ctx: 8 (over z_hi, x), head: 8 (over y, core).
Axes of the slice: x: 4, y: 4, z: 16 (z_hi: 2, z_lo: 8; z = z_hi * 8 + z_lo), core: 2. Of those that a mesh axis runs over, the one named last changes fastest.
Arguments:
- queries: bfloat16 [8, 1024, 2048], P('dp', 'ctx', 'head')
- keyval: bfloat16 [8, 2, 1024, 1024], P('dp', None, 'ctx', 'head')
- attn_grad: bfloat16 [8, 1024, 2048], P('dp', 'ctx', 'head'), may hold values from -6 to 6
- doc_ids: int32 [8, 1024], P('dp', 'ctx'), may hold values from 0 to 3, never falling along the last dimension, each value on 1 to 512 neighbouring positions
- ssm_in: bfloat16 [8, 1024, 8192], P('dp', 'ctx', 'head'), may hold values from -6 to 6
- bc_pair: bfloat16 [8, 2, 1024, 128], P('dp', None, 'ctx'), may hold values from -0.625 to 0.625
- step_size: float32 [8, 128, 1024], P('dp', 'head', 'ctx'), as said below
- decay_rate: float32 [128], P('head'), may hold values from 0.5 to 2
- skip_gain: float32 [128], P('head'), may hold values from 0.5 to 1.5
- ssm_grad: bfloat16 [8, 1024, 8192], P('dp', 'ctx', 'head'), may hold values from -6 to 6
Outputs:
- query_grad: bfloat16 [8, 1024, 2048], P('dp', 'ctx', 'head')
- keyval_grad: bfloat16 [8, 2, 1024, 1024], P('dp', None, 'ctx', 'head')
- input_grad: bfloat16 [8, 1024, 8192], P('dp', 'ctx', 'head')
- shared_grad: float32 [8, 2, 1024, 128], P('dp', None, ('ctx', 'head'))
- step_grad: float32 [8, 128, 1024], P('dp', 'head', 'ctx')
- param_grads: float32 [2, 128], P(None, 'head')
Inputs may be any that keep to these rules, and one draw needn't show every extreme that they name: `step_size`: positive. `doc_ids`: document numbers of each sequence never fall; a document holds at most 512 positions and one holds exactly 512.
All inputs are finite; a program needn't handle non-finite values.
Results may differ from a plain program's by a relative error of at most 0.017.
Values may be sent and summed in bfloat16 or wider, within the bound.
No kernel may reach another device: no remote copies, remote signals or barrier semaphores. Data moves between devices by JAX's collectives and lax.ppermute only.
A program may use at most 64 MiB of HBM per device.

v0:
```python
import math

import jax
import jax.numpy as jnp
from jax import lax
from jax.sharding import PartitionSpec as P

TOK_DEV = 128
HEAD_WIDTH = 128
QUERY_PER_KV = 2
KV_DEV = 1
SSM_DEV = 16
PD = 64
NS = 128


HIGHEST_PRECISION = lax.Precision.HIGHEST
NEGATIVE = -1e30


def from_behind(value, axis, steps):
    count = lax.axis_size(axis)
    initial, last = (max(0, -steps), min(count, count - steps))
    return lax.ppermute(value, axis, [(source, source + steps) for source in range(initial, last)])


def shifted(x, axis, by):
    size = lax.axis_size(axis)
    return lax.ppermute(x, axis, [(i, (i + by) % size) for i in range(size)])


def prefix(value, axis, join, neutral, backward):
    count, mine = (lax.axis_size(axis), lax.axis_index(axis))
    pieces = jax.tree.map(lambda part: lax.all_gather(part, axis), value)
    if backward:
        pieces = jax.tree.map(lambda part: part[::-1], pieces)
        mine = count - 1 - mine
    total = jax.tree.map(
        lambda part, zero: jnp.full_like(part, 0) + jnp.asarray(zero, part.dtype), value, neutral
    )

    def lap(position, total):
        longer = join(total, jax.tree.map(lambda part: part[position], pieces))
        return jax.tree.map(lambda new, old: jnp.where(position < mine, new, old), longer, total)

    return lax.fori_loop(0, count - 1, lap, total)


def compose(earlier, later):
    return (earlier[0] * later[0], later[0][:, None, None] * earlier[1] + later[1])


def decay_terms(step_rows, doc_rows, doc_before, rate):
    number = doc_rows.shape[0]
    log_decay = -step_rows * rate[:, None]
    cumulative = jnp.cumsum(log_decay, axis=-1)
    ending = cumulative[:, -1]
    places = jnp.arange(number)
    joined = (places[None, :] <= places[:, None]) & (doc_rows[None, :] == doc_rows[:, None])
    spread = cumulative[:, :, None] - cumulative[:, None, :]
    weights = jnp.where(joined[None], jnp.exp(jnp.minimum(spread, 0.0)), 0.0)
    entering = jnp.where(doc_rows[None, :] == doc_before, jnp.exp(cumulative), 0.0)
    leaving = jnp.where(
        doc_rows[None, :] == doc_rows[-1], jnp.exp(ending[:, None] - cumulative), 0.0
    )
    through = (doc_rows[0] == doc_before) & (doc_rows[-1] == doc_rows[0])
    passage = jnp.where(through, jnp.exp(ending), 0.0)
    return (weights, entering, leaving, passage)


def body(
    queries, keyval, attn_grad, doc_ids, ssm_in, bc_pair, step_size, decay_rate, skip_gain, ssm_grad
):
    shards = lax.axis_size("ctx")
    place_index = lax.axis_index("ctx")
    scaling = HEAD_WIDTH ** (-0.5)
    row_count = QUERY_PER_KV * TOK_DEV
    seg_full = lax.all_gather(doc_ids, "ctx", axis=1, tiled=True)[0]
    doc_here = doc_ids[0]
    first_row = place_index * TOK_DEV
    query_rows = jnp.transpose(
        queries[0].reshape(TOK_DEV, KV_DEV, QUERY_PER_KV, HEAD_WIDTH), (1, 2, 0, 3)
    ).reshape(KV_DEV, row_count, HEAD_WIDTH)
    grad_rows = jnp.transpose(
        attn_grad[0].reshape(TOK_DEV, KV_DEV, QUERY_PER_KV, HEAD_WIDTH), (1, 2, 0, 3)
    ).reshape(KV_DEV, row_count, HEAD_WIDTH)

    def rows_of(shard_start, shard_docs):
        return (
            jnp.tile(shard_start + jnp.arange(TOK_DEV), QUERY_PER_KV),
            jnp.tile(shard_docs, QUERY_PER_KV),
        )

    row_place, row_doc = rows_of(first_row, doc_here)

    def admitted(query_place, query_doc, key_place, key_doc):
        return (key_place[None, :] <= query_place[:, None]) & (
            key_doc[None, :] == query_doc[:, None]
        )

    def split_pair(portion):
        number = portion.shape[2]
        return (
            portion[0, 0].reshape(number, KV_DEV, HEAD_WIDTH),
            portion[0, 1].reshape(number, KV_DEV, HEAD_WIDTH),
        )

    def tile_grads(query_side, key_rows, value_rows, key_place, key_doc):
        side_queries, side_grads, query_place, query_doc, logsum, row_delta = query_side
        allowed = admitted(query_place, query_doc, key_place, key_doc)[None]
        scores = (
            jnp.einsum("hre,khe->hrk", side_queries, key_rows, preferred_element_type=jnp.float32)
            * scaling
        )
        dot_grads = jnp.einsum(
            "hre,khe->hrk", side_grads, value_rows, preferred_element_type=jnp.float32
        )
        masked = jnp.where(allowed, scores, NEGATIVE)
        attention = jnp.where(allowed, jnp.exp(masked - logsum[..., None]), 0.0)
        rounded = attention.astype(jnp.bfloat16)
        dscore = (rounded.astype(jnp.float32) * (dot_grads - row_delta[..., None])).astype(
            jnp.bfloat16
        )
        query_part = (
            jnp.einsum("hrk,khe->hre", dscore, key_rows, preferred_element_type=jnp.float32)
            * scaling
        )
        key_part = (
            jnp.einsum("hrk,hre->khe", dscore, side_queries, preferred_element_type=jnp.float32)
            * scaling
        )
        value_part = jnp.einsum(
            "hrk,hre->khe", rounded, side_grads, preferred_element_type=jnp.float32
        )
        return (query_part, jnp.stack([key_part, value_part]))

    row_max = jnp.full((KV_DEV, row_count), NEGATIVE, jnp.float32)
    key_rows, value_rows = split_pair(lax.all_gather(keyval, "ctx", axis=2, tiled=True))
    number = key_rows.shape[0]
    allowed = admitted(row_place, row_doc, jnp.arange(number), seg_full)[None]
    scores = (
        jnp.einsum("hre,khe->hrk", query_rows, key_rows, preferred_element_type=jnp.float32)
        * scaling
    )
    dot_grads = jnp.einsum(
        "hre,khe->hrk", grad_rows, value_rows, preferred_element_type=jnp.float32
    )
    masked = jnp.where(allowed, scores, NEGATIVE)
    new_max = jnp.maximum(row_max, jnp.max(masked, axis=-1))
    expos = jnp.where(allowed, jnp.exp(masked - new_max[..., None]), 0.0)
    stats = (new_max, jnp.sum(expos, axis=-1), jnp.sum(expos * dot_grads, axis=-1))
    logsum = stats[0] + jnp.log(stats[1])
    row_delta = stats[2] / stats[1]
    own_keys, own_values = split_pair(keyval)
    own_place = first_row + jnp.arange(TOK_DEV)

    def contribute(holding, stats, offset):
        anchor = (place_index + offset) % shards

        def active(unused):
            travel_place, travel_doc = rows_of(
                anchor * TOK_DEV, lax.dynamic_slice_in_dim(seg_full, anchor * TOK_DEV, TOK_DEV)
            )
            query_side = (holding[0], holding[1], travel_place, travel_doc, stats[0], stats[1])
            return tile_grads(query_side, own_keys, own_values, own_place, doc_here)

        def resting(unused):
            return (
                jnp.zeros((KV_DEV, row_count, HEAD_WIDTH), jnp.float32),
                jnp.zeros((2, TOK_DEV, KV_DEV, HEAD_WIDTH), jnp.float32),
            )

        return lax.cond(place_index + offset < shards, active, resting, 0)

    def advance(offset, loop_state):
        holding, stats, carried, pair_total = loop_state
        query_part, pair_part = contribute(holding, stats, offset)
        holding = from_behind((holding[0], holding[1]), "ctx", -1)
        stats = from_behind((stats[0], stats[1]), "ctx", -1)
        carried = shifted((carried + query_part).astype(jnp.bfloat16), "ctx", -1).astype(
            jnp.float32
        )
        return (holding, stats, carried, pair_total + pair_part)

    start_state = (
        (query_rows, grad_rows),
        (logsum, row_delta),
        jnp.zeros((KV_DEV, row_count, HEAD_WIDTH), jnp.float32),
        jnp.zeros((2, TOK_DEV, KV_DEV, HEAD_WIDTH), jnp.float32),
    )
    holding, stats, carried, pair_total = lax.fori_loop(0, shards - 1, advance, start_state)
    query_part, pair_part = contribute(holding, stats, shards - 1)
    query_grad = shifted((carried + query_part).astype(jnp.bfloat16), "ctx", -1).astype(jnp.float32)
    pair_total = pair_total + pair_part
    keyval_grad = pair_total.reshape(1, 2, TOK_DEV, KV_DEV * HEAD_WIDTH).astype(jnp.bfloat16)
    query_out = jnp.transpose(
        query_grad.reshape(KV_DEV, QUERY_PER_KV, TOK_DEV, HEAD_WIDTH), (2, 0, 1, 3)
    )
    query_out = query_out.reshape(1, TOK_DEV, KV_DEV * QUERY_PER_KV * HEAD_WIDTH).astype(
        jnp.bfloat16
    )
    inputs = ssm_in[0].reshape(TOK_DEV, SSM_DEV, PD)
    out_grads = ssm_grad[0].reshape(TOK_DEV, SSM_DEV, PD)
    writes = bc_pair[0, 0]
    reads = bc_pair[0, 1]
    step_rows = step_size[0]
    doc_before = jnp.where(
        place_index > 0, lax.dynamic_slice_in_dim(seg_full, jnp.maximum(first_row - 1, 0), 1)[0], -1
    )
    weights, entering, leaving, passage = decay_terms(step_rows, doc_here, doc_before, decay_rate)
    inputs_wide = inputs.astype(jnp.float32)
    grads_wide = out_grads.astype(jnp.float32)
    write_wide = writes.astype(jnp.float32)
    read_wide = reads.astype(jnp.float32)
    scaled_in = jnp.transpose(leaving)[:, :, None] * inputs_wide
    scaled_grad = jnp.transpose(entering)[:, :, None] * grads_wide
    closing = jnp.einsum("sn,shp->hnp", write_wide, scaled_in, precision=HIGHEST_PRECISION)
    opening = jnp.einsum("tn,thp->hnp", read_wide, scaled_grad, precision=HIGHEST_PRECISION)
    identity = (jnp.ones((SSM_DEV,), jnp.float32), jnp.zeros((SSM_DEV, NS, PD), jnp.float32))
    state_in = prefix((passage, closing), "ctx", compose, identity, False)[1]
    grad_in = prefix((passage, opening), "ctx", compose, identity, True)[1]
    affinity = jnp.dot(reads, jnp.transpose(writes), preferred_element_type=jnp.float32)
    pairing = jnp.einsum("thp,shp->hts", out_grads, inputs, preferred_element_type=jnp.float32)
    mixing = weights * affinity[None]
    paired = weights * pairing
    back_state = jnp.einsum("sn,hnp->shp", write_wide, grad_in, precision=HIGHEST_PRECISION)
    forward_read = jnp.einsum("tn,hnp->thp", read_wide, state_in, precision=HIGHEST_PRECISION)
    input_grad = (
        jnp.einsum("hts,thp->shp", mixing, grads_wide, precision=HIGHEST_PRECISION)
        + jnp.transpose(leaving)[:, :, None] * back_state
        + skip_gain[None, :, None] * grads_wide
    )
    write_grad = jnp.einsum(
        "hts,tn->sn", paired, read_wide, precision=HIGHEST_PRECISION
    ) + jnp.einsum("shp,hnp->sn", scaled_in, grad_in, precision=HIGHEST_PRECISION)
    read_grad = jnp.einsum(
        "hts,sn->tn", paired, write_wide, precision=HIGHEST_PRECISION
    ) + jnp.einsum("thp,hnp->tn", scaled_grad, state_in, precision=HIGHEST_PRECISION)
    triple = paired * affinity[None]
    places = jnp.arange(TOK_DEV)
    earlier = jnp.cumsum(triple, axis=2) - triple
    inside = jnp.sum(jnp.where((places[:, None] >= places[None, :])[None], earlier, 0.0), axis=1)
    enter_term = entering * jnp.transpose(jnp.sum(forward_read * grads_wide, axis=-1))
    leave_term = leaving * jnp.transpose(jnp.sum(back_state * inputs_wide, axis=-1))
    enter_sum = jnp.flip(jnp.cumsum(jnp.flip(enter_term, -1), -1), -1)
    leave_sum = jnp.cumsum(leave_term, -1) - leave_term
    across = passage * jnp.sum(state_in * grad_in, axis=(1, 2))
    log_grad = inside + enter_sum + leave_sum + across[:, None]
    step_grad = (-decay_rate[:, None] * log_grad)[None]
    rate_term = jnp.sum(-step_rows * log_grad, axis=-1)
    skip_term = jnp.sum(inputs_wide * grads_wide, axis=(0, 2))
    input_out = input_grad.reshape(1, TOK_DEV, SSM_DEV * PD).astype(jnp.bfloat16)
    shared_out = lax.psum_scatter(
        jnp.stack([write_grad, read_grad]).astype(jnp.bfloat16),
        "head",
        scatter_dimension=1,
        tiled=True,
    ).astype(jnp.float32)[None]
    totals = lax.psum(jnp.stack([rate_term, skip_term]), ("dp", "ctx"))
    param_out = totals / math.sqrt(lax.axis_size("dp") * TOK_DEV * shards * PD)
    return (query_out, keyval_grad, input_out, shared_out, step_grad, param_out)


def solution(mesh):
    placed = (
        P("dp", "ctx", "head"),
        P("dp", None, "ctx", "head"),
        P("dp", "ctx", "head"),
        P("dp", "ctx"),
        P("dp", "ctx", "head"),
        P("dp", None, "ctx", None),
        P("dp", "head", "ctx"),
        P("head"),
        P("head"),
        P("dp", "ctx", "head"),
    )
    return jax.shard_map(
        body,
        mesh=mesh,
        in_specs=placed,
        out_specs=(
            P("dp", "ctx", "head"),
            P("dp", None, "ctx", "head"),
            P("dp", "ctx", "head"),
            P("dp", None, ("ctx", "head"), None),
            P("dp", "head", "ctx"),
            P(None, "head"),
        ),
        check_vma=False,
    )
```

profile of v0, /device:TPU:1, one launch (start us, length us, event | category | flops | bytes accessed | tf_op | source)
XLA Modules:
  0.0 952.7 jit_solution(8767642057807582961)
XLA Ops:
  7.2 45.7 %all_gather.24 = s32[1,1024]{1,0:T(1,128)S(1)} all-gather(s32[1,128]{1,0:T(1,128)} %param.23), channel_id=1, replica_groups=mesh['dp'=8,'ctx'=8,'head'=8] {'ctx'}, dimensions={1}, use_global_device_ids=true | all-gather | bytes 4608 | tf_op jit(solution)/shard_map/all_gather | solution.py:78
  52.9 1.3 fusion.86
  57.4 1.3 compare_bitcast_fusion.1
  63.8 2.0 convolution_bitcast_fusion.3
  65.8 1.9 convolution_bitcast_fusion.2
  67.8 72.5 %all_gather.25 = bf16[1,2,1024,128]{3,2,1,0:T(8,128)(2,1)S(1)} all-gather(bf16[1,2,128,128]{3,2,1,0:T(8,128)(2,1)} %param.21), channel_id=1, replica_groups=mesh['dp'=8,'ctx'=8,'head'=8] {'ctx'}, dimensions={2}, use_global_device_ids=true | all-gather | bytes 589824 | tf_op jit(solution)/shard_map/all_gather | solution.py:138
  144.3 272.2 %while.54 = (s32[]{:T(128)}, bf16[1,256,128]{2,1,0:T(8,128)(2,1)S(1)}, bf16[1,256,128]{2,1,0:T(8,128)(2,1)S(1)}, f32[1,256]{1,0:T(1,128)S(1)}, f32[1,256]{1,0:T(...) while((s32[]{:T(128)}, ...), condition=%wide.region_6.7_spmd.clone, body=%wide.region_3.6_spmd.clone.sunk | while | flops 42615060 | bytes 3268241 | solution.py:191
  151.8 4.4 conditional.5
  156.3 5.9 collective-permute-start.4
  162.2 6.5 collective-permute-done.4
  176.3 4.4 conditional.5
  180.8 27.2 %collective-permute-start.4 = (bf16[1,256,128]{2,1,0:T(8,128)(2,1)S(1)}, bf16[1,256,128]{2,1,0:T(8,128)(2,1)S(1)}, u32[]{:S(2)}, u32[]{:S(2)}) collective-permute-start(bf16[1,256,128]{2,1,0:T(8,128)(2,1)S(1)} %fusion.112), channel_id=1, source_target_pairs={{0,56},{8,0},{16,8},{24,16},{32,24},{40,32},{48,40},{56,48},{1,57}... | collective-permute-start | bytes 196616 | tf_op jit(solution)/shard_map/while/body/eval_jaxpr/ppermute | solution.py:29
  208.1 25.7 %collective-permute-done.4 = bf16[1,256,128]{2,1,0:T(8,128)(2,1)S(1)} collective-permute-done((bf16[1,256,128]{2,1,0:T(8,128)(2,1)S(1)}, bf16[1,256,128]{2,1,0:T(8,128)(2,1)S(1)}, u32[]{:S(2)}, u32[]{:S(2)}) %collective-permute-start.4) | collective-permute-done | bytes 65568 | tf_op jit(solution)/shard_map/while/body/eval_jaxpr/ppermute | solution.py:29
  241.5 4.4 conditional.5
  245.9 34.1 %collective-permute-start.4 = (bf16[1,256,128]{2,1,0:T(8,128)(2,1)S(1)}, bf16[1,256,128]{2,1,0:T(8,128)(2,1)S(1)}, u32[]{:S(2)}, u32[]{:S(2)}) collective-permute-start(bf16[1,256,128]{2,1,0:T(8,128)(2,1)S(1)} %fusion.112), channel_id=1, source_target_pairs={{0,56},{8,0},{16,8},{24,16},{32,24},{40,32},{48,40},{56,48},{1,57}... | collective-permute-start | bytes 196616 | tf_op jit(solution)/shard_map/while/body/eval_jaxpr/ppermute | solution.py:29
  289.0 4.4 conditional.5
  293.5 17.1 %collective-permute-start.4 = (bf16[1,256,128]{2,1,0:T(8,128)(2,1)S(1)}, bf16[1,256,128]{2,1,0:T(8,128)(2,1)S(1)}, u32[]{:S(2)}, u32[]{:S(2)}) collective-permute-start(bf16[1,256,128]{2,1,0:T(8,128)(2,1)S(1)} %fusion.112), channel_id=1, source_target_pairs={{0,56},{8,0},{16,8},{24,16},{32,24},{40,32},{48,40},{56,48},{1,57}... | collective-permute-start | bytes 196616 | tf_op jit(solution)/shard_map/while/body/eval_jaxpr/ppermute | solution.py:29
  310.6 2.6 collective-permute-done.4
  320.8 4.4 conditional.5
  325.3 15.8 %collective-permute-start.4 = (bf16[1,256,128]{2,1,0:T(8,128)(2,1)S(1)}, bf16[1,256,128]{2,1,0:T(8,128)(2,1)S(1)}, u32[]{:S(2)}, u32[]{:S(2)}) collective-permute-start(bf16[1,256,128]{2,1,0:T(8,128)(2,1)S(1)} %fusion.112), channel_id=1, source_target_pairs={{0,56},{8,0},{16,8},{24,16},{32,24},{40,32},{48,40},{56,48},{1,57}... | collective-permute-start | bytes 196616 | tf_op jit(solution)/shard_map/while/body/eval_jaxpr/ppermute | solution.py:29
  341.2 4.0 collective-permute-done.4
  352.8 4.4 conditional.5
  357.3 20.7 %collective-permute-start.4 = (bf16[1,256,128]{2,1,0:T(8,128)(2,1)S(1)}, bf16[1,256,128]{2,1,0:T(8,128)(2,1)S(1)}, u32[]{:S(2)}, u32[]{:S(2)}) collective-permute-start(bf16[1,256,128]{2,1,0:T(8,128)(2,1)S(1)} %fusion.112), channel_id=1, source_target_pairs={{0,56},{8,0},{16,8},{24,16},{32,24},{40,32},{48,40},{56,48},{1,57}... | collective-permute-start | bytes 196616 | tf_op jit(solution)/shard_map/while/body/eval_jaxpr/ppermute | solution.py:29
  378.1 7.6 collective-permute-done.4
  393.3 4.4 conditional.5
  397.8 10.5 %collective-permute-start.4 = (bf16[1,256,128]{2,1,0:T(8,128)(2,1)S(1)}, bf16[1,256,128]{2,1,0:T(8,128)(2,1)S(1)}, u32[]{:S(2)}, u32[]{:S(2)}) collective-permute-start(bf16[1,256,128]{2,1,0:T(8,128)(2,1)S(1)} %fusion.112), channel_id=1, source_target_pairs={{0,56},{8,0},{16,8},{24,16},{32,24},{40,32},{48,40},{56,48},{1,57}... | collective-permute-start | bytes 196616 | tf_op jit(solution)/shard_map/while/body/eval_jaxpr/ppermute | solution.py:29
  408.4 8.0 collective-permute-done.4
  418.2 13.9 %collective-permute-start.5 = (bf16[1,256,128]{2,1,0:T(8,128)(2,1)}, bf16[1,256,128]{2,1,0:T(8,128)(2,1)}, u32[]{:S(2)}, u32[]{:S(2)}) collective-permute-start(bf16[1,256,128]{2,1,0:T(8,128)(2,1)} %add_convert_fusion), channel_id=1, source_target_pairs={{0,56},{8,0},{16,8},{24,16},{32,24},{40,32},{48,40},{56,48},{1,57}... | collective-permute-start | bytes 196616 | tf_op jit(solution)/shard_map/ppermute | solution.py:29
  434.1 23.3 %fusion.88 = f32[16,128,128]{1,0,2:T(8,128)S(1)} fusion(f32[16,128,128]{1,0,2:T(8,128)S(1)} %copy.89), kind=kOutput, calls=%fused_computation.170 | output fusion | flops 33292288 | bytes 2097152 | tf_op jit(solution)/shard_map/jit(cumsum)/reduce_window_sum | solution.py:241
  457.9 1.6 fusion.61
  461.3 1.3 dynamic-slice.1
  464.1 31.8 %all-reduce = f32[128]{0:T(128)S(1)} all-reduce(f32[128]{0:T(128)S(1)} %dynamic-update-slice), channel_id=2, replica_groups=mesh['dp'=8,'ctx'=8,'head'=8] {'ctx'}, use_global_device_ids=true, to_apply=%add | all-reduce | flops 128 | bytes 1024
  499.6 6.9 copy.82
  506.5 7.7 rev.14
  514.2 10.5 %while.55 = (s32[]{:T(128)}, f32[16,128,64]{2,1,0:T(8,128)S(1)}, s32[]{:T(128)}, f32[8,16]{1,0:T(8,128)S(1)}, f32[8,16,128,64]{3,2,1,0:T(8,128)}, /*index=5*/s32[]{:T(128)}, s32[]{:T(128)}) while((s32[]{:T(128)}, f32[16,128,64]{2,1,0:T(8,128)S(1)}, s32[]{:T(128)}, f32[8,16]{1,0:T(8,128)S(1)}, f32[8,16,128,64]{3,2,1,0:T(8,128)}, ...), condition=%wide.region_11.12_spmd.clone, body=%wide.region_10.11_spmd.clone.sunk | while | flops 524292 | bytes 1573161 | solution.py:46
  514.3 1.5 fusion.113
  515.8 1.5 fusion.113
  517.3 1.5 fusion.113
  518.8 1.5 fusion.113
  520.3 1.5 fusion.113
  521.8 1.5 fusion.113
  523.3 1.5 fusion.113
  524.8 2.4 fusion.51
  527.1 37.8 %while.56 = (s32[]{:T(128)}, f32[16,128,64]{2,1,0:T(8,128)S(1)}, s32[]{:T(128)}, f32[8,16]{1,0:T(8,128)}, f32[8,16,128,64]{2,3,1,0:T(8,128)}, /*index=5*/s32[]{:T(128)}, s32[]{:T(128)}) while((s32[]{:T(128)}, f32[16,128,64]{2,1,0:T(8,128)S(1)}, s32[]{:T(128)}, f32[8,16]{1,0:T(8,128)}, f32[8,16,128,64]{2,3,1,0:T(8,128)}, ...), condition=%wide.region_14.15_spmd.clone, body=%wide.region_13.14_spmd.clone.sunk | while | flops 524292 | bytes 3670313 | solution.py:46
  527.1 1.9 constant_dynamic-slice_fusion.3
  529.1 1.4 copy.102
  532.6 1.9 constant_dynamic-slice_fusion.3
  534.5 1.4 copy.102
  538.0 1.9 constant_dynamic-slice_fusion.3
  539.9 1.4 copy.102
  543.4 1.9 constant_dynamic-slice_fusion.3
  545.3 1.4 copy.102
  548.7 1.9 constant_dynamic-slice_fusion.3
  550.7 1.4 copy.102
  554.1 1.9 constant_dynamic-slice_fusion.3
  556.1 1.4 copy.102
  559.5 1.9 constant_dynamic-slice_fusion.3
  561.4 1.4 copy.102
  564.9 2.0 fusion.43
  567.1 1.8 convolution_bitcast_fusion.8
  569.0 2.8 convolution_bitcast_fusion.7
  575.1 219.9 %psum.7 = f32[2,16]{1,0:T(2,128)S(1)} all-reduce(f32[2,16]{1,0:T(2,128)S(1)} %pad_maximum_fusion.3), channel_id=1, replica_groups=mesh['dp'=8,'ctx'=8,'head'=8] {'dp','ctx'}, use_global_device_ids=true, to_apply=%region_26.27 | all-reduce | flops 32 | bytes 256 | tf_op jit(solution)/shard_map/psum | solution.py:259
  796.1 2.2 fusion.42
  800.4 144.5 %reduce-scatter.2.cloned.1.call-done = bf16[2,16,128]{2,1,0:T(8,128)(2,1)} async-done(((bf16[2,128,128]{2,1,0:T(8,128)(2,1)}), bf16[2,16,128]{2,1,0:T(8,128)(2,1)}) %reduce-scatter.2.cloned.1.call-update) | async-done | bytes 8208 | tf_op jit(solution)/shard_map/reduce_scatter | solution.py:253
  (311 shorter events, 129.0 us)
Async XLA Ops:
  7.2 137.1 %copy-start.8 = (s32[1,128]{1,0:T(1,128)S(1)}, s32[1,128]{1,0:T(1,128)}, u32[]{:S(2)}) copy-start(s32[1,128]{1,0:T(1,128)} %param.23) | copy-start | bytes 1540
  7.2 136.0 %copy-start.6 = (bf16[1,128,256]{2,1,0:T(8,128)(2,1)S(1)}, bf16[1,128,256]{2,1,0:T(8,128)(2,1)}, u32[]{:S(2)}) copy-start(bf16[1,128,256]{2,1,0:T(8,128)(2,1)} %param.22) | copy-start | bytes 196612
  7.2 492.5 %all-gather.6.cloned.1.call-start = ((), (), s32[]{:S(2)}) async-start(), calls=%async_computation.2 | async-start | bytes 4718592 | tf_op jit(solution)/shard_map/all_gather | solution.py:34
  58.7 82.4 %copy-start.11 = (pred[128]{0:T(512)(128)(4,1)}, pred[128]{0:T(512)(128)(4,1)S(1)}, u32[]{:S(2)}) copy-start(pred[128]{0:T(512)(128)(4,1)S(1)} %get-tuple-element.930) | copy-start | bytes 388
  58.7 82.4 %copy-start.12 = (pred[128]{0:T(512)(128)(4,1)}, pred[128]{0:T(512)(128)(4,1)S(1)}, u32[]{:S(2)}) copy-start(pred[128]{0:T(512)(128)(4,1)S(1)} %get-tuple-element.931) | copy-start | bytes 388
  59.8 372.6 %copy-start = (bf16[1,128,1024]{1,2,0:T(8,128)(2,1)}, bf16[1,128,1024]{1,2,0:T(8,128)(2,1)S(1)}, u32[]{:S(2)}) copy-start(bf16[1,128,1024]{1,2,0:T(8,128)(2,1)S(1)} %copy.80) | copy-start | bytes 786436
  62.9 78.2 %copy-start.13 = (f32[16]{0:T(128)}, f32[16]{0:T(128)S(1)}, u32[]{:S(2)}) copy-start(f32[16]{0:T(128)S(1)} %get-tuple-element.863) | copy-start | bytes 196
  63.0 78.1 %copy-start.5 = (f32[128,16]{0,1:T(8,128)}, f32[128,16]{0,1:T(8,128)S(1)}, u32[]{:S(2)}) copy-start(f32[128,16]{0,1:T(8,128)S(1)} %get-tuple-element.927) | copy-start | bytes 24580
  65.7 461.4 %all-gather.8.cloned.1.call-start = ((), (), s32[]{:S(2)}) async-start(), calls=%async_computation.3 | async-start | bytes 4718592 | tf_op jit(solution)/shard_map/all_gather | solution.py:34
  67.8 877.1 %reduce-scatter.2.cloned.1.call-start = ((), (), s32[]{:S(2)}) async-start(), calls=%async_computation.1 | async-start | bytes 73728 | tf_op jit(solution)/shard_map/reduce_scatter | solution.py:253
  144.2 288.0 %copy-start.1 = (bf16[1,2,128,128]{3,2,1,0:T(8,128)(2,1)S(1)}, bf16[1,2,128,128]{3,2,1,0:T(8,128)(2,1)}, u32[]{:S(2)}) copy-start(bf16[1,2,128,128]{3,2,1,0:T(8,128)(2,1)} %param.25) | copy-start | bytes 196612
  144.9 23.8 %collective-permute-start = (bf16[1,256,128]{2,1,0:T(8,128)(2,1)}, bf16[1,256,128]{2,1,0:T(8,128)(2,1)S(1)}, u32[]{:S(2)}, u32[]{:S(2)}) collective-permute-start(bf16[1,256,128]{2,1,0:T(8,128)(2,1)} %copy.115), channel_id=1, source_target_pairs={{8,0},{16,8},{24,16},{32,24},{40,32},{48,40},{56,48},{9,1},{17,9},... | collective-permute-start | bytes 196616 | tf_op jit(solution)/shard_map/while/body/eval_jaxpr/ppermute | solution.py:24
  146.8 21.9 %collective-permute-start.1 = (bf16[1,256,128]{2,1,0:T(8,128)(2,1)}, bf16[1,256,128]{2,1,0:T(8,128)(2,1)S(1)}, u32[]{:S(2)}, u32[]{:S(2)}) collective-permute-start(bf16[1,256,128]{2,1,0:T(8,128)(2,1)} %copy.116), channel_id=1, source_target_pairs={{8,0},{16,8},{24,16},{32,24},{40,32},{48,40},{56,48},{9,1},{17,9},... | collective-permute-start | bytes 196616 | tf_op jit(solution)/shard_map/while/body/eval_jaxpr/ppermute | solution.py:24
  148.7 20.0 %collective-permute-start.2 = (f32[1,256]{1,0:T(1,128)}, f32[1,256]{1,0:T(1,128)S(1)}, u32[]{:S(2)}, u32[]{:S(2)}) collective-permute-start(f32[1,256]{1,0:T(1,128)} %copy.117), channel_id=1, source_target_pairs={{8,0},{16,8},{24,16},{32,24},{40,32},{48,40},{56,48},{9,1},{17,9},... | collective-permute-start | bytes 3080 | tf_op jit(solution)/shard_map/while/body/eval_jaxpr/ppermute | solution.py:24
  150.5 18.2 %collective-permute-start.3 = (f32[1,256]{1,0:T(1,128)}, f32[1,256]{1,0:T(1,128)S(1)}, u32[]{:S(2)}, u32[]{:S(2)}) collective-permute-start(f32[1,256]{1,0:T(1,128)} %copy.118), channel_id=1, source_target_pairs={{8,0},{16,8},{24,16},{32,24},{40,32},{48,40},{56,48},{9,1},{17,9},... | collective-permute-start | bytes 3080 | tf_op jit(solution)/shard_map/while/body/eval_jaxpr/ppermute | solution.py:24
  156.3 12.4 %collective-permute-start.4 = (bf16[1,256,128]{2,1,0:T(8,128)(2,1)S(1)}, bf16[1,256,128]{2,1,0:T(8,128)(2,1)S(1)}, u32[]{:S(2)}, u32[]{:S(2)}) collective-permute-start(bf16[1,256,128]{2,1,0:T(8,128)(2,1)S(1)} %fusion.112), channel_id=1, source_target_pairs={{0,56},{8,0},{16,8},{24,16},{32,24},{40,32},{48,40},{56,48},{1,57}... | collective-permute-start | bytes 196616 | tf_op jit(solution)/shard_map/while/body/eval_jaxpr/ppermute | solution.py:29
  169.4 64.5 %collective-permute-start = (bf16[1,256,128]{2,1,0:T(8,128)(2,1)}, bf16[1,256,128]{2,1,0:T(8,128)(2,1)S(1)}, u32[]{:S(2)}, u32[]{:S(2)}) collective-permute-start(bf16[1,256,128]{2,1,0:T(8,128)(2,1)} %copy.115), channel_id=1, source_target_pairs={{8,0},{16,8},{24,16},{32,24},{40,32},{48,40},{56,48},{9,1},{17,9},... | collective-permute-start | bytes 196616 | tf_op jit(solution)/shard_map/while/body/eval_jaxpr/ppermute | solution.py:24
  171.3 62.5 %collective-permute-start.1 = (bf16[1,256,128]{2,1,0:T(8,128)(2,1)}, bf16[1,256,128]{2,1,0:T(8,128)(2,1)S(1)}, u32[]{:S(2)}, u32[]{:S(2)}) collective-permute-start(bf16[1,256,128]{2,1,0:T(8,128)(2,1)} %copy.116), channel_id=1, source_target_pairs={{8,0},{16,8},{24,16},{32,24},{40,32},{48,40},{56,48},{9,1},{17,9},... | collective-permute-start | bytes 196616 | tf_op jit(solution)/shard_map/while/body/eval_jaxpr/ppermute | solution.py:24
  173.2 60.7 %collective-permute-start.2 = (f32[1,256]{1,0:T(1,128)}, f32[1,256]{1,0:T(1,128)S(1)}, u32[]{:S(2)}, u32[]{:S(2)}) collective-permute-start(f32[1,256]{1,0:T(1,128)} %copy.117), channel_id=1, source_target_pairs={{8,0},{16,8},{24,16},{32,24},{40,32},{48,40},{56,48},{9,1},{17,9},... | collective-permute-start | bytes 3080 | tf_op jit(solution)/shard_map/while/body/eval_jaxpr/ppermute | solution.py:24
  175.0 58.8 %collective-permute-start.3 = (f32[1,256]{1,0:T(1,128)}, f32[1,256]{1,0:T(1,128)S(1)}, u32[]{:S(2)}, u32[]{:S(2)}) collective-permute-start(f32[1,256]{1,0:T(1,128)} %copy.118), channel_id=1, source_target_pairs={{8,0},{16,8},{24,16},{32,24},{40,32},{48,40},{56,48},{9,1},{17,9},... | collective-permute-start | bytes 3080 | tf_op jit(solution)/shard_map/while/body/eval_jaxpr/ppermute | solution.py:24
  180.8 53.0 %collective-permute-start.4 = (bf16[1,256,128]{2,1,0:T(8,128)(2,1)S(1)}, bf16[1,256,128]{2,1,0:T(8,128)(2,1)S(1)}, u32[]{:S(2)}, u32[]{:S(2)}) collective-permute-start(bf16[1,256,128]{2,1,0:T(8,128)(2,1)S(1)} %fusion.112), channel_id=1, source_target_pairs={{0,56},{8,0},{16,8},{24,16},{32,24},{40,32},{48,40},{56,48},{1,57}... | collective-permute-start | bytes 196616 | tf_op jit(solution)/shard_map/while/body/eval_jaxpr/ppermute | solution.py:29
  234.5 46.9 %collective-permute-start = (bf16[1,256,128]{2,1,0:T(8,128)(2,1)}, bf16[1,256,128]{2,1,0:T(8,128)(2,1)S(1)}, u32[]{:S(2)}, u32[]{:S(2)}) collective-permute-start(bf16[1,256,128]{2,1,0:T(8,128)(2,1)} %copy.115), channel_id=1, source_target_pairs={{8,0},{16,8},{24,16},{32,24},{40,32},{48,40},{56,48},{9,1},{17,9},... | collective-permute-start | bytes 196616 | tf_op jit(solution)/shard_map/while/body/eval_jaxpr/ppermute | solution.py:24
  236.4 45.0 %collective-permute-start.1 = (bf16[1,256,128]{2,1,0:T(8,128)(2,1)}, bf16[1,256,128]{2,1,0:T(8,128)(2,1)S(1)}, u32[]{:S(2)}, u32[]{:S(2)}) collective-permute-start(bf16[1,256,128]{2,1,0:T(8,128)(2,1)} %copy.116), channel_id=1, source_target_pairs={{8,0},{16,8},{24,16},{32,24},{40,32},{48,40},{56,48},{9,1},{17,9},... | collective-permute-start | bytes 196616 | tf_op jit(solution)/shard_map/while/body/eval_jaxpr/ppermute | solution.py:24
  238.3 43.1 %collective-permute-start.2 = (f32[1,256]{1,0:T(1,128)}, f32[1,256]{1,0:T(1,128)S(1)}, u32[]{:S(2)}, u32[]{:S(2)}) collective-permute-start(f32[1,256]{1,0:T(1,128)} %copy.117), channel_id=1, source_target_pairs={{8,0},{16,8},{24,16},{32,24},{40,32},{48,40},{56,48},{9,1},{17,9},... | collective-permute-start | bytes 3080 | tf_op jit(solution)/shard_map/while/body/eval_jaxpr/ppermute | solution.py:24
  240.2 41.2 %collective-permute-start.3 = (f32[1,256]{1,0:T(1,128)}, f32[1,256]{1,0:T(1,128)S(1)}, u32[]{:S(2)}, u32[]{:S(2)}) collective-permute-start(f32[1,256]{1,0:T(1,128)} %copy.118), channel_id=1, source_target_pairs={{8,0},{16,8},{24,16},{32,24},{40,32},{48,40},{56,48},{9,1},{17,9},... | collective-permute-start | bytes 3080 | tf_op jit(solution)/shard_map/while/body/eval_jaxpr/ppermute | solution.py:24
  245.9 35.4 %collective-permute-start.4 = (bf16[1,256,128]{2,1,0:T(8,128)(2,1)S(1)}, bf16[1,256,128]{2,1,0:T(8,128)(2,1)S(1)}, u32[]{:S(2)}, u32[]{:S(2)}) collective-permute-start(bf16[1,256,128]{2,1,0:T(8,128)(2,1)S(1)} %fusion.112), channel_id=1, source_target_pairs={{0,56},{8,0},{16,8},{24,16},{32,24},{40,32},{48,40},{56,48},{1,57}... | collective-permute-start | bytes 196616 | tf_op jit(solution)/shard_map/while/body/eval_jaxpr/ppermute | solution.py:29
  282.1 31.1 %collective-permute-start = (bf16[1,256,128]{2,1,0:T(8,128)(2,1)}, bf16[1,256,128]{2,1,0:T(8,128)(2,1)S(1)}, u32[]{:S(2)}, u32[]{:S(2)}) collective-permute-start(bf16[1,256,128]{2,1,0:T(8,128)(2,1)} %copy.115), channel_id=1, source_target_pairs={{8,0},{16,8},{24,16},{32,24},{40,32},{48,40},{56,48},{9,1},{17,9},... | collective-permute-start | bytes 196616 | tf_op jit(solution)/shard_map/while/body/eval_jaxpr/ppermute | solution.py:24
  284.0 29.2 %collective-permute-start.1 = (bf16[1,256,128]{2,1,0:T(8,128)(2,1)}, bf16[1,256,128]{2,1,0:T(8,128)(2,1)S(1)}, u32[]{:S(2)}, u32[]{:S(2)}) collective-permute-start(bf16[1,256,128]{2,1,0:T(8,128)(2,1)} %copy.116), channel_id=1, source_target_pairs={{8,0},{16,8},{24,16},{32,24},{40,32},{48,40},{56,48},{9,1},{17,9},... | collective-permute-start | bytes 196616 | tf_op jit(solution)/shard_map/while/body/eval_jaxpr/ppermute | solution.py:24
  285.9 27.3 %collective-permute-start.2 = (f32[1,256]{1,0:T(1,128)}, f32[1,256]{1,0:T(1,128)S(1)}, u32[]{:S(2)}, u32[]{:S(2)}) collective-permute-start(f32[1,256]{1,0:T(1,128)} %copy.117), channel_id=1, source_target_pairs={{8,0},{16,8},{24,16},{32,24},{40,32},{48,40},{56,48},{9,1},{17,9},... | collective-permute-start | bytes 3080 | tf_op jit(solution)/shard_map/while/body/eval_jaxpr/ppermute | solution.py:24
  287.7 25.5 %collective-permute-start.3 = (f32[1,256]{1,0:T(1,128)}, f32[1,256]{1,0:T(1,128)S(1)}, u32[]{:S(2)}, u32[]{:S(2)}) collective-permute-start(f32[1,256]{1,0:T(1,128)} %copy.118), channel_id=1, source_target_pairs={{8,0},{16,8},{24,16},{32,24},{40,32},{48,40},{56,48},{9,1},{17,9},... | collective-permute-start | bytes 3080 | tf_op jit(solution)/shard_map/while/body/eval_jaxpr/ppermute | solution.py:24
  293.5 19.7 %collective-permute-start.4 = (bf16[1,256,128]{2,1,0:T(8,128)(2,1)S(1)}, bf16[1,256,128]{2,1,0:T(8,128)(2,1)S(1)}, u32[]{:S(2)}, u32[]{:S(2)}) collective-permute-start(bf16[1,256,128]{2,1,0:T(8,128)(2,1)S(1)} %fusion.112), channel_id=1, source_target_pairs={{0,56},{8,0},{16,8},{24,16},{32,24},{40,32},{48,40},{56,48},{1,57}... | collective-permute-start | bytes 196616 | tf_op jit(solution)/shard_map/while/body/eval_jaxpr/ppermute | solution.py:29
  313.9 31.3 %collective-permute-start = (bf16[1,256,128]{2,1,0:T(8,128)(2,1)}, bf16[1,256,128]{2,1,0:T(8,128)(2,1)S(1)}, u32[]{:S(2)}, u32[]{:S(2)}) collective-permute-start(bf16[1,256,128]{2,1,0:T(8,128)(2,1)} %copy.115), channel_id=1, source_target_pairs={{8,0},{16,8},{24,16},{32,24},{40,32},{48,40},{56,48},{9,1},{17,9},... | collective-permute-start | bytes 196616 | tf_op jit(solution)/shard_map/while/body/eval_jaxpr/ppermute | solution.py:24
  315.8 29.4 %collective-permute-start.1 = (bf16[1,256,128]{2,1,0:T(8,128)(2,1)}, bf16[1,256,128]{2,1,0:T(8,128)(2,1)S(1)}, u32[]{:S(2)}, u32[]{:S(2)}) collective-permute-start(bf16[1,256,128]{2,1,0:T(8,128)(2,1)} %copy.116), channel_id=1, source_target_pairs={{8,0},{16,8},{24,16},{32,24},{40,32},{48,40},{56,48},{9,1},{17,9},... | collective-permute-start | bytes 196616 | tf_op jit(solution)/shard_map/while/body/eval_jaxpr/ppermute | solution.py:24
  317.7 27.5 %collective-permute-start.2 = (f32[1,256]{1,0:T(1,128)}, f32[1,256]{1,0:T(1,128)S(1)}, u32[]{:S(2)}, u32[]{:S(2)}) collective-permute-start(f32[1,256]{1,0:T(1,128)} %copy.117), channel_id=1, source_target_pairs={{8,0},{16,8},{24,16},{32,24},{40,32},{48,40},{56,48},{9,1},{17,9},... | collective-permute-start | bytes 3080 | tf_op jit(solution)/shard_map/while/body/eval_jaxpr/ppermute | solution.py:24
  319.5 25.7 %collective-permute-start.3 = (f32[1,256]{1,0:T(1,128)}, f32[1,256]{1,0:T(1,128)S(1)}, u32[]{:S(2)}, u32[]{:S(2)}) collective-permute-start(f32[1,256]{1,0:T(1,128)} %copy.118), channel_id=1, source_target_pairs={{8,0},{16,8},{24,16},{32,24},{40,32},{48,40},{56,48},{9,1},{17,9},... | collective-permute-start | bytes 3080 | tf_op jit(solution)/shard_map/while/body/eval_jaxpr/ppermute | solution.py:24
  325.3 19.9 %collective-permute-start.4 = (bf16[1,256,128]{2,1,0:T(8,128)(2,1)S(1)}, bf16[1,256,128]{2,1,0:T(8,128)(2,1)S(1)}, u32[]{:S(2)}, u32[]{:S(2)}) collective-permute-start(bf16[1,256,128]{2,1,0:T(8,128)(2,1)S(1)} %fusion.112), channel_id=1, source_target_pairs={{0,56},{8,0},{16,8},{24,16},{32,24},{40,32},{48,40},{56,48},{1,57}... | collective-permute-start | bytes 196616 | tf_op jit(solution)/shard_map/while/body/eval_jaxpr/ppermute | solution.py:29
  345.9 39.9 %collective-permute-start = (bf16[1,256,128]{2,1,0:T(8,128)(2,1)}, bf16[1,256,128]{2,1,0:T(8,128)(2,1)S(1)}, u32[]{:S(2)}, u32[]{:S(2)}) collective-permute-start(bf16[1,256,128]{2,1,0:T(8,128)(2,1)} %copy.115), channel_id=1, source_target_pairs={{8,0},{16,8},{24,16},{32,24},{40,32},{48,40},{56,48},{9,1},{17,9},... | collective-permute-start | bytes 196616 | tf_op jit(solution)/shard_map/while/body/eval_jaxpr/ppermute | solution.py:24
  347.8 38.0 %collective-permute-start.1 = (bf16[1,256,128]{2,1,0:T(8,128)(2,1)}, bf16[1,256,128]{2,1,0:T(8,128)(2,1)S(1)}, u32[]{:S(2)}, u32[]{:S(2)}) collective-permute-start(bf16[1,256,128]{2,1,0:T(8,128)(2,1)} %copy.116), channel_id=1, source_target_pairs={{8,0},{16,8},{24,16},{32,24},{40,32},{48,40},{56,48},{9,1},{17,9},... | collective-permute-start | bytes 196616 | tf_op jit(solution)/shard_map/while/body/eval_jaxpr/ppermute | solution.py:24
  349.7 36.1 %collective-permute-start.2 = (f32[1,256]{1,0:T(1,128)}, f32[1,256]{1,0:T(1,128)S(1)}, u32[]{:S(2)}, u32[]{:S(2)}) collective-permute-start(f32[1,256]{1,0:T(1,128)} %copy.117), channel_id=1, source_target_pairs={{8,0},{16,8},{24,16},{32,24},{40,32},{48,40},{56,48},{9,1},{17,9},... | collective-permute-start | bytes 3080 | tf_op jit(solution)/shard_map/while/body/eval_jaxpr/ppermute | solution.py:24
  351.5 34.2 %collective-permute-start.3 = (f32[1,256]{1,0:T(1,128)}, f32[1,256]{1,0:T(1,128)S(1)}, u32[]{:S(2)}, u32[]{:S(2)}) collective-permute-start(f32[1,256]{1,0:T(1,128)} %copy.118), channel_id=1, source_target_pairs={{8,0},{16,8},{24,16},{32,24},{40,32},{48,40},{56,48},{9,1},{17,9},... | collective-permute-start | bytes 3080 | tf_op jit(solution)/shard_map/while/body/eval_jaxpr/ppermute | solution.py:24
  357.3 28.4 %collective-permute-start.4 = (bf16[1,256,128]{2,1,0:T(8,128)(2,1)S(1)}, bf16[1,256,128]{2,1,0:T(8,128)(2,1)S(1)}, u32[]{:S(2)}, u32[]{:S(2)}) collective-permute-start(bf16[1,256,128]{2,1,0:T(8,128)(2,1)S(1)} %fusion.112), channel_id=1, source_target_pairs={{0,56},{8,0},{16,8},{24,16},{32,24},{40,32},{48,40},{56,48},{1,57}... | collective-permute-start | bytes 196616 | tf_op jit(solution)/shard_map/while/body/eval_jaxpr/ppermute | solution.py:29
  386.4 30.0 %collective-permute-start = (bf16[1,256,128]{2,1,0:T(8,128)(2,1)}, bf16[1,256,128]{2,1,0:T(8,128)(2,1)S(1)}, u32[]{:S(2)}, u32[]{:S(2)}) collective-permute-start(bf16[1,256,128]{2,1,0:T(8,128)(2,1)} %copy.115), channel_id=1, source_target_pairs={{8,0},{16,8},{24,16},{32,24},{40,32},{48,40},{56,48},{9,1},{17,9},... | collective-permute-start | bytes 196616 | tf_op jit(solution)/shard_map/while/body/eval_jaxpr/ppermute | solution.py:24
  388.3 28.1 %collective-permute-start.1 = (bf16[1,256,128]{2,1,0:T(8,128)(2,1)}, bf16[1,256,128]{2,1,0:T(8,128)(2,1)S(1)}, u32[]{:S(2)}, u32[]{:S(2)}) collective-permute-start(bf16[1,256,128]{2,1,0:T(8,128)(2,1)} %copy.116), channel_id=1, source_target_pairs={{8,0},{16,8},{24,16},{32,24},{40,32},{48,40},{56,48},{9,1},{17,9},... | collective-permute-start | bytes 196616 | tf_op jit(solution)/shard_map/while/body/eval_jaxpr/ppermute | solution.py:24
  390.2 26.2 %collective-permute-start.2 = (f32[1,256]{1,0:T(1,128)}, f32[1,256]{1,0:T(1,128)S(1)}, u32[]{:S(2)}, u32[]{:S(2)}) collective-permute-start(f32[1,256]{1,0:T(1,128)} %copy.117), channel_id=1, source_target_pairs={{8,0},{16,8},{24,16},{32,24},{40,32},{48,40},{56,48},{9,1},{17,9},... | collective-permute-start | bytes 3080 | tf_op jit(solution)/shard_map/while/body/eval_jaxpr/ppermute | solution.py:24
  392.0 24.4 %collective-permute-start.3 = (f32[1,256]{1,0:T(1,128)}, f32[1,256]{1,0:T(1,128)S(1)}, u32[]{:S(2)}, u32[]{:S(2)}) collective-permute-start(f32[1,256]{1,0:T(1,128)} %copy.118), channel_id=1, source_target_pairs={{8,0},{16,8},{24,16},{32,24},{40,32},{48,40},{56,48},{9,1},{17,9},... | collective-permute-start | bytes 3080 | tf_op jit(solution)/shard_map/while/body/eval_jaxpr/ppermute | solution.py:24
  397.8 18.6 %collective-permute-start.4 = (bf16[1,256,128]{2,1,0:T(8,128)(2,1)S(1)}, bf16[1,256,128]{2,1,0:T(8,128)(2,1)S(1)}, u32[]{:S(2)}, u32[]{:S(2)}) collective-permute-start(bf16[1,256,128]{2,1,0:T(8,128)(2,1)S(1)} %fusion.112), channel_id=1, source_target_pairs={{0,56},{8,0},{16,8},{24,16},{32,24},{40,32},{48,40},{56,48},{1,57}... | collective-permute-start | bytes 196616 | tf_op jit(solution)/shard_map/while/body/eval_jaxpr/ppermute | solution.py:29
  417.5 14.9 %copy-start.3 = (f32[2,128,1,128]{3,1,2,0:T(8,128)}, f32[2,128,1,128]{3,1,2,0:T(8,128)S(1)}, u32[]{:S(2)}) copy-start(f32[2,128,1,128]{3,1,2,0:T(8,128)S(1)} %get-tuple-element.730) | copy-start | bytes 393220
  418.2 79.8 %collective-permute-start.5 = (bf16[1,256,128]{2,1,0:T(8,128)(2,1)}, bf16[1,256,128]{2,1,0:T(8,128)(2,1)}, u32[]{:S(2)}, u32[]{:S(2)}) collective-permute-start(bf16[1,256,128]{2,1,0:T(8,128)(2,1)} %add_convert_fusion), channel_id=1, source_target_pairs={{0,56},{8,0},{16,8},{24,16},{32,24},{40,32},{48,40},{56,48},{1,57}... | collective-permute-start | bytes 196616 | tf_op jit(solution)/shard_map/ppermute | solution.py:29
  432.2 1.3 copy-start.9
  432.4 1.2 copy-start.7
  496.0 0.6 copy-start.10
  514.2 10.5 %copy-start.2 = (bf16[1,2,128,128]{3,2,1,0:T(8,128)(2,1)S(1)}, bf16[1,2,128,128]{3,2,1,0:T(8,128)(2,1)}, u32[]{:S(2)}) copy-start(bf16[1,2,128,128]{3,2,1,0:T(8,128)(2,1)} %param.25) | copy-start | bytes 196612
  527.1 267.9 %copy-start.4 = (f32[128,128]{1,0:T(8,128)S(1)}, f32[128,128]{1,0:T(8,128)}, u32[]{:S(2)}) copy-start(f32[128,128]{1,0:T(8,128)} %get-tuple-element.918) | copy-start | bytes 196612
  564.9 234.2 %copy-start.14 = (f32[16]{0:T(128)S(1)}, f32[16]{0:T(128)}, u32[]{:S(2)}) copy-start(f32[16]{0:T(128)} %neg.13) | copy-start | bytes 196
Sparse Core Ops, SparseCore 0:
  65.9 194.7 all-gather.5
  263.9 235.0 all-gather.7
  796.3 148.5 reduce-scatter.1
where the time goes:
time: 958 us; the launch traced here: 953 us
  blocking collectives  370 us (39%)
  waiting for transfers between devices  200 us (21%)
  starting transfers between devices  181 us (19%)
  local copies, waits for them, and re-layouts  77.4 us (8%)
  other arithmetic  56.3 us (6%)
  matrix products  48.5 us (5%)
  between operations  17.3 us (2%)
    psum x1, blocking collectives, body(): totals = lax.psum(jnp.stack([rate_term, skip_term]), ('dp', 'ctx'))  220 us
    ppermute x8, starting transfers between devices, shifted(): return lax.ppermute(x, axis, [(i, (i + by) % size) for i in range(size)])  145 us
    reduce_scatter x1, waiting for transfers between devices, body(): lax.psum_scatter(jnp.stack([write_grad, read_grad]).astype(jnp.bfloat16),...  144 us
    all_gather x1, blocking collectives, body(): lax.all_gather(keyval, 'ctx', axis=2, tiled=True)  72.5 us
    ppermute x8, waiting for transfers between devices, shifted(): return lax.ppermute(x, axis, [(i, (i + by) % size) for i in range(size)])  55.7 us
    all_gather x1, blocking collectives, body(): seg_full = lax.all_gather(doc_ids, 'ctx', axis=1, tiled=True)[0]  45.7 us
    ppermute x28, starting transfers between devices, from_behind(): lax.ppermute(value, axis, [(source, source + steps) for source in range(i...  35.8 us
    unnamed x1, blocking collectives  31.8 us
  transfers between devices with their start and end apart: 39, of which 8 were waited for; matrix products, arithmetic and copies ran while one was open for 13% of the time, Pallas kernels for 0%

commit v1 on v0

v1 whole, which is shorter than its diff:
```python
import functools
import math

import jax
import jax.numpy as jnp
from jax import lax
from jax.experimental import pallas as pl
from jax.experimental.pallas import tpu as pltpu
from jax.sharding import PartitionSpec as P

TOK = 128
WIDTH = 128
PD = 64
NS = 128
SSM_DEV = 16
COLS = SSM_DEV * PD
SIDE = 4
GROUP_COLS = COLS // SIDE
WINDOW = 5 * TOK
META = 16
STATE_ROWS = 2 * NS + META
ATT_ROWS = 3 * TOK + META
NEGATIVE = -1e30
F32 = jnp.float32
BF16 = jnp.bfloat16

NN = (((1,), (0,)), ((), ()))
NT = (((1,), (1,)), ((), ()))
TN = (((0,), (0,)), ((), ()))


def dot(a, b, dims):
    return lax.dot_general(a, b, dims, preferred_element_type=F32)


def pieces(value, count):
    out = []
    for _ in range(count):
        part = value.astype(BF16)
        out.append(part)
        value = value - part.astype(F32)
    return out


def exact_right(value, fixed, dims, count=2):
    return sum(dot(part, fixed, dims) for part in pieces(value, count))


def exact_left(fixed, value, dims, count=2):
    return sum(dot(fixed, part, dims) for part in pieces(value, count))


def iota(shape, dim):
    return lax.broadcasted_iota(jnp.int32, shape, dim)


def head_table(rows=SSM_DEV):
    lanes, row = iota((rows, COLS), 1), iota((rows, COLS), 0)
    return jnp.where((lanes >= row * PD) & (lanes < (row + 1) * PD), 1.0, 0.0).astype(BF16)


def triangle(keep):
    return jnp.where(keep(iota((TOK, TOK), 0), iota((TOK, TOK), 1)), 1.0, 0.0).astype(BF16)


def head_column(ref):
    row = iota((SSM_DEV, TOK), 0)
    out = jnp.zeros((SSM_DEV, TOK), F32)
    for h in range(SSM_DEV):
        out = jnp.where(row == h, ref[h], out)
    return out


def decays(step, rate, docs):
    cumulative = exact_right(-step * rate, triangle(lambda s, t: s <= t), NN, 3)
    ending = cumulative[:, TOK - 1 :]
    entering = jnp.where(docs == docs[:, :1], jnp.exp(cumulative), 0.0)
    leaving = jnp.where(docs == docs[:, TOK - 1 :], jnp.exp(ending - cumulative), 0.0)
    return cumulative, ending, entering, leaving


def local_states(x_ref, dy_ref, bc_ref, step_ref, rate_ref, docs_ref, out_ref, sin_ref, sgr_ref):
    docs = docs_ref[...]
    table = head_table()
    _, ending, entering, leaving = decays(step_ref[0], head_column(rate_ref), docs)
    scaled_in = (exact_right(leaving, table, TN) * x_ref[0].astype(F32)).astype(BF16)
    scaled_grad = (exact_right(entering, table, TN) * dy_ref[0].astype(F32)).astype(BF16)
    sin_ref[...] = scaled_in
    sgr_ref[...] = scaled_grad
    closing = dot(bc_ref[0, 0], scaled_in, TN).astype(BF16)
    opening = dot(bc_ref[0, 1], scaled_grad, TN).astype(BF16)
    passing = pieces(jnp.broadcast_to(jnp.exp(ending), (SSM_DEV, META)), 2)
    high, low = (dot(part, table, TN) for part in passing)
    row = iota((META, GROUP_COLS), 0)
    wide_docs = jnp.concatenate([docs.astype(F32), jnp.zeros((1, GROUP_COLS - TOK), F32)], axis=1)
    for g in range(SIDE):
        at = slice(g * GROUP_COLS, (g + 1) * GROUP_COLS)
        out_ref[g, :NS] = closing[:, at]
        out_ref[g, NS : 2 * NS] = opening[:, at]
        meta = jnp.where(row == 1, high[:, at], jnp.where(row == 2, low[:, at], 0.0))
        out_ref[g, 2 * NS :] = jnp.where(row == 0, wide_docs, meta).astype(BF16)


def carried(ref, state_start, grad_start):
    first, last, through = [], [], []
    for p in range(SIDE):
        meta = ref[p, 2 * NS :].astype(F32)
        first.append(meta[:1, :1])
        last.append(meta[:1, TOK - 1 : TOK])
        through.append(jnp.where(first[p] == last[p], meta[1:2] + meta[2:3], 0.0))
    state_in, grad_in = [state_start], [grad_start]
    for p in range(SIDE):
        leaves = ref[p, :NS].astype(F32) + through[p] * state_in[p]
        if p < SIDE - 1:
            leaves = jnp.where(last[p] == first[p + 1], 1.0, 0.0) * leaves
        state_in.append(leaves)
    for p in range(SIDE - 1, -1, -1):
        leaves = ref[p, NS : 2 * NS].astype(F32) + through[p] * grad_in[0]
        if p > 0:
            leaves = jnp.where(first[p] == last[p - 1], 1.0, 0.0) * leaves
        grad_in.insert(0, leaves)
    return state_in, grad_in, first[0], last[-1]


def half_totals(half_ref, ref, out_ref):
    zero = jnp.zeros((NS, GROUP_COLS), F32)
    state_in, grad_in, first, last = carried(ref, zero, zero)
    upper = half_ref[0] > 0
    out_ref[:NS] = jnp.where(upper, grad_in[0], state_in[-1]).astype(BF16)
    edge = jnp.where(upper, first, last)
    out_ref[NS:] = jnp.broadcast_to(edge, (META, GROUP_COLS)).astype(BF16)


def entering_states(half_ref, ref, other_ref, out_ref):
    upper = half_ref[0] > 0
    first = ref[0, 2 * NS :].astype(F32)[:1, :1]
    last = ref[SIDE - 1, 2 * NS :].astype(F32)[:1, TOK - 1 : TOK]
    edge = other_ref[NS:].astype(F32)[:1, :1]
    meets = jnp.where(edge == jnp.where(upper, first, last), 1.0, 0.0)
    arrived = meets * other_ref[:NS].astype(F32)
    zero = jnp.zeros_like(arrived)
    state_in, grad_in, _, _ = carried(
        ref, jnp.where(upper, arrived, zero), jnp.where(upper, zero, arrived)
    )
    for p in range(SIDE):
        out_ref[p, :NS] = state_in[p].astype(BF16)
        out_ref[p, NS:] = grad_in[p + 1].astype(BF16)


def inside_shard(
    x_ref, dy_ref, bc_ref, step_ref, rate_ref, skip_ref, docs_ref, near_ref, shared_ref, log_ref
):
    docs = docs_ref[...]
    cumulative = decays(step_ref[0], head_column(rate_ref), docs)[0]
    log_decay = -step_ref[0] * head_column(rate_ref)
    cumulative_t = exact_left(triangle(lambda t, s: s <= t), log_decay, NT, 3)
    writes, reads = bc_ref[0, 0], bc_ref[0, 1]
    wide = jnp.broadcast_to(docs.astype(F32), (SSM_DEV, TOK)).astype(BF16)
    docs_t = dot(triangle(lambda t, s: s == t), wide, NT)[:, :1]
    source, target = iota((TOK, TOK), 0), iota((TOK, TOK), 1)
    joined = (source <= target) & (docs_t == docs.astype(F32))
    affinity = dot(writes, reads, NT)
    after = triangle(lambda u, t: u >= t)
    paired_sum = jnp.zeros((TOK, TOK), F32)
    for h in range(SSM_DEV):
        at = slice(h * PD, (h + 1) * PD)
        x, dy = x_ref[0, :, at], dy_ref[0, :, at]
        spread = cumulative[h : h + 1] - cumulative_t[:, h : h + 1]
        weights = jnp.where(joined, jnp.exp(jnp.minimum(spread, 0.0)), 0.0)
        paired = weights * dot(x, dy, NT)
        near_ref[:, at] = dot((weights * affinity).astype(BF16), dy, NN) + skip_ref[h] * dy.astype(
            F32
        )
        paired_sum = paired_sum + paired
        reaching = exact_right(paired * affinity, after, NN)
        log_ref[h : h + 1] = jnp.sum(
            jnp.where(source < target, reaching, 0.0), axis=0, keepdims=True
        )
    shared_ref[0] = exact_right(paired_sum, reads, NN)
    shared_ref[1] = exact_right(paired_sum, writes, TN)


def finish_ssm(
    peers,
    params_rows,
    in_ref,
    x_ref,
    dy_ref,
    bc_ref,
    step_ref,
    rate_ref,
    docs_ref,
    sin_ref,
    sgr_ref,
    near_ref,
    shared_ref,
    log_ref,
    dx_ref,
    step_grad_ref,
    share_ref,
    params_ref,
):
    docs = docs_ref[...]
    table = head_table()
    rate = head_column(rate_ref)
    step = step_ref[0]
    _, ending, entering, leaving = decays(step, rate, docs)
    leave_term = jnp.zeros((SSM_DEV, TOK), F32)
    enter_term = jnp.zeros((SSM_DEV, TOK), F32)
    across = jnp.zeros((SSM_DEV, 8), F32)
    skips = jnp.zeros((8, SSM_DEV), F32)
    write_grad, read_grad = shared_ref[0], shared_ref[1]
    for g in range(SIDE):
        at = slice(g * GROUP_COLS, (g + 1) * GROUP_COLS)
        part = table[:, at]
        state_in, grad_in = in_ref[g, :NS], in_ref[g, NS:]
        x, dy = x_ref[0, :, at].astype(F32), dy_ref[0, :, at].astype(F32)
        back = exact_right(leaving, part, TN) * dot(bc_ref[0, 0], grad_in, NN)
        ahead = exact_right(entering, part, TN) * dot(bc_ref[0, 1], state_in, NN)
        dx_ref[0, :, at] = (near_ref[:, at] + back).astype(BF16)
        leave_term += exact_left(part, back * x, NT)
        enter_term += exact_left(part, ahead * dy, NT)
        meeting = jnp.sum(state_in.astype(F32) * grad_in.astype(F32), axis=0, keepdims=True)
        across += exact_left(part, jnp.broadcast_to(meeting, (8, GROUP_COLS)), NT)
        skip = jnp.sum(x * dy, axis=0, keepdims=True)
        skips += exact_right(jnp.broadcast_to(skip, (8, GROUP_COLS)), part, NT, 3)
        write_grad += dot(sin_ref[:, at], grad_in, NT)
        read_grad += dot(sgr_ref[:, at], state_in, NT)
    through = jnp.where(docs[:, :1] == docs[:, TOK - 1 :], jnp.exp(ending), 0.0)
    log_grad = (
        log_ref[...]
        + exact_right(enter_term, triangle(lambda u, t: u >= t), NN)
        + exact_right(leave_term, triangle(lambda s, t: s < t), NN)
        + through * across[:, :1]
    )
    step_grad_ref[0] = -rate * log_grad
    rates = exact_left(jnp.ones((8, TOK), BF16), -step * log_grad, NT, 3)
    rows = TOK // peers
    for k in range(peers):
        at = slice(k * rows, (k + 1) * rows)
        share_ref[k, 0] = write_grad[at].astype(BF16)
        share_ref[k, 1] = read_grad[at].astype(BF16)
    both = jnp.concatenate(
        [rates[:1], skips[:1], jnp.zeros((1, TOK - 2 * SSM_DEV), F32)], axis=1
    )
    params_ref[...] = jnp.broadcast_to(both, (params_rows, TOK))


def attention(place_ref, in_ref, dq_ref, dkv_ref, key_scr, value_scr, doc_scr, total_scr):
    half, mine = place_ref[0], place_ref[1]
    scaling = WIDTH ** (-0.5)

    for j in range(2 * SIDE):
        which = lax.bitwise_xor(half, j // SIDE)
        rows = pl.ds(j * TOK, TOK)
        key_scr[rows] = in_ref[j % SIDE, which, 2 * TOK : 3 * TOK, :WIDTH]
        value_scr[rows] = in_ref[j % SIDE, which, 2 * TOK : 3 * TOK, WIDTH:]
        doc_scr[:, rows] = in_ref[j % SIDE, which, 3 * TOK :, :TOK].astype(F32)[:8]

    eye = triangle(lambda a, b: a == b)
    own_start = pl.multiple_of(mine * TOK, TOK)
    own_rows = pl.ds(own_start, TOK)
    own_keys, own_values = key_scr[own_rows], value_scr[own_rows]
    own_docs = doc_scr[:1, own_rows]
    key_lane = iota((TOK, WINDOW), 1)
    row_place = iota((TOK, WINDOW), 0)
    own_diff = iota((TOK, TOK), 1) - iota((TOK, TOK), 0)

    def rows_of(r, h):
        which = lax.bitwise_xor(half, r // SIDE)
        at = slice(h * WIDTH, (h + 1) * WIDTH)
        return in_ref[r % SIDE, which, :TOK, at], in_ref[r % SIDE, which, TOK : 2 * TOK, at]

    def shard(r, own):
        start = pl.multiple_of(jnp.maximum(r - SIDE, 0) * TOK, TOK)
        window = pl.ds(start, WINDOW)
        keys, values = key_scr[window], value_scr[window]
        row_docs = doc_scr[:, pl.ds(pl.multiple_of(r * TOK, TOK), TOK)].astype(BF16)
        docs_t = dot(eye, row_docs, NT)[:, :1]
        allowed = (key_lane + (start - r * TOK) <= row_place) & (docs_t == doc_scr[:1, window])
        own_allowed = (own_diff <= (r - mine) * TOK) & (docs_t == own_docs)
        for h in range(2):
            queries, grads = rows_of(r, h)
            scores = jnp.where(allowed, dot(queries, keys, NT) * scaling, NEGATIVE)
            top = jnp.max(scores, axis=1, keepdims=True)
            expos = jnp.where(allowed, jnp.exp(scores - top), 0.0)
            sums = jnp.sum(expos, axis=1, keepdims=True)
            dot_grads = dot(grads, values, NT)
            delta = jnp.sum(expos * dot_grads, axis=1, keepdims=True) / sums
            logsum = top + jnp.log(sums)
            if own:
                probs = jnp.where(allowed, jnp.exp(scores - logsum), 0.0).astype(BF16)
                dscore = (probs.astype(F32) * (dot_grads - delta)).astype(BF16)
                at = slice(h * WIDTH, (h + 1) * WIDTH)
                dq_ref[0, :, at] = (dot(dscore, keys, NN) * scaling).astype(BF16)
            scores = jnp.where(own_allowed, dot(queries, own_keys, NT) * scaling, NEGATIVE)
            probs = jnp.where(own_allowed, jnp.exp(scores - logsum), 0.0).astype(BF16)
            dot_grads = dot(grads, own_values, NT)
            dscore = (probs.astype(F32) * (dot_grads - delta)).astype(BF16)
            key_part = dot(dscore, queries, TN) * scaling
            value_part = dot(probs, grads, TN)
            if own and h == 0:
                total_scr[0] = key_part
                total_scr[1] = value_part
            else:
                total_scr[0] += key_part
                total_scr[1] += value_part

    shard(mine, True)
    lax.fori_loop(
        mine + 1,
        jnp.minimum(mine + SIDE, 2 * SIDE - 1) + 1,
        lambda r, _: (shard(r, False), 0)[1],
        0,
    )
    dkv_ref[0] = total_scr[...].astype(BF16)


def whole(count):
    return [pl.BlockSpec(memory_space=pltpu.VMEM)] * count


def scalars():
    return pl.BlockSpec(memory_space=pltpu.SMEM)


def params(megabytes=24):
    return pltpu.CompilerParams(vmem_limit_bytes=megabytes << 20)


def shape(dims, dtype):
    return jax.ShapeDtypeStruct(dims, dtype)


def body(
    queries, keyval, attn_grad, doc_ids, ssm_in, bc_pair, step_size, decay_rate, skip_gain, ssm_grad
):
    mine = lax.axis_index("ctx")
    half = mine // SIDE
    place = jnp.stack([half, mine]).astype(jnp.int32)
    peers = lax.axis_size("head")
    everyone = lax.axis_size("dp") * lax.axis_size("ctx")
    sides = [list(range(SIDE)), list(range(SIDE, 2 * SIDE))]
    across = [(i, i ^ SIDE) for i in range(2 * SIDE)]

    def between(value):
        return lax.all_to_all(value, "ctx", 0, 0, axis_index_groups=sides, tiled=True)

    docs_rows = jnp.broadcast_to(
        jnp.pad(doc_ids.astype(BF16), ((0, 0), (0, 2 * WIDTH - TOK))), (META, 2 * WIDTH)
    )
    attention_own = jnp.concatenate(
        [queries[0], attn_grad[0], jnp.concatenate([keyval[0, 0], keyval[0, 1]], axis=1), docs_rows]
    )
    attention_other = lax.ppermute(attention_own, "ctx", across)

    sent, scaled_in, scaled_grad = pl.pallas_call(
        local_states,
        out_shape=(
            shape((SIDE, STATE_ROWS, GROUP_COLS), BF16),
            shape((TOK, COLS), BF16),
            shape((TOK, COLS), BF16),
        ),
        in_specs=whole(4) + [scalars()] + whole(1),
        out_specs=tuple(whole(3)),
        compiler_params=params(),
        name="local_states",
    )(ssm_in, ssm_grad, bc_pair, step_size, decay_rate, doc_ids)
    received = between(sent)
    total = pl.pallas_call(
        half_totals,
        out_shape=shape((NS + META, GROUP_COLS), BF16),
        in_specs=[scalars()] + whole(1),
        out_specs=whole(1)[0],
        compiler_params=params(),
        name="half_totals",
    )(place, received)
    other_total = lax.ppermute(total, "ctx", across)

    step_after, _ = lax.optimization_barrier((step_size, total))
    near, shared_near, log_near = pl.pallas_call(
        inside_shard,
        out_shape=(
            shape((TOK, COLS), F32),
            shape((2, TOK, NS), F32),
            shape((SSM_DEV, TOK), F32),
        ),
        in_specs=whole(4) + [scalars(), scalars()] + whole(1),
        out_specs=tuple(whole(3)),
        compiler_params=params(),
        name="inside_shard",
        cost_estimate=pl.CostEstimate(flops=400 << 20, bytes_accessed=2 << 20, transcendentals=0),
    )(ssm_in, ssm_grad, bc_pair, step_after, decay_rate, skip_gain, doc_ids)

    own_after, _ = lax.optimization_barrier((attention_own, log_near))
    gathered = between(
        jnp.broadcast_to(
            jnp.stack([own_after, attention_other])[None], (SIDE, 2, ATT_ROWS, 2 * WIDTH)
        )
    )

    entering = pl.pallas_call(
        entering_states,
        out_shape=shape((SIDE, 2 * NS, GROUP_COLS), BF16),
        in_specs=[scalars()] + whole(2),
        out_specs=whole(1)[0],
        compiler_params=params(),
        name="entering_states",
    )(place, received, other_total)
    entered = between(entering)

    input_grad, step_grad, share, both = pl.pallas_call(
        functools.partial(finish_ssm, peers, everyone),
        out_shape=(
            shape((1, TOK, COLS), BF16),
            shape((1, SSM_DEV, TOK), F32),
            shape((peers, 2, TOK // peers, NS), BF16),
            shape((everyone, TOK), F32),
        ),
        in_specs=whole(5) + [scalars()] + whole(6),
        out_specs=tuple(whole(4)),
        compiler_params=params(),
        name="finish_ssm",
    )(
        entered,
        ssm_in,
        ssm_grad,
        bc_pair,
        step_size,
        decay_rate,
        doc_ids,
        scaled_in,
        scaled_grad,
        near,
        shared_near,
        log_near,
    )
    everywhere = lax.all_to_all(both, ("dp", "ctx"), 0, 0, tiled=True)
    shares = lax.all_to_all(share, "head", 0, 0, tiled=True)

    gathered, _ = lax.optimization_barrier((gathered, both))
    query_grad, keyval_grad = pl.pallas_call(
        attention,
        out_shape=(shape((1, TOK, 2 * WIDTH), BF16), shape((1, 2, TOK, WIDTH), BF16)),
        in_specs=[scalars()] + whole(1),
        out_specs=tuple(whole(2)),
        scratch_shapes=[
            pltpu.VMEM((2 * SIDE * TOK, WIDTH), BF16),
            pltpu.VMEM((2 * SIDE * TOK, WIDTH), BF16),
            pltpu.VMEM((8, 2 * SIDE * TOK), F32),
            pltpu.VMEM((2, TOK, WIDTH), F32),
        ],
        compiler_params=params(),
        name="attention",
        cost_estimate=pl.CostEstimate(flops=2 << 30, bytes_accessed=4 << 20, transcendentals=1 << 20),
    )(place, gathered)

    shared_grad = jnp.sum(shares.astype(F32), axis=0)[None]
    totals = jnp.sum(everywhere, axis=0)[: 2 * SSM_DEV].reshape(2, SSM_DEV)
    param_grads = totals / math.sqrt(lax.axis_size("dp") * lax.axis_size("ctx") * TOK * PD)
    return (query_grad, keyval_grad, input_grad, shared_grad, step_grad, param_grads)


def solution(mesh):
    placed = (
        P("dp", "ctx", "head"),
        P("dp", None, "ctx", "head"),
        P("dp", "ctx", "head"),
        P("dp", "ctx"),
        P("dp", "ctx", "head"),
        P("dp", None, "ctx", None),
        P("dp", "head", "ctx"),
        P("head"),
        P("head"),
        P("dp", "ctx", "head"),
    )
    return jax.shard_map(
        body,
        mesh=mesh,
        in_specs=placed,
        out_specs=(
            P("dp", "ctx", "head"),
            P("dp", None, "ctx", "head"),
            P("dp", "ctx", "head"),
            P("dp", None, ("ctx", "head"), None),
            P("dp", "head", "ctx"),
            P(None, "head"),
        ),
        check_vma=False,
    )
```

time: 958 us -> 133 us (0.14)
  blocking collectives: 370 us -> 12.9 us
  waiting for transfers between devices: 200 us -> 39.9 us
  starting transfers between devices: 181 us -> 52 us
  local copies, waits for them, and re-layouts: 77.4 us -> 6.77 us
  other arithmetic: 56.3 us -> 0.85 us
  matrix products: 48.5 us -> 0 us
  Pallas kernels: 0 us -> 18.4 us
  between operations: 17.3 us -> 0.88 us
    psum x1 -> x0, blocking collectives: 220 us -> none  [body(): totals = lax.psum(jnp.stack([rate_term, skip_term]), ('dp', 'ctx'))]
    ppermute x36 -> x2, starting transfers between devices: 181 us -> 30.6 us  [the longest x1 17.2 us: body(): other_total = lax.ppermute(total, 'ctx', across)]
    reduce_scatter x1 -> x0, waiting for transfers between devices: 144 us -> none  [body(): lax.psum_scatter(jnp.stack([write_grad, read_grad]).astype(jnp.bfloat16),...]
    all_gather x2 -> x0, blocking collectives: 118 us -> none  [the longest x1 72.5 us: body(): lax.all_gather(keyval, 'ctx', axis=2, tiled=True)]
    ppermute x36 -> x2, waiting for transfers between devices: 55.7 us -> 1.8 us  [the longest x1 1.79 us: body(): other_total = lax.ppermute(total, 'ctx', across)]
    dot_general x53 -> x0, matrix products: 48.5 us -> none  [the longest x8 7.47 us: tile_grads(): jnp.einsum('hre,khe->hrk', side_queries, key_rows, preferred_element_type...]
    all_to_all x0 -> x4, waiting for transfers between devices: none -> 38.1 us  [the longest x3 25.2 us: between(): lax.all_to_all(value, 'ctx', 0, 0, axis_index_groups=sides, tiled=True)]
    unnamed x1 -> x0, blocking collectives: 31.8 us -> none
  transfers between devices with their start and end apart: 39 -> 6, of which waited for: 8 -> 4; matrix products, arithmetic and copies ran while one was open for 13% -> 1% of each run, Pallas kernels for 0% -> 5%
where the time goes in v1:
time: 133 us; the launch traced here: 132 us
  starting transfers between devices  52 us (39%)
  waiting for transfers between devices  39.9 us (30%)
  Pallas kernels  18.4 us (14%)
  blocking collectives  12.9 us (10%)
  local copies, waits for them, and re-layouts  6.77 us (5%)
    all_to_all x3, waiting for transfers between devices, between(): lax.all_to_all(value, 'ctx', 0, 0, axis_index_groups=sides, tiled=True)  25.2 us
    ppermute x1, starting transfers between devices, body(): other_total = lax.ppermute(total, 'ctx', across)  17.2 us
    ppermute x1, starting transfers between devices, body(): attention_other = lax.ppermute(attention_own, 'ctx', across)  13.3 us
    all_to_all x1, waiting for transfers between devices, body(): everywhere = lax.all_to_all(both, ('dp', 'ctx'), 0, 0, tiled=True)  13 us
    all_to_all x1, blocking collectives, body(): shares = lax.all_to_all(share, 'head', 0, 0, tiled=True)  12.9 us
    all_to_all x3, starting transfers between devices, between(): lax.all_to_all(value, 'ctx', 0, 0, axis_index_groups=sides, tiled=True)  11.9 us
    all_to_all x1, starting transfers between devices, body(): everywhere = lax.all_to_all(both, ('dp', 'ctx'), 0, 0, tiled=True)  9.5 us
    pallas_call x1, Pallas kernels, body(): pl.pallas_call(attention, out_shape=(shape((1, TOK, 2 * WIDTH), BF16), sh...  7.65 us
  transfers between devices with their start and end apart: 6, of which 4 were waited for; matrix products, arithmetic and copies ran while one was open for 1% of the time, Pallas kernels for 5%

profile of v1, /device:TPU:1, one launch (start us, length us, event | category | flops | bytes accessed | tf_op | source)
XLA Modules:
  0.0 131.7 jit_solution(2739188774338214242)
XLA Ops:
  0.6 0.0 copy-start
  0.6 0.9 copy-done
  1.6 0.0 copy-start.2
  1.6 0.9 copy-done.2
  2.5 0.0 copy-start.4
  2.5 0.8 copy-done.4
  3.4 0.0 copy-start.6
  3.4 0.7 copy-done.6
  4.1 0.0 copy-start.8
  4.1 0.7 copy-done.8
  4.7 0.0 copy-start.10
  4.7 0.7 copy-done.10
  5.4 0.0 copy-start.9
  5.4 2.3 %local_states.1 = (bf16[4,272,256]{2,1,0:T(8,128)(2,1)}, bf16[128,1024]{1,0:T(8,128)(2,1)S(1)}, bf16[128,1024]{1,0:T(8,128)(2,1)S(1)}) custom-call(bf16[1,128,1024]{2,1,0:T(8,128)(2,1)S(1)} %copy-done, bf16[1,128,1024]{2,1,0:T(8,128)(2,1)S(1)} %copy-done.2, bf16[1,2,128,128]{3,2,1,0:T(8,128)(2,1)S(1)} %copy-done.4, f32[1,16,128]{2,1,0:T(8,128)S(1)} %copy-done.6, ...), custom_call_target="tpu_custom_call" | custom-call | tf_op jit(solution)/shard_map/local_states/pallas_call | solution.py:357
  7.6 4.8 %all-to-all-start = ((bf16[4,272,256]{2,1,0:T(8,128)(2,1)}), bf16[4,272,256]{2,1,0:T(8,128)(2,1)S(1)}, u32[]{:S(2)}, u32[]{:S(2)}) async-start(bf16[4,272,256]{2,1,0:T(8,128)(2,1)} %get-tuple-element.21), calls=%async_computation | async-start | bytes 1114112 | tf_op jit(solution)/shard_map/all_to_all | solution.py:347
  12.5 0.0 copy-start.15
  12.5 0.0 copy-start.13
  12.5 0.0 copy-start.14
  12.5 0.1 pad_add_fusion.half_ref.place_ref
  12.6 0.0 copy-start.1
  12.6 0.0 copy-start.3
  12.6 0.0 copy-start.5
  12.6 0.0 copy-start.7
  12.6 0.0 copy-start.11
  12.6 0.0 copy-start.12
  12.6 7.0 %all-to-all-done.ref = bf16[4,272,256]{2,1,0:T(8,128)(2,1)S(1)} async-done(((bf16[4,272,256]{2,1,0:T(8,128)(2,1)}), bf16[4,272,256]{2,1,0:T(8,128)(2,1)S(1)}, u32[]{:S(2)}, u32[]{:S(2)}) %all-to-all-start) | async-done | bytes 557088 | tf_op jit(solution)/shard_map/all_to_all | solution.py:347
  19.6 0.8 half_totals.1
  20.4 17.2 %collective-permute-start.1 = (bf16[144,256]{1,0:T(8,128)(2,1)S(1)}, bf16[144,256]{1,0:T(8,128)(2,1)S(1)}, u32[]{:S(2)}, u32[]{:S(2)}) collective-permute-start(bf16[144,256]{1,0:T(8,128)(2,1)S(1)} %half_totals.1), channel_id=1, source_target_pairs={{0,32},{8,40},{16,48},{24,56},{32,0},{40,8},{48,16},{56,24},{1,33}... | collective-permute-start | bytes 221192 | tf_op jit(solution)/shard_map/ppermute | solution.py:378
  37.7 0.0 copy-done.9
  37.7 1.8 %collective-permute-done.1.other_ref = bf16[144,256]{1,0:T(8,128)(2,1)S(1)} collective-permute-done((bf16[144,256]{1,0:T(8,128)(2,1)S(1)}, bf16[144,256]{1,0:T(8,128)(2,1)S(1)}, u32[]{:S(2)}, u32[]{:S(2)}) %collective-permute-start.1) | collective-permute-done | bytes 73760 | tf_op jit(solution)/shard_map/ppermute | solution.py:378
  39.5 1.6 %entering_states.1 = bf16[4,256,256]{2,1,0:T(8,128)(2,1)} custom-call(s32[2]{0:T(128)S(1)} %pad_add_fusion.half_ref.place_ref, bf16[4,272,256]{2,1,0:T(8,128)(2,1)S(1)} %all-to-all-done.ref, bf16[144,256]{1,0:T(8,128)(2,1)S(1)} %collective-permute-done.1.other_ref), custom_call_target="tpu_custom_call" | custom-call | tf_op jit(solution)/shard_map/entering_states/pallas_call | solution.py:402
  41.2 3.5 %all-to-all-start.2 = ((bf16[4,256,256]{2,1,0:T(8,128)(2,1)}), bf16[4,256,256]{2,1,0:T(8,128)(2,1)S(1)}, u32[]{:S(2)}, u32[]{:S(2)}) async-start(bf16[4,256,256]{2,1,0:T(8,128)(2,1)} %entering_states.1), calls=%async_computation.2 | async-start | bytes 1048576 | tf_op jit(solution)/shard_map/all_to_all | solution.py:347
  44.6 0.0 copy-done.15
  44.7 0.0 copy-done.13
  44.7 0.0 copy-done.14
  44.7 13.3 %collective-permute-start = (bf16[400,256]{1,0:T(8,128)(2,1)S(1)}, bf16[400,256]{1,0:T(8,128)(2,1)S(1)}, u32[]{:S(2)}, u32[]{:S(2)}) collective-permute-start(bf16[400,256]{1,0:T(8,128)(2,1)S(1)} %pad_maximum_fusion.1), channel_id=1, source_target_pairs={{0,32},{8,40},{16,48},{24,56},{32,0},{40,8},{48,16},{56,24},{1,33}... | collective-permute-start | bytes 614408 | tf_op jit(solution)/shard_map/ppermute | solution.py:355
  58.1 0.0 copy-done.1
  58.1 0.0 copy-done.3
  58.1 0.0 copy-done.5
  58.1 0.0 copy-done.7
  58.1 0.0 copy-done.11
  58.1 0.0 copy-done.12
  58.1 2.8 %inside_shard.1 = (f32[128,1024]{1,0:T(8,128)S(1)}, f32[2,128,128]{2,1,0:T(8,128)S(1)}, f32[16,128]{1,0:T(8,128)S(1)}) custom-call(bf16[1,128,1024]{2,1,0:T(8,128)(2,1)S(1)} %copy-done.1, bf16[1,128,1024]{2,1,0:T(8,128)(2,1)S(1)} %copy-done.3, bf16[1,2,128,128]{3,2,1,0:T(8,128)(2,1)S(1)} %copy-done.5, f32[1,16,128]{2,1,0:T(8,128)S(1)} %copy-done.7, ...), custom_call_target="tpu_custom_call" | custom-call | flops 419430400 | bytes 2097152 | tf_op jit(solution)/shard_map/inside_shard/pallas_call | solution.py:381
  61.0 0.0 all-to-all-done.2.in_ref
  61.0 3.2 %finish_ssm.1 = (bf16[1,128,1024]{2,1,0:T(8,128)(2,1)}, f32[1,16,128]{2,1,0:T(8,128)}, bf16[8,2,16,128]{3,2,1,0:T(8,128)(2,1)S(1)}, f32[64,128]{1,0:T(8,128)}) custom-call(bf16[4,256,256]{2,1,0:T(8,128)(2,1)S(1)} %all-to-all-done.2.in_ref, bf16[1,128,1024]{2,1,0:T(8,128)(2,1)S(1)} %copy-done.1, bf16[1,128,1024]{2,1,0:T(8,128)(2,1)S(1)} %copy-done.3, ...), custom_call_target="tpu_custom_call" | custom-call | tf_op jit(solution)/shard_map/finish_ssm/pallas_call | solution.py:412
  64.2 12.9 %all_to_all.29 = bf16[8,2,16,128]{3,2,1,0:T(8,128)(2,1)S(1)} all-to-all(bf16[8,2,16,128]{3,2,1,0:T(8,128)(2,1)S(1)} %get-tuple-element.34), channel_id=1, replica_groups=mesh['dp'=8,'ctx'=8,'head'=8] {'head'}, dimensions={0} | all-to-all | bytes 131072 | tf_op jit(solution)/shard_map/all_to_all | solution.py:439
  77.1 9.5 %all-to-all-start.4 = ((f32[64,1,128]{2,1,0:T(1,128)}), f32[64,1,128]{2,1,0:T(1,128)S(1)}, u32[]{:S(2)}, u32[]{:S(2)}) async-start(f32[64,1,128]{2,1,0:T(1,128)} %bitcast.10), calls=%async_computation.4 | async-start | bytes 65536 | tf_op jit(solution)/shard_map/all_to_all | solution.py:438
  86.6 0.0 collective-permute-done
  86.6 13.0 %all-to-all-done.4 = f32[64,1,128]{2,1,0:T(1,128)S(1)} async-done(((f32[64,1,128]{2,1,0:T(1,128)}), f32[64,1,128]{2,1,0:T(1,128)S(1)}, u32[]{:S(2)}, u32[]{:S(2)}) %all-to-all-start.4) | async-done | bytes 32800 | tf_op jit(solution)/shard_map/all_to_all | solution.py:438
  99.6 1.3 broadcast_in_dim.18
  100.9 3.6 %all-to-all-start.1 = ((bf16[4,2,400,256]{3,2,1,0:T(8,128)(2,1)}), bf16[4,2,400,256]{3,2,1,0:T(8,128)(2,1)S(1)}, u32[]{:S(2)}, u32[]{:S(2)}) async-start(bf16[4,2,400,256]{3,2,1,0:T(8,128)(2,1)} %broadcast_in_dim.18), calls=%async_computation.1 | async-start | bytes 3276800 | tf_op jit(solution)/shard_map/all_to_all | solution.py:347
  104.5 0.6 convert_reduce_fusion
  105.1 0.1 reduce_sum.19
  105.2 0.6 div.21
  105.8 18.2 %all-to-all-done.1.in_ref = bf16[4,2,400,256]{3,2,1,0:T(8,128)(2,1)S(1)} async-done(((bf16[4,2,400,256]{3,2,1,0:T(8,128)(2,1)}), bf16[4,2,400,256]{3,2,1,0:T(8,128)(2,1)S(1)}, u32[]{:S(2)}, u32[]{:S(2)}) %all-to-all-start.1) | async-done | bytes 1638432 | tf_op jit(solution)/shard_map/all_to_all | solution.py:347
  124.0 7.7 %attention.1 = (bf16[1,128,256]{2,1,0:T(8,128)(2,1)}, bf16[1,2,128,128]{3,2,1,0:T(8,128)(2,1)}) custom-call(s32[2]{0:T(128)S(1)} %pad_add_fusion.half_ref.place_ref, bf16[4,2,400,256]{3,2,1,0:T(8,128)(2,1)S(1)} %all-to-all-done.1.in_ref), custom_call_target="tpu_custom_call" | custom-call | flops 2147483648 | bytes 4194304 | tf_op jit(solution)/shard_map/attention/pallas_call | solution.py:442
  (7 shorter events, 0.1 us)
Async XLA Ops:
  0.6 1.0 copy-start
  1.6 0.9 copy-start.2
  2.5 0.8 copy-start.4
  3.4 0.7 copy-start.6
  4.1 0.7 copy-start.8
  4.7 0.7 copy-start.10
  5.4 32.3 %copy-start.9 = (s32[1,128]{1,0:T(1,128)S(1)}, s32[1,128]{1,0:T(1,128)}, u32[]{:S(2)}) copy-start(s32[1,128]{1,0:T(1,128)} %docs_ref.5) | copy-start | bytes 1540
  7.6 12.0 %all-to-all-start = ((bf16[4,272,256]{2,1,0:T(8,128)(2,1)}), bf16[4,272,256]{2,1,0:T(8,128)(2,1)S(1)}, u32[]{:S(2)}, u32[]{:S(2)}) async-start(bf16[4,272,256]{2,1,0:T(8,128)(2,1)} %get-tuple-element.21), calls=%async_computation | async-start | bytes 1114112 | tf_op jit(solution)/shard_map/all_to_all | solution.py:347
  12.5 32.2 %copy-start.15 = (bf16[1,2,128,128]{3,2,1,0:T(8,128)(2,1)S(1)}, bf16[1,2,128,128]{3,2,1,0:T(8,128)(2,1)}, u32[]{:S(2)}) copy-start(bf16[1,2,128,128]{3,2,1,0:T(8,128)(2,1)} %param.11) | copy-start | bytes 196612
  12.5 32.2 %copy-start.13 = (bf16[1,128,256]{2,1,0:T(8,128)(2,1)S(1)}, bf16[1,128,256]{2,1,0:T(8,128)(2,1)}, u32[]{:S(2)}) copy-start(bf16[1,128,256]{2,1,0:T(8,128)(2,1)} %param.12) | copy-start | bytes 196612
  12.5 32.2 %copy-start.14 = (bf16[1,128,256]{2,1,0:T(8,128)(2,1)S(1)}, bf16[1,128,256]{2,1,0:T(8,128)(2,1)}, u32[]{:S(2)}) copy-start(bf16[1,128,256]{2,1,0:T(8,128)(2,1)} %param.10) | copy-start | bytes 196612
  12.6 45.5 %copy-start.1 = (bf16[1,128,1024]{2,1,0:T(8,128)(2,1)S(1)}, bf16[1,128,1024]{2,1,0:T(8,128)(2,1)}, u32[]{:S(2)}) copy-start(bf16[1,128,1024]{2,1,0:T(8,128)(2,1)} %x_ref.5) | copy-start | bytes 786436
  12.6 45.5 %copy-start.3 = (bf16[1,128,1024]{2,1,0:T(8,128)(2,1)S(1)}, bf16[1,128,1024]{2,1,0:T(8,128)(2,1)}, u32[]{:S(2)}) copy-start(bf16[1,128,1024]{2,1,0:T(8,128)(2,1)} %dy_ref.5) | copy-start | bytes 786436
  12.6 45.5 %copy-start.5 = (bf16[1,2,128,128]{3,2,1,0:T(8,128)(2,1)S(1)}, bf16[1,2,128,128]{3,2,1,0:T(8,128)(2,1)}, u32[]{:S(2)}) copy-start(bf16[1,2,128,128]{3,2,1,0:T(8,128)(2,1)} %bc_ref.5) | copy-start | bytes 196612
  12.6 45.5 %copy-start.7 = (f32[1,16,128]{2,1,0:T(8,128)S(1)}, f32[1,16,128]{2,1,0:T(8,128)}, u32[]{:S(2)}) copy-start(f32[1,16,128]{2,1,0:T(8,128)} %step_ref.4) | copy-start | bytes 24580
  12.6 45.5 %copy-start.11 = (f32[16]{0:T(128)S(1)}, f32[16]{0:T(128)}, u32[]{:S(2)}) copy-start(f32[16]{0:T(128)} %rate_ref.5) | copy-start | bytes 196
  12.6 45.5 %copy-start.12 = (f32[16]{0:T(128)S(1)}, f32[16]{0:T(128)}, u32[]{:S(2)}) copy-start(f32[16]{0:T(128)} %skip_ref.1) | copy-start | bytes 196
  20.4 19.1 %collective-permute-start.1 = (bf16[144,256]{1,0:T(8,128)(2,1)S(1)}, bf16[144,256]{1,0:T(8,128)(2,1)S(1)}, u32[]{:S(2)}, u32[]{:S(2)}) collective-permute-start(bf16[144,256]{1,0:T(8,128)(2,1)S(1)} %half_totals.1), channel_id=1, source_target_pairs={{0,32},{8,40},{16,48},{24,56},{32,0},{40,8},{48,16},{56,24},{1,33}... | collective-permute-start | bytes 221192 | tf_op jit(solution)/shard_map/ppermute | solution.py:378
  41.2 19.8 %all-to-all-start.2 = ((bf16[4,256,256]{2,1,0:T(8,128)(2,1)}), bf16[4,256,256]{2,1,0:T(8,128)(2,1)S(1)}, u32[]{:S(2)}, u32[]{:S(2)}) async-start(bf16[4,256,256]{2,1,0:T(8,128)(2,1)} %entering_states.1), calls=%async_computation.2 | async-start | bytes 1048576 | tf_op jit(solution)/shard_map/all_to_all | solution.py:347
  44.7 41.9 %collective-permute-start = (bf16[400,256]{1,0:T(8,128)(2,1)S(1)}, bf16[400,256]{1,0:T(8,128)(2,1)S(1)}, u32[]{:S(2)}, u32[]{:S(2)}) collective-permute-start(bf16[400,256]{1,0:T(8,128)(2,1)S(1)} %pad_maximum_fusion.1), channel_id=1, source_target_pairs={{0,32},{8,40},{16,48},{24,56},{32,0},{40,8},{48,16},{56,24},{1,33}... | collective-permute-start | bytes 614408 | tf_op jit(solution)/shard_map/ppermute | solution.py:355
  77.1 22.5 %all-to-all-start.4 = ((f32[64,1,128]{2,1,0:T(1,128)}), f32[64,1,128]{2,1,0:T(1,128)S(1)}, u32[]{:S(2)}, u32[]{:S(2)}) async-start(f32[64,1,128]{2,1,0:T(1,128)} %bitcast.10), calls=%async_computation.4 | async-start | bytes 65536 | tf_op jit(solution)/shard_map/all_to_all | solution.py:438
  100.9 23.1 %all-to-all-start.1 = ((bf16[4,2,400,256]{3,2,1,0:T(8,128)(2,1)}), bf16[4,2,400,256]{3,2,1,0:T(8,128)(2,1)S(1)}, u32[]{:S(2)}, u32[]{:S(2)}) async-start(bf16[4,2,400,256]{3,2,1,0:T(8,128)(2,1)} %broadcast_in_dim.18), calls=%async_computation.1 | async-start | bytes 3276800 | tf_op jit(solution)/shard_map/all_to_all | solution.py:347

commit v2 on v1

--- a/solution.py
+++ b/solution.py
@@ -79,15 +79,46 @@
     return cumulative, ending, entering, leaving
 
 
-def local_states(x_ref, dy_ref, bc_ref, step_ref, rate_ref, docs_ref, out_ref, sin_ref, sgr_ref):
+def local_states(
+    x_hbm,
+    dy_hbm,
+    bc_hbm,
+    step_hbm,
+    docs_hbm,
+    rate_ref,
+    out_ref,
+    sin_ref,
+    sgr_ref,
+    x_ref,
+    dy_ref,
+    bc_ref,
+    step_ref,
+    docs_ref,
+    arrived,
+):
+    pairs = ((step_hbm, step_ref), (docs_hbm, docs_ref), (x_hbm, x_ref), (bc_hbm, bc_ref))
+    pairs += ((dy_hbm, dy_ref),)
+    copies = [
+        pltpu.make_async_copy(source, target, arrived.at[i])
+        for i, (source, target) in enumerate(pairs)
+    ]
+    for copy in copies:
+        copy.start()
+    table = head_table()
+    rate = head_column(rate_ref)
+    copies[0].wait()
+    copies[1].wait()
     docs = docs_ref[...]
-    table = head_table()
-    _, ending, entering, leaving = decays(step_ref[0], head_column(rate_ref), docs)
-    scaled_in = (exact_right(leaving, table, TN) * x_ref[0].astype(F32)).astype(BF16)
-    scaled_grad = (exact_right(entering, table, TN) * dy_ref[0].astype(F32)).astype(BF16)
+    _, ending, entering, leaving = decays(step_ref[0], rate, docs)
+    leaving, entering = exact_right(leaving, table, TN), exact_right(entering, table, TN)
+    copies[2].wait()
+    scaled_in = (leaving * x_ref[0].astype(F32)).astype(BF16)
     sin_ref[...] = scaled_in
+    copies[3].wait()
+    closing = dot(bc_ref[0, 0], scaled_in, TN).astype(BF16)
+    copies[4].wait()
+    scaled_grad = (entering * dy_ref[0].astype(F32)).astype(BF16)
     sgr_ref[...] = scaled_grad
-    closing = dot(bc_ref[0, 0], scaled_in, TN).astype(BF16)
     opening = dot(bc_ref[0, 1], scaled_grad, TN).astype(BF16)
     passing = pieces(jnp.broadcast_to(jnp.exp(ending), (SSM_DEV, META)), 2)
     high, low = (dot(part, table, TN) for part in passing)
@@ -99,6 +130,17 @@
         out_ref[g, NS : 2 * NS] = opening[:, at]
         meta = jnp.where(row == 1, high[:, at], jnp.where(row == 2, low[:, at], 0.0))
         out_ref[g, 2 * NS :] = jnp.where(row == 0, wide_docs, meta).astype(BF16)
+
+
+def pack(queries_ref, grads_ref, keyval_ref, docs_ref, out_ref, pair_ref):
+    out_ref[:TOK] = queries_ref[0]
+    out_ref[TOK : 2 * TOK] = grads_ref[0]
+    out_ref[2 * TOK : 3 * TOK, :WIDTH] = keyval_ref[0, 0]
+    out_ref[2 * TOK : 3 * TOK, WIDTH:] = keyval_ref[0, 1]
+    docs = jnp.broadcast_to(docs_ref[...].astype(F32), (META, TOK)).astype(BF16)
+    out_ref[3 * TOK :, :WIDTH] = docs
+    out_ref[3 * TOK :, WIDTH:] = docs
+    pair_ref[...] = out_ref[2 * TOK :]
 
 
 def carried(ref, state_start, grad_start):
@@ -148,11 +190,23 @@
 
 
 def inside_shard(
-    x_ref, dy_ref, bc_ref, step_ref, rate_ref, skip_ref, docs_ref, near_ref, shared_ref, log_ref
+    x_ref, dy_ref, bc_ref, step_ref, rate_ref, skip_ref, docs_ref, near_ref, shared_ref, aux_ref
 ):
     docs = docs_ref[...]
-    cumulative = decays(step_ref[0], head_column(rate_ref), docs)[0]
-    log_decay = -step_ref[0] * head_column(rate_ref)
+    rate = head_column(rate_ref)
+    cumulative, ending, entering, leaving = decays(step_ref[0], rate, docs)
+    log_decay = -step_ref[0] * rate
+    aux_ref[1] = entering
+    aux_ref[2] = leaving
+    through = jnp.where(docs[:, :1] == docs[:, TOK - 1 :], jnp.exp(ending), 0.0)
+    aux_ref[3] = jnp.broadcast_to(through, (SSM_DEV, TOK))
+    aux_ref[4] = -rate
+    aux_ref[5] = -step_ref[0]
+    skip = jnp.sum(x_ref[0].astype(F32) * dy_ref[0].astype(F32), axis=0, keepdims=True)
+    lanes, row = iota((TOK, COLS), 1), iota((TOK, COLS), 0) - SSM_DEV
+    later_table = jnp.where((lanes >= row * PD) & (lanes < (row + 1) * PD), 1.0, 0.0).astype(BF16)
+    skips = exact_right(jnp.broadcast_to(skip, (SSM_DEV, COLS)), later_table, NT, 3)
+    aux_ref[6] = skips
     cumulative_t = exact_left(triangle(lambda t, s: s <= t), log_decay, NT, 3)
     writes, reads = bc_ref[0, 0], bc_ref[0, 1]
     wide = jnp.broadcast_to(docs.astype(F32), (SSM_DEV, TOK)).astype(BF16)
@@ -173,7 +227,7 @@
         )
         paired_sum = paired_sum + paired
         reaching = exact_right(paired * affinity, after, NN)
-        log_ref[h : h + 1] = jnp.sum(
+        aux_ref[0, h : h + 1] = jnp.sum(
             jnp.where(source < target, reaching, 0.0), axis=0, keepdims=True
         )
     shared_ref[0] = exact_right(paired_sum, reads, NN)
@@ -181,34 +235,26 @@
 
 
 def finish_ssm(
-    peers,
-    params_rows,
+    scale,
     in_ref,
     x_ref,
     dy_ref,
     bc_ref,
-    step_ref,
-    rate_ref,
-    docs_ref,
+    near_ref,
+    shared_ref,
+    aux_ref,
     sin_ref,
     sgr_ref,
-    near_ref,
-    shared_ref,
-    log_ref,
     dx_ref,
     step_grad_ref,
     share_ref,
     params_ref,
 ):
-    docs = docs_ref[...]
     table = head_table()
-    rate = head_column(rate_ref)
-    step = step_ref[0]
-    _, ending, entering, leaving = decays(step, rate, docs)
+    entering, leaving = aux_ref[1], aux_ref[2]
     leave_term = jnp.zeros((SSM_DEV, TOK), F32)
     enter_term = jnp.zeros((SSM_DEV, TOK), F32)
     across = jnp.zeros((SSM_DEV, 8), F32)
-    skips = jnp.zeros((8, SSM_DEV), F32)
     write_grad, read_grad = shared_ref[0], shared_ref[1]
     for g in range(SIDE):
         at = slice(g * GROUP_COLS, (g + 1) * GROUP_COLS)
@@ -222,40 +268,40 @@
         enter_term += exact_left(part, ahead * dy, NT)
         meeting = jnp.sum(state_in.astype(F32) * grad_in.astype(F32), axis=0, keepdims=True)
         across += exact_left(part, jnp.broadcast_to(meeting, (8, GROUP_COLS)), NT)
-        skip = jnp.sum(x * dy, axis=0, keepdims=True)
-        skips += exact_right(jnp.broadcast_to(skip, (8, GROUP_COLS)), part, NT, 3)
         write_grad += dot(sin_ref[:, at], grad_in, NT)
         read_grad += dot(sgr_ref[:, at], state_in, NT)
-    through = jnp.where(docs[:, :1] == docs[:, TOK - 1 :], jnp.exp(ending), 0.0)
     log_grad = (
-        log_ref[...]
+        aux_ref[0]
         + exact_right(enter_term, triangle(lambda u, t: u >= t), NN)
         + exact_right(leave_term, triangle(lambda s, t: s < t), NN)
-        + through * across[:, :1]
+        + aux_ref[3] * across[:, :1]
     )
-    step_grad_ref[0] = -rate * log_grad
-    rates = exact_left(jnp.ones((8, TOK), BF16), -step * log_grad, NT, 3)
-    rows = TOK // peers
+    step_grad_ref[0] = aux_ref[4] * log_grad
+    rates = exact_left(jnp.ones((8, TOK), BF16), aux_ref[5] * log_grad, NT, 3)
+    peers, _, rows, _ = share_ref.shape
     for k in range(peers):
         at = slice(k * rows, (k + 1) * rows)
         share_ref[k, 0] = write_grad[at].astype(BF16)
         share_ref[k, 1] = read_grad[at].astype(BF16)
-    both = jnp.concatenate(
-        [rates[:1], skips[:1], jnp.zeros((1, TOK - 2 * SSM_DEV), F32)], axis=1
-    )
-    params_ref[...] = jnp.broadcast_to(both, (params_rows, TOK))
-
-
-def attention(place_ref, in_ref, dq_ref, dkv_ref, key_scr, value_scr, doc_scr, total_scr):
+    both = jnp.concatenate([rates[:1], jnp.zeros((1, TOK - SSM_DEV), F32)], axis=1)
+    both = (both + aux_ref[6, :1]) * scale
+    params_ref[...] = jnp.broadcast_to(both, params_ref.shape)
+
+
+def attention(place_ref, *refs):
+    dq_ref, dkv_ref, query_scr, grad_scr, key_scr, value_scr, doc_scr, total_scr = refs[SIDE:]
     half, mine = place_ref[0], place_ref[1]
     scaling = WIDTH ** (-0.5)
 
-    for j in range(2 * SIDE):
-        which = lax.bitwise_xor(half, j // SIDE)
-        rows = pl.ds(j * TOK, TOK)
-        key_scr[rows] = in_ref[j % SIDE, which, 2 * TOK : 3 * TOK, :WIDTH]
-        value_scr[rows] = in_ref[j % SIDE, which, 2 * TOK : 3 * TOK, WIDTH:]
-        doc_scr[:, rows] = in_ref[j % SIDE, which, 3 * TOK :, :TOK].astype(F32)[:8]
+    for k in range(2):
+        for step, ref in enumerate(refs[:SIDE]):
+            shard_at = lax.bitwise_xor(half, k) * SIDE + lax.rem(mine + SIDE - step, SIDE)
+            rows = pl.ds(pl.multiple_of(shard_at * TOK, TOK), TOK)
+            query_scr[rows] = ref[k, :TOK]
+            grad_scr[rows] = ref[k, TOK : 2 * TOK]
+            key_scr[rows] = ref[k, 2 * TOK : 3 * TOK, :WIDTH]
+            value_scr[rows] = ref[k, 2 * TOK : 3 * TOK, WIDTH:]
+            doc_scr[:, rows] = ref[k, 3 * TOK :, :TOK].astype(F32)[:8]
 
     eye = triangle(lambda a, b: a == b)
     own_start = pl.multiple_of(mine * TOK, TOK)
@@ -267,9 +313,8 @@
     own_diff = iota((TOK, TOK), 1) - iota((TOK, TOK), 0)
 
     def rows_of(r, h):
-        which = lax.bitwise_xor(half, r // SIDE)
-        at = slice(h * WIDTH, (h + 1) * WIDTH)
-        return in_ref[r % SIDE, which, :TOK, at], in_ref[r % SIDE, which, TOK : 2 * TOK, at]
+        at, rows = slice(h * WIDTH, (h + 1) * WIDTH), pl.ds(pl.multiple_of(r * TOK, TOK), TOK)
+        return query_scr[rows, at], grad_scr[rows, at]
 
     def shard(r, own):
         start = pl.multiple_of(jnp.maximum(r - SIDE, 0) * TOK, TOK)
@@ -346,14 +391,6 @@
     def between(value):
         return lax.all_to_all(value, "ctx", 0, 0, axis_index_groups=sides, tiled=True)
 
-    docs_rows = jnp.broadcast_to(
-        jnp.pad(doc_ids.astype(BF16), ((0, 0), (0, 2 * WIDTH - TOK))), (META, 2 * WIDTH)
-    )
-    attention_own = jnp.concatenate(
-        [queries[0], attn_grad[0], jnp.concatenate([keyval[0, 0], keyval[0, 1]], axis=1), docs_rows]
-    )
-    attention_other = lax.ppermute(attention_own, "ctx", across)
-
     sent, scaled_in, scaled_grad = pl.pallas_call(
         local_states,
         out_shape=(
@@ -361,12 +398,34 @@
             shape((TOK, COLS), BF16),
             shape((TOK, COLS), BF16),
         ),
-        in_specs=whole(4) + [scalars()] + whole(1),
+        in_specs=[pl.BlockSpec(memory_space=pltpu.HBM)] * 5 + [scalars()],
         out_specs=tuple(whole(3)),
+        scratch_shapes=[
+            pltpu.VMEM(ssm_in.shape, BF16),
+            pltpu.VMEM(ssm_grad.shape, BF16),
+            pltpu.VMEM(bc_pair.shape, BF16),
+            pltpu.VMEM(step_size.shape, F32),
+            pltpu.VMEM(doc_ids.shape, jnp.int32),
+            pltpu.SemaphoreType.DMA((5,)),
+        ],
+        compiler_params=params(63),
+        name="local_states",
+    )(ssm_in, ssm_grad, bc_pair, step_size, doc_ids, decay_rate)
+    received = between(sent)
+
+    docs_after, _ = lax.optimization_barrier((doc_ids, sent))
+    own, own_pair = pl.pallas_call(
+        pack,
+        out_shape=(shape((ATT_ROWS, 2 * WIDTH), BF16), shape((TOK + META, 2 * WIDTH), BF16)),
+        in_specs=whole(4),
+        out_specs=tuple(whole(2)),
         compiler_params=params(),
-        name="local_states",
-    )(ssm_in, ssm_grad, bc_pair, step_size, decay_rate, doc_ids)
-    received = between(sent)
+        name="pack",
+    )(queries, attn_grad, keyval, docs_after)
+    from_above = lax.ppermute(own, "ctx", [(i + SIDE, i) for i in range(SIDE)])
+    from_below = lax.ppermute(own_pair, "ctx", [(i, i + SIDE) for i in range(SIDE)])
+
+    received, _ = lax.optimization_barrier((received, own))
     total = pl.pallas_call(
         half_totals,
         out_shape=shape((NS + META, GROUP_COLS), BF16),
@@ -377,28 +436,28 @@
     )(place, received)
     other_total = lax.ppermute(total, "ctx", across)
 
+    def round_side(value, step):
+        turn = [(i, (i & SIDE) | ((i + step) % SIDE)) for i in range(2 * SIDE)]
+        return lax.ppermute(value, "ctx", turn)
+
     step_after, _ = lax.optimization_barrier((step_size, total))
-    near, shared_near, log_near = pl.pallas_call(
+    near, shared_near, aux = pl.pallas_call(
         inside_shard,
         out_shape=(
             shape((TOK, COLS), F32),
             shape((2, TOK, NS), F32),
-            shape((SSM_DEV, TOK), F32),
+            shape((7, SSM_DEV, TOK), F32),
         ),
         in_specs=whole(4) + [scalars(), scalars()] + whole(1),
         out_specs=tuple(whole(3)),
         compiler_params=params(),
         name="inside_shard",
-        cost_estimate=pl.CostEstimate(flops=400 << 20, bytes_accessed=2 << 20, transcendentals=0),
+        cost_estimate=pl.CostEstimate(flops=1 << 10, bytes_accessed=1 << 10, transcendentals=0),
     )(ssm_in, ssm_grad, bc_pair, step_after, decay_rate, skip_gain, doc_ids)
 
-    own_after, _ = lax.optimization_barrier((attention_own, log_near))
-    gathered = between(
-        jnp.broadcast_to(
-            jnp.stack([own_after, attention_other])[None], (SIDE, 2, ATT_ROWS, 2 * WIDTH)
-        )
+    received, aux, from_above, from_below = lax.optimization_barrier(
+        (received, aux, from_above, from_below)
     )
-
     entering = pl.pallas_call(
         entering_states,
         out_shape=shape((SIDE, 2 * NS, GROUP_COLS), BF16),
@@ -409,42 +468,39 @@
     )(place, received, other_total)
     entered = between(entering)
 
+    from_above, from_below, _ = lax.optimization_barrier((from_above, from_below, entering))
+    other = from_above + jnp.pad(from_below, ((2 * TOK, 0), (0, 0)))
+    halves = jnp.stack([own, other])
+    shards = [halves] + [round_side(halves, step) for step in range(1, SIDE)]
+
+    near, _ = lax.optimization_barrier((near, halves))
+    scale = 1.0 / math.sqrt(everyone * TOK * PD)
     input_grad, step_grad, share, both = pl.pallas_call(
-        functools.partial(finish_ssm, peers, everyone),
+        functools.partial(finish_ssm, scale),
         out_shape=(
             shape((1, TOK, COLS), BF16),
             shape((1, SSM_DEV, TOK), F32),
             shape((peers, 2, TOK // peers, NS), BF16),
             shape((everyone, TOK), F32),
         ),
-        in_specs=whole(5) + [scalars()] + whole(6),
+        in_specs=whole(9),
         out_specs=tuple(whole(4)),
         compiler_params=params(),
         name="finish_ssm",
-    )(
-        entered,
-        ssm_in,
-        ssm_grad,
-        bc_pair,
-        step_size,
-        decay_rate,
-        doc_ids,
-        scaled_in,
-        scaled_grad,
-        near,
-        shared_near,
-        log_near,
-    )
+    )(entered, ssm_in, ssm_grad, bc_pair, near, shared_near, aux, scaled_in, scaled_grad)
+    shares = lax.all_to_all(share, "head", 0, 0, tiled=True)
+    both, shares = lax.optimization_barrier((both, shares))
     everywhere = lax.all_to_all(both, ("dp", "ctx"), 0, 0, tiled=True)
-    shares = lax.all_to_all(share, "head", 0, 0, tiled=True)
-
-    gathered, _ = lax.optimization_barrier((gathered, both))
+
+    shards, _ = lax.optimization_barrier((shards, both))
     query_grad, keyval_grad = pl.pallas_call(
         attention,
         out_shape=(shape((1, TOK, 2 * WIDTH), BF16), shape((1, 2, TOK, WIDTH), BF16)),
-        in_specs=[scalars()] + whole(1),
+        in_specs=[scalars()] + whole(SIDE),
         out_specs=tuple(whole(2)),
         scratch_shapes=[
+            pltpu.VMEM((2 * SIDE * TOK, 2 * WIDTH), BF16),
+            pltpu.VMEM((2 * SIDE * TOK, 2 * WIDTH), BF16),
             pltpu.VMEM((2 * SIDE * TOK, WIDTH), BF16),
             pltpu.VMEM((2 * SIDE * TOK, WIDTH), BF16),
             pltpu.VMEM((8, 2 * SIDE * TOK), F32),
@@ -453,11 +509,11 @@
         compiler_params=params(),
         name="attention",
         cost_estimate=pl.CostEstimate(flops=2 << 30, bytes_accessed=4 << 20, transcendentals=1 << 20),
-    )(place, gathered)
-
+    )(place, *shards)
+
+    everywhere, shares, query_grad = lax.optimization_barrier((everywhere, shares, query_grad))
     shared_grad = jnp.sum(shares.astype(F32), axis=0)[None]
-    totals = jnp.sum(everywhere, axis=0)[: 2 * SSM_DEV].reshape(2, SSM_DEV)
-    param_grads = totals / math.sqrt(lax.axis_size("dp") * lax.axis_size("ctx") * TOK * PD)
+    param_grads = jnp.sum(everywhere, axis=0)[: 2 * SSM_DEV].reshape(2, SSM_DEV)
     return (query_grad, keyval_grad, input_grad, shared_grad, step_grad, param_grads)
 
 

time: 133 us -> 106 us (0.80)
  waiting for transfers between devices: 39.9 us -> 13 us
  starting transfers between devices: 52 us -> 58.7 us
  local copies, waits for them, and re-layouts: 6.77 us -> 0.71 us
    all_to_all x3 -> x2, waiting for transfers between devices: 25.2 us -> 0.01 us  [between(): lax.all_to_all(value, 'ctx', 0, 0, axis_index_groups=sides, tiled=True)]
    ppermute x1 -> x5, starting transfers between devices: 13.3 us -> 26.4 us  [the longest x1 15.5 us: body(): lax.ppermute(own_pair, 'ctx', [(i, i + SIDE) for i in range(SIDE)])]
    ppermute x1, starting transfers between devices: 17.2 us -> 7.41 us  [body(): other_total = lax.ppermute(total, 'ctx', across)]
    all_to_all x1, waiting for transfers between devices: 13 us -> 4.72 us  [body(): everywhere = lax.all_to_all(both, ('dp', 'ctx'), 0, 0, tiled=True)]
    ppermute x1, waiting for transfers between devices: 1.79 us -> 8.29 us  [body(): other_total = lax.ppermute(total, 'ctx', across)]
    unnamed x32 -> x24, local copies, waits for them, and re-layouts: 4.78 us -> 0.06 us
    all_to_all x1, starting transfers between devices: 9.5 us -> 14.2 us  [body(): everywhere = lax.all_to_all(both, ('dp', 'ctx'), 0, 0, tiled=True)]
    all_to_all x3 -> x2, starting transfers between devices: 11.9 us -> 10.7 us  [between(): lax.all_to_all(value, 'ctx', 0, 0, axis_index_groups=sides, tiled=True)]
  transfers between devices with their start and end apart: 6 -> 9, of which waited for: 4 -> 2; matrix products, arithmetic and copies ran while one was open for 1% -> 0% of each run, Pallas kernels for 5% -> 14%
where the time goes in v2:
time: 106 us
  starting transfers between devices  58.7 us (55%)
  Pallas kernels  19.7 us (19%)
  waiting for transfers between devices  13 us (12%)
  blocking collectives  11.8 us (11%)
    ppermute x1, starting transfers between devices, body(): lax.ppermute(own_pair, 'ctx', [(i, i + SIDE) for i in range(SIDE)])  15.5 us
    all_to_all x1, starting transfers between devices, body(): everywhere = lax.all_to_all(both, ('dp', 'ctx'), 0, 0, tiled=True)  14.2 us
    all_to_all x1, blocking collectives, body(): shares = lax.all_to_all(share, 'head', 0, 0, tiled=True)  11.8 us
    all_to_all x2, starting transfers between devices, between(): lax.all_to_all(value, 'ctx', 0, 0, axis_index_groups=sides, tiled=True)  10.7 us
    ppermute x3, starting transfers between devices, round_side(): return lax.ppermute(value, 'ctx', turn)  9.69 us
    pallas_call x1, Pallas kernels, body(): pl.pallas_call(attention, out_shape=(shape((1, TOK, 2 * WIDTH), BF16), sh...  8.31 us
    ppermute x1, waiting for transfers between devices, body(): other_total = lax.ppermute(total, 'ctx', across)  8.29 us
    ppermute x1, starting transfers between devices, body(): other_total = lax.ppermute(total, 'ctx', across)  7.41 us
  transfers between devices with their start and end apart: 9, of which 2 were waited for; matrix products, arithmetic and copies ran while one was open for 0% of the time, Pallas kernels for 14%

profile of v2, /device:TPU:1, one launch (start us, length us, event | category | flops | bytes accessed | tf_op | source)
XLA Modules:
  0.0 105.7 jit_solution(6416048098573290973)
XLA Ops:
  0.6 3.5 %local_states.1 = (bf16[4,272,256]{2,1,0:T(8,128)(2,1)}, bf16[128,1024]{1,0:T(8,128)(2,1)}, bf16[128,1024]{1,0:T(8,128)(2,1)}) custom-call(bf16[1,128,1024]{2,1,0:T(8,128)(2,1)} %x_ref.3, bf16[1,128,1024]{2,1,0:T(8,128)(2,1)} %dy_ref.3, bf16[1,2,128,128]{3,2,1,0:T(8,128)(2,1)} %bc_ref.3, f32[1,16,128]{2,1,0:T(8,128)} %step_ref, s32[1,128]{1,0:T(1,128)} %docs_ref.2, ...), custom_call_target="tpu_custom_call" | custom-call | tf_op jit(solution)/shard_map/local_states/pallas_call | solution.py:394
  4.2 0.0 copy-start.5
  4.2 0.0 copy-start.6
  4.2 0.0 copy-start.7
  4.2 0.0 copy-start.9
  4.2 5.0 %all-to-all-start = ((bf16[4,272,256]{2,1,0:T(8,128)(2,1)}), bf16[4,272,256]{2,1,0:T(8,128)(2,1)S(1)}, u32[]{:S(2)}, u32[]{:S(2)}) async-start(bf16[4,272,256]{2,1,0:T(8,128)(2,1)} %get-tuple-element.39), calls=%async_computation | async-start | bytes 1114112 | tf_op jit(solution)/shard_map/all_to_all | solution.py:392
  9.2 0.0 copy-done.5
  9.2 0.0 copy-done.6
  9.2 0.0 copy-done.7
  9.2 0.0 copy-done.9
  9.3 1.3 %collective-permute-start = (bf16[400,256]{1,0:T(8,128)(2,1)S(1)}, bf16[400,256]{1,0:T(8,128)(2,1)S(1)}, u32[]{:S(2)}, u32[]{:S(2)}) collective-permute-start(bf16[400,256]{1,0:T(8,128)(2,1)S(1)} %get-tuple-element.41), channel_id=1, source_target_pairs={{32,0},{40,8},{48,16},{56,24},{33,1},{41,9},{49,17},{57,25},{34,2}... | collective-permute-start | bytes 614408 | tf_op jit(solution)/shard_map/ppermute | solution.py:425
  10.6 15.5 %collective-permute-start.1 = (bf16[144,256]{1,0:T(8,128)(2,1)S(1)}, bf16[144,256]{1,0:T(8,128)(2,1)S(1)}, u32[]{:S(2)}, u32[]{:S(2)}) collective-permute-start(bf16[144,256]{1,0:T(8,128)(2,1)S(1)} %get-tuple-element.45), channel_id=1, source_target_pairs={{0,32},{8,40},{16,48},{24,56},{1,33},{9,41},{17,49},{25,57},{2,34}... | collective-permute-start | bytes 221192 | tf_op jit(solution)/shard_map/ppermute | solution.py:426
  26.0 0.1 pad_add_fusion.half_ref.place_ref
  26.1 0.0 copy-start
  26.1 0.0 copy-start.1
  26.1 0.0 copy-start.2
  26.1 0.0 copy-start.8
  26.1 0.0 copy-start.10
  26.1 0.0 copy-start.11
  26.2 0.0 all-to-all-done.ref
  26.2 0.8 half_totals.1
  27.0 7.4 %collective-permute-start.2 = (bf16[144,256]{1,0:T(8,128)(2,1)S(1)}, bf16[144,256]{1,0:T(8,128)(2,1)S(1)}, u32[]{:S(2)}, u32[]{:S(2)}) collective-permute-start(bf16[144,256]{1,0:T(8,128)(2,1)S(1)} %half_totals.1), channel_id=1, source_target_pairs={{0,32},{8,40},{16,48},{24,56},{32,0},{40,8},{48,16},{56,24},{1,33}... | collective-permute-start | bytes 221192 | tf_op jit(solution)/shard_map/ppermute | solution.py:437
  34.4 0.0 copy-done
  34.4 0.0 copy-done.1
  34.4 0.0 copy-done.2
  34.4 0.0 copy-done.8
  34.5 0.0 copy-done.10
  34.5 0.0 copy-done.11
  34.5 3.0 %inside_shard.1 = (f32[128,1024]{1,0:T(8,128)S(1)}, f32[2,128,128]{2,1,0:T(8,128)S(1)}, f32[7,16,128]{2,1,0:T(8,128)S(1)}) custom-call(bf16[1,128,1024]{2,1,0:T(8,128)(2,1)S(1)} %copy-done, bf16[1,128,1024]{2,1,0:T(8,128)(2,1)S(1)} %copy-done.1, bf16[1,2,128,128]{3,2,1,0:T(8,128)(2,1)S(1)} %copy-done.2, f32[1,16,128]{2,1,0:T(8,128)S(1)} %copy-done.8, ...), custom_call_target="tpu_custom_call" | custom-call | flops 1024 | bytes 1024 | tf_op jit(solution)/shard_map/inside_shard/pallas_call | solution.py:444
  37.5 0.0 collective-permute-done.1
  37.5 0.0 collective-permute-done
  37.5 8.3 %collective-permute-done.2.other_ref = bf16[144,256]{1,0:T(8,128)(2,1)S(1)} collective-permute-done((bf16[144,256]{1,0:T(8,128)(2,1)S(1)}, bf16[144,256]{1,0:T(8,128)(2,1)S(1)}, u32[]{:S(2)}, u32[]{:S(2)}) %collective-permute-start.2) | collective-permute-done | bytes 73760 | tf_op jit(solution)/shard_map/ppermute | solution.py:437
  45.8 1.6 %entering_states.1 = bf16[4,256,256]{2,1,0:T(8,128)(2,1)} custom-call(s32[2]{0:T(128)S(1)} %pad_add_fusion.half_ref.place_ref, bf16[4,272,256]{2,1,0:T(8,128)(2,1)S(1)} %all-to-all-done.ref, bf16[144,256]{1,0:T(8,128)(2,1)S(1)} %collective-permute-done.2.other_ref), custom_call_target="tpu_custom_call" | custom-call | tf_op jit(solution)/shard_map/entering_states/pallas_call | solution.py:461
  47.5 5.7 %all-to-all-start.1 = ((bf16[4,256,256]{2,1,0:T(8,128)(2,1)}), bf16[4,256,256]{2,1,0:T(8,128)(2,1)S(1)}, u32[]{:S(2)}, u32[]{:S(2)}) async-start(bf16[4,256,256]{2,1,0:T(8,128)(2,1)} %entering_states.1), calls=%async_computation.1 | async-start | bytes 1048576 | tf_op jit(solution)/shard_map/all_to_all | solution.py:392
  53.2 0.0 copy-start.3
  53.2 0.0 copy-start.4
  53.2 4.7 %collective-permute-start.5 = (bf16[2,400,256]{2,1,0:T(8,128)(2,1)S(1)}, bf16[2,400,256]{2,1,0:T(8,128)(2,1)S(1)}, u32[]{:S(2)}, u32[]{:S(2)}) collective-permute-start(bf16[2,400,256]{2,1,0:T(8,128)(2,1)S(1)} %pad_maximum_fusion.refs_0_), channel_id=1, source_target_pairs={{0,24},{8,0},{16,8},{24,16},{32,56},{40,32},{48,40},{56,48},{1,25}... | collective-permute-start | bytes 1228808 | tf_op jit(solution)/shard_map/ppermute | solution.py:441
  58.0 2.5 %collective-permute-start.4 = (bf16[2,400,256]{2,1,0:T(8,128)(2,1)S(1)}, bf16[2,400,256]{2,1,0:T(8,128)(2,1)}, u32[]{:S(2)}, u32[]{:S(2)}) collective-permute-start(bf16[2,400,256]{2,1,0:T(8,128)(2,1)S(1)} %pad_maximum_fusion.refs_0_), channel_id=1, source_target_pairs={{0,16},{8,24},{16,0},{24,8},{32,48},{40,56},{48,32},{56,40},{1,17}... | collective-permute-start | bytes 1228808 | tf_op jit(solution)/shard_map/ppermute | solution.py:441
  60.5 2.5 %collective-permute-start.3 = (bf16[2,400,256]{2,1,0:T(8,128)(2,1)S(1)}, bf16[2,400,256]{2,1,0:T(8,128)(2,1)}, u32[]{:S(2)}, u32[]{:S(2)}) collective-permute-start(bf16[2,400,256]{2,1,0:T(8,128)(2,1)S(1)} %pad_maximum_fusion.refs_0_), channel_id=1, source_target_pairs={{0,8},{8,16},{16,24},{24,0},{32,40},{40,48},{48,56},{56,32},{1,9},... | collective-permute-start | bytes 1228808 | tf_op jit(solution)/shard_map/ppermute | solution.py:441
  63.0 0.0 all-to-all-done.1.in_ref
  63.0 0.0 copy-done.3
  63.0 0.0 copy-done.4
  63.0 2.4 %finish_ssm.1 = (bf16[1,128,1024]{2,1,0:T(8,128)(2,1)}, f32[1,16,128]{2,1,0:T(8,128)}, bf16[8,2,16,128]{3,2,1,0:T(8,128)(2,1)S(1)}, f32[64,128]{1,0:T(8,128)}) custom-call(bf16[4,256,256]{2,1,0:T(8,128)(2,1)S(1)} %all-to-all-done.1.in_ref, bf16[1,128,1024]{2,1,0:T(8,128)(2,1)S(1)} %copy-done, bf16[1,128,1024]{2,1,0:T(8,128)(2,1)S(1)} %copy-done.1, ...), custom_call_target="tpu_custom_call" | custom-call | tf_op jit(solution)/shard_map/finish_ssm/pallas_call | solution.py:478
  65.3 11.8 %all_to_all.27 = bf16[8,2,16,128]{3,2,1,0:T(8,128)(2,1)S(1)} all-to-all(bf16[8,2,16,128]{3,2,1,0:T(8,128)(2,1)S(1)} %get-tuple-element.58), channel_id=1, replica_groups=mesh['dp'=8,'ctx'=8,'head'=8] {'head'}, dimensions={0} | all-to-all | bytes 131072 | tf_op jit(solution)/shard_map/all_to_all | solution.py:491
  77.1 14.2 %all-to-all-start.3 = ((f32[64,1,128]{2,1,0:T(1,128)}), f32[64,1,128]{2,1,0:T(1,128)S(1)}, u32[]{:S(2)}, u32[]{:S(2)}) async-start(f32[64,1,128]{2,1,0:T(1,128)} %bitcast.5), calls=%async_computation.3 | async-start | bytes 65536 | tf_op jit(solution)/shard_map/all_to_all | solution.py:493
  91.3 0.0 collective-permute-done.5.refs_3_
  91.3 0.0 collective-permute-done.4.refs_2_
  91.3 0.0 collective-permute-done.3.refs_1_
  91.3 8.3 %attention.1 = (bf16[1,128,256]{2,1,0:T(8,128)(2,1)}, bf16[1,2,128,128]{3,2,1,0:T(8,128)(2,1)}) custom-call(s32[2]{0:T(128)S(1)} %pad_add_fusion.half_ref.place_ref, bf16[2,400,256]{2,1,0:T(8,128)(2,1)S(1)} %pad_maximum_fusion.refs_0_, bf16[2,400,256]{2,1,0:T(8,128)(2,1)} %collective-permute-done.3.refs_1_, ...), custom_call_target="tpu_custom_call" | custom-call | flops 2147483648 | bytes 4194304 | tf_op jit(solution)/shard_map/attention/pallas_call | solution.py:496
  99.6 4.7 %all-to-all-done.3 = f32[64,1,128]{2,1,0:T(1,128)S(1)} async-done(((f32[64,1,128]{2,1,0:T(1,128)}), f32[64,1,128]{2,1,0:T(1,128)S(1)}, u32[]{:S(2)}, u32[]{:S(2)}) %all-to-all-start.3) | async-done | bytes 32800 | tf_op jit(solution)/shard_map/all_to_all | solution.py:493
  104.4 0.6 reshape.25
  105.0 0.6 convert_reduce_fusion
  (4 shorter events, 0.1 us)
Async XLA Ops:
  4.2 5.0 %copy-start.5 = (bf16[1,128,256]{2,1,0:T(8,128)(2,1)S(1)}, bf16[1,128,256]{2,1,0:T(8,128)(2,1)}, u32[]{:S(2)}) copy-start(bf16[1,128,256]{2,1,0:T(8,128)(2,1)} %queries_ref.1) | copy-start | bytes 196612
  4.2 5.0 %copy-start.6 = (bf16[1,128,256]{2,1,0:T(8,128)(2,1)S(1)}, bf16[1,128,256]{2,1,0:T(8,128)(2,1)}, u32[]{:S(2)}) copy-start(bf16[1,128,256]{2,1,0:T(8,128)(2,1)} %grads_ref.1) | copy-start | bytes 196612
  4.2 5.0 %copy-start.7 = (bf16[1,2,128,128]{3,2,1,0:T(8,128)(2,1)S(1)}, bf16[1,2,128,128]{3,2,1,0:T(8,128)(2,1)}, u32[]{:S(2)}) copy-start(bf16[1,2,128,128]{3,2,1,0:T(8,128)(2,1)} %keyval_ref.1) | copy-start | bytes 196612
  4.2 5.0 %copy-start.9 = (s32[1,128]{1,0:T(1,128)S(1)}, s32[1,128]{1,0:T(1,128)}, u32[]{:S(2)}) copy-start(s32[1,128]{1,0:T(1,128)} %docs_ref.2) | copy-start | bytes 1540
  4.2 21.9 %all-to-all-start = ((bf16[4,272,256]{2,1,0:T(8,128)(2,1)}), bf16[4,272,256]{2,1,0:T(8,128)(2,1)S(1)}, u32[]{:S(2)}, u32[]{:S(2)}) async-start(bf16[4,272,256]{2,1,0:T(8,128)(2,1)} %get-tuple-element.39), calls=%async_computation | async-start | bytes 1114112 | tf_op jit(solution)/shard_map/all_to_all | solution.py:392
  9.3 28.3 %collective-permute-start = (bf16[400,256]{1,0:T(8,128)(2,1)S(1)}, bf16[400,256]{1,0:T(8,128)(2,1)S(1)}, u32[]{:S(2)}, u32[]{:S(2)}) collective-permute-start(bf16[400,256]{1,0:T(8,128)(2,1)S(1)} %get-tuple-element.41), channel_id=1, source_target_pairs={{32,0},{40,8},{48,16},{56,24},{33,1},{41,9},{49,17},{57,25},{34,2}... | collective-permute-start | bytes 614408 | tf_op jit(solution)/shard_map/ppermute | solution.py:425
  10.6 26.9 %collective-permute-start.1 = (bf16[144,256]{1,0:T(8,128)(2,1)S(1)}, bf16[144,256]{1,0:T(8,128)(2,1)S(1)}, u32[]{:S(2)}, u32[]{:S(2)}) collective-permute-start(bf16[144,256]{1,0:T(8,128)(2,1)S(1)} %get-tuple-element.45), channel_id=1, source_target_pairs={{0,32},{8,40},{16,48},{24,56},{1,33},{9,41},{17,49},{25,57},{2,34}... | collective-permute-start | bytes 221192 | tf_op jit(solution)/shard_map/ppermute | solution.py:426
  26.1 8.3 %copy-start = (bf16[1,128,1024]{2,1,0:T(8,128)(2,1)S(1)}, bf16[1,128,1024]{2,1,0:T(8,128)(2,1)}, u32[]{:S(2)}) copy-start(bf16[1,128,1024]{2,1,0:T(8,128)(2,1)} %x_ref.3) | copy-start | bytes 786436
  26.1 8.3 %copy-start.1 = (bf16[1,128,1024]{2,1,0:T(8,128)(2,1)S(1)}, bf16[1,128,1024]{2,1,0:T(8,128)(2,1)}, u32[]{:S(2)}) copy-start(bf16[1,128,1024]{2,1,0:T(8,128)(2,1)} %dy_ref.3) | copy-start | bytes 786436
  26.1 8.3 %copy-start.2 = (bf16[1,2,128,128]{3,2,1,0:T(8,128)(2,1)S(1)}, bf16[1,2,128,128]{3,2,1,0:T(8,128)(2,1)}, u32[]{:S(2)}) copy-start(bf16[1,2,128,128]{3,2,1,0:T(8,128)(2,1)} %bc_ref.3) | copy-start | bytes 196612
  26.1 8.3 %copy-start.8 = (f32[1,16,128]{2,1,0:T(8,128)S(1)}, f32[1,16,128]{2,1,0:T(8,128)}, u32[]{:S(2)}) copy-start(f32[1,16,128]{2,1,0:T(8,128)} %step_ref) | copy-start | bytes 24580
  26.1 8.3 %copy-start.10 = (f32[16]{0:T(128)S(1)}, f32[16]{0:T(128)}, u32[]{:S(2)}) copy-start(f32[16]{0:T(128)} %rate_ref.3) | copy-start | bytes 196
  26.1 8.3 %copy-start.11 = (f32[16]{0:T(128)S(1)}, f32[16]{0:T(128)}, u32[]{:S(2)}) copy-start(f32[16]{0:T(128)} %skip_ref.1) | copy-start | bytes 196
  27.0 18.8 %collective-permute-start.2 = (bf16[144,256]{1,0:T(8,128)(2,1)S(1)}, bf16[144,256]{1,0:T(8,128)(2,1)S(1)}, u32[]{:S(2)}, u32[]{:S(2)}) collective-permute-start(bf16[144,256]{1,0:T(8,128)(2,1)S(1)} %half_totals.1), channel_id=1, source_target_pairs={{0,32},{8,40},{16,48},{24,56},{32,0},{40,8},{48,16},{56,24},{1,33}... | collective-permute-start | bytes 221192 | tf_op jit(solution)/shard_map/ppermute | solution.py:437
  47.5 15.5 %all-to-all-start.1 = ((bf16[4,256,256]{2,1,0:T(8,128)(2,1)}), bf16[4,256,256]{2,1,0:T(8,128)(2,1)S(1)}, u32[]{:S(2)}, u32[]{:S(2)}) async-start(bf16[4,256,256]{2,1,0:T(8,128)(2,1)} %entering_states.1), calls=%async_computation.1 | async-start | bytes 1048576 | tf_op jit(solution)/shard_map/all_to_all | solution.py:392
  53.2 9.8 %copy-start.3 = (bf16[128,1024]{1,0:T(8,128)(2,1)S(1)}, bf16[128,1024]{1,0:T(8,128)(2,1)}, u32[]{:S(2)}) copy-start(bf16[128,1024]{1,0:T(8,128)(2,1)} %get-tuple-element.55.sin_ref) | copy-start | bytes 786436
  53.2 9.8 %copy-start.4 = (bf16[128,1024]{1,0:T(8,128)(2,1)S(1)}, bf16[128,1024]{1,0:T(8,128)(2,1)}, u32[]{:S(2)}) copy-start(bf16[128,1024]{1,0:T(8,128)(2,1)} %get-tuple-element.56.sgr_ref) | copy-start | bytes 786436
  53.2 38.1 %collective-permute-start.5 = (bf16[2,400,256]{2,1,0:T(8,128)(2,1)S(1)}, bf16[2,400,256]{2,1,0:T(8,128)(2,1)S(1)}, u32[]{:S(2)}, u32[]{:S(2)}) collective-permute-start(bf16[2,400,256]{2,1,0:T(8,128)(2,1)S(1)} %pad_maximum_fusion.refs_0_), channel_id=1, source_target_pairs={{0,24},{8,0},{16,8},{24,16},{32,56},{40,32},{48,40},{56,48},{1,25}... | collective-permute-start | bytes 1228808 | tf_op jit(solution)/shard_map/ppermute | solution.py:441
  58.0 33.4 %collective-permute-start.4 = (bf16[2,400,256]{2,1,0:T(8,128)(2,1)S(1)}, bf16[2,400,256]{2,1,0:T(8,128)(2,1)}, u32[]{:S(2)}, u32[]{:S(2)}) collective-permute-start(bf16[2,400,256]{2,1,0:T(8,128)(2,1)S(1)} %pad_maximum_fusion.refs_0_), channel_id=1, source_target_pairs={{0,16},{8,24},{16,0},{24,8},{32,48},{40,56},{48,32},{56,40},{1,17}... | collective-permute-start | bytes 1228808 | tf_op jit(solution)/shard_map/ppermute | solution.py:441
  60.5 30.9 %collective-permute-start.3 = (bf16[2,400,256]{2,1,0:T(8,128)(2,1)S(1)}, bf16[2,400,256]{2,1,0:T(8,128)(2,1)}, u32[]{:S(2)}, u32[]{:S(2)}) collective-permute-start(bf16[2,400,256]{2,1,0:T(8,128)(2,1)S(1)} %pad_maximum_fusion.refs_0_), channel_id=1, source_target_pairs={{0,8},{8,16},{16,24},{24,0},{32,40},{40,48},{48,56},{56,32},{1,9},... | collective-permute-start | bytes 1228808 | tf_op jit(solution)/shard_map/ppermute | solution.py:441
  77.1 27.2 %all-to-all-start.3 = ((f32[64,1,128]{2,1,0:T(1,128)}), f32[64,1,128]{2,1,0:T(1,128)S(1)}, u32[]{:S(2)}, u32[]{:S(2)}) async-start(f32[64,1,128]{2,1,0:T(1,128)} %bitcast.5), calls=%async_computation.3 | async-start | bytes 65536 | tf_op jit(solution)/shard_map/all_to_all | solution.py:493

commit v3 on v2

--- a/solution.py
+++ b/solution.py
@@ -132,7 +132,9 @@
         out_ref[g, 2 * NS :] = jnp.where(row == 0, wide_docs, meta).astype(BF16)
 
 
-def pack(queries_ref, grads_ref, keyval_ref, docs_ref, out_ref, pair_ref):
+def pack(queries_ref, grads_ref, keyval_ref, docs_ref, out_ref, pair_ref, rows_ref, cots_ref):
+    rows_ref[...] = queries_ref[0]
+    cots_ref[...] = grads_ref[0]
     out_ref[:TOK] = queries_ref[0]
     out_ref[TOK : 2 * TOK] = grads_ref[0]
     out_ref[2 * TOK : 3 * TOK, :WIDTH] = keyval_ref[0, 0]
@@ -203,9 +205,9 @@
     aux_ref[4] = -rate
     aux_ref[5] = -step_ref[0]
     skip = jnp.sum(x_ref[0].astype(F32) * dy_ref[0].astype(F32), axis=0, keepdims=True)
-    lanes, row = iota((TOK, COLS), 1), iota((TOK, COLS), 0) - SSM_DEV
-    later_table = jnp.where((lanes >= row * PD) & (lanes < (row + 1) * PD), 1.0, 0.0).astype(BF16)
-    skips = exact_right(jnp.broadcast_to(skip, (SSM_DEV, COLS)), later_table, NT, 3)
+    lanes, row = iota((TOK, COLS), 1), iota((TOK, COLS), 0)
+    wide_table = jnp.where((lanes >= row * PD) & (lanes < (row + 1) * PD), 1.0, 0.0).astype(BF16)
+    skips = exact_right(jnp.broadcast_to(skip, (SSM_DEV, COLS)), wide_table, NT, 3)
     aux_ref[6] = skips
     cumulative_t = exact_left(triangle(lambda t, s: s <= t), log_decay, NT, 3)
     writes, reads = bc_ref[0, 0], bc_ref[0, 1]
@@ -283,9 +285,11 @@
         at = slice(k * rows, (k + 1) * rows)
         share_ref[k, 0] = write_grad[at].astype(BF16)
         share_ref[k, 1] = read_grad[at].astype(BF16)
-    both = jnp.concatenate([rates[:1], jnp.zeros((1, TOK - SSM_DEV), F32)], axis=1)
-    both = (both + aux_ref[6, :1]) * scale
-    params_ref[...] = jnp.broadcast_to(both, params_ref.shape)
+    rates = jnp.concatenate([rates[:1], jnp.zeros((1, TOK - SSM_DEV), F32)], axis=1)
+    for row, value in enumerate((rates, aux_ref[6, :1])):
+        params_ref[:, row : row + 1, :] = jnp.broadcast_to(
+            (value * scale)[None], (params_ref.shape[0], 1, TOK)
+        )
 
 
 def attention(place_ref, *refs):
@@ -388,6 +392,30 @@
     sides = [list(range(SIDE)), list(range(SIDE, 2 * SIDE))]
     across = [(i, i ^ SIDE) for i in range(2 * SIDE)]
 
+    half_ring = lax.axis_size("dp")
+
+    def at_place(place_on_ring, x):
+        return (place_on_ring % half_ring) * 2 * SIDE + (place_on_ring // half_ring) * SIDE + x
+
+    def stops(k, sign):
+        step = k - sign
+        return k + half_ring, step % half_ring, k
+
+    def leg(number, sign):
+        return [
+            (at_place(stops(k, sign)[number], x), at_place(stops(k, sign)[number + 1], x))
+            for k in range(half_ring)
+            for x in range(SIDE)
+            if 0 <= k - sign < half_ring
+        ]
+
+    straight = [
+        (at_place(k + half_ring, x), at_place(k, x))
+        for k in sorted({0, half_ring - 1})
+        for x in range(SIDE)
+    ]
+    at_start = lax.axis_index("dp") == 0
+
     def between(value):
         return lax.all_to_all(value, "ctx", 0, 0, axis_index_groups=sides, tiled=True)
 
@@ -414,33 +442,24 @@
     received = between(sent)
 
     docs_after, _ = lax.optimization_barrier((doc_ids, sent))
-    own, own_pair = pl.pallas_call(
+    own, own_pair, own_rows, own_cots = pl.pallas_call(
         pack,
-        out_shape=(shape((ATT_ROWS, 2 * WIDTH), BF16), shape((TOK + META, 2 * WIDTH), BF16)),
+        out_shape=(
+            shape((ATT_ROWS, 2 * WIDTH), BF16),
+            shape((TOK + META, 2 * WIDTH), BF16),
+            shape((TOK, 2 * WIDTH), BF16),
+            shape((TOK, 2 * WIDTH), BF16),
+        ),
         in_specs=whole(4),
-        out_specs=tuple(whole(2)),
+        out_specs=tuple(whole(4)),
         compiler_params=params(),
         name="pack",
     )(queries, attn_grad, keyval, docs_after)
-    from_above = lax.ppermute(own, "ctx", [(i + SIDE, i) for i in range(SIDE)])
-    from_below = lax.ppermute(own_pair, "ctx", [(i, i + SIDE) for i in range(SIDE)])
-
-    received, _ = lax.optimization_barrier((received, own))
-    total = pl.pallas_call(
-        half_totals,
-        out_shape=shape((NS + META, GROUP_COLS), BF16),
-        in_specs=[scalars()] + whole(1),
-        out_specs=whole(1)[0],
-        compiler_params=params(),
-        name="half_totals",
-    )(place, received)
-    other_total = lax.ppermute(total, "ctx", across)
-
-    def round_side(value, step):
-        turn = [(i, (i & SIDE) | ((i + step) % SIDE)) for i in range(2 * SIDE)]
-        return lax.ppermute(value, "ctx", turn)
-
-    step_after, _ = lax.optimization_barrier((step_size, total))
+    ends = lax.ppermute(jnp.where(at_start, own_cots, own_rows), ("dp", "ctx"), straight)
+    near_rows = lax.ppermute(own_rows, ("dp", "ctx"), leg(0, -1))
+    near_cots = lax.ppermute(own_cots, ("dp", "ctx"), leg(0, 1))
+
+    step_after, _ = lax.optimization_barrier((step_size, own))
     near, shared_near, aux = pl.pallas_call(
         inside_shard,
         out_shape=(
@@ -455,9 +474,26 @@
         cost_estimate=pl.CostEstimate(flops=1 << 10, bytes_accessed=1 << 10, transcendentals=0),
     )(ssm_in, ssm_grad, bc_pair, step_after, decay_rate, skip_gain, doc_ids)
 
-    received, aux, from_above, from_below = lax.optimization_barrier(
-        (received, aux, from_above, from_below)
-    )
+    received, aux = lax.optimization_barrier((received, aux))
+    total = pl.pallas_call(
+        half_totals,
+        out_shape=shape((NS + META, GROUP_COLS), BF16),
+        in_specs=[scalars()] + whole(1),
+        out_specs=whole(1)[0],
+        compiler_params=params(),
+        name="half_totals",
+    )(place, received)
+    other_total = lax.ppermute(total, "ctx", across)
+    own_pair, _ = lax.optimization_barrier((own_pair, total))
+    other_pair = lax.ppermute(own_pair, "ctx", across)
+
+    def round_side(value, step):
+        turn = [(i, (i & SIDE) | ((i + step) % SIDE)) for i in range(2 * SIDE)]
+        return lax.ppermute(value, "ctx", turn)
+
+    rows_above = lax.ppermute(near_rows, ("dp", "ctx"), leg(1, -1))
+    cots_above = lax.ppermute(near_cots, ("dp", "ctx"), leg(1, 1))
+    above = (rows_above, cots_above, ends)
     entering = pl.pallas_call(
         entering_states,
         out_shape=shape((SIDE, 2 * NS, GROUP_COLS), BF16),
@@ -468,8 +504,12 @@
     )(place, received, other_total)
     entered = between(entering)
 
-    from_above, from_below, _ = lax.optimization_barrier((from_above, from_below, entering))
-    other = from_above + jnp.pad(from_below, ((2 * TOK, 0), (0, 0)))
+    above, other_pair, _ = lax.optimization_barrier((above, other_pair, entering))
+    rows_above, cots_above, ends = above
+    none = jnp.zeros_like(ends)
+    rows_above = rows_above + jnp.where(at_start, none, ends)
+    cots_above = cots_above + jnp.where(at_start, ends, none)
+    other = jnp.concatenate([rows_above, cots_above, other_pair])
     halves = jnp.stack([own, other])
     shards = [halves] + [round_side(halves, step) for step in range(1, SIDE)]
 
@@ -481,7 +521,7 @@
             shape((1, TOK, COLS), BF16),
             shape((1, SSM_DEV, TOK), F32),
             shape((peers, 2, TOK // peers, NS), BF16),
-            shape((everyone, TOK), F32),
+            shape((everyone, 2, TOK), F32),
         ),
         in_specs=whole(9),
         out_specs=tuple(whole(4)),
@@ -511,9 +551,10 @@
         cost_estimate=pl.CostEstimate(flops=2 << 30, bytes_accessed=4 << 20, transcendentals=1 << 20),
     )(place, *shards)
 
-    everywhere, shares, query_grad = lax.optimization_barrier((everywhere, shares, query_grad))
+    shares, query_grad = lax.optimization_barrier((shares, query_grad))
     shared_grad = jnp.sum(shares.astype(F32), axis=0)[None]
-    param_grads = jnp.sum(everywhere, axis=0)[: 2 * SSM_DEV].reshape(2, SSM_DEV)
+    everywhere, shared_grad = lax.optimization_barrier((everywhere, shared_grad))
+    param_grads = jnp.sum(everywhere, axis=0)[:, :SSM_DEV]
     return (query_grad, keyval_grad, input_grad, shared_grad, step_grad, param_grads)
 
 

time: 106 us -> 104 us (0.981)
  waiting for transfers between devices: 13 us -> 10.8 us
    ppermute x1, starting transfers between devices: 7.41 us -> 17.3 us  [body(): other_total = lax.ppermute(total, 'ctx', across)]
    ppermute x1, waiting for transfers between devices: 8.29 us -> 0.01 us  [body(): other_total = lax.ppermute(total, 'ctx', across)]
    ppermute x2 -> x6, starting transfers between devices: 16.7 us -> 10.5 us  [the longest x1 3.99 us: body(): cots_above = lax.ppermute(near_cots, ('dp', 'ctx'), leg(1, 1))]
    ppermute x2 -> x6, waiting for transfers between devices: 0.01 us -> 4.49 us  [the longest x1 4.47 us: body(): lax.ppermute(jnp.where(at_start, own_cots, own_rows), ('dp', 'ctx'), stra...]
    all_to_all x2, starting transfers between devices: 10.7 us -> 8.45 us  [between(): lax.all_to_all(value, 'ctx', 0, 0, axis_index_groups=sides, tiled=True)]
    all_to_all x2, waiting for transfers between devices: 0.01 us -> 1.85 us  [between(): lax.all_to_all(value, 'ctx', 0, 0, axis_index_groups=sides, tiled=True)]
  transfers between devices with their start and end apart: 9 -> 13, of which waited for: 2 -> 3; matrix products, arithmetic and copies ran while one was open for 0% -> 1% of each run, Pallas kernels for 14% -> 16%
where the time goes in v3:
time: 104 us
  starting transfers between devices  59.3 us (57%)
  Pallas kernels  19.8 us (19%)
  blocking collectives  11.1 us (11%)
  waiting for transfers between devices  10.8 us (10%)
  other arithmetic  1.41 us (1%)
  between operations  1.04 us (1%)
    ppermute x1, starting transfers between devices, body(): other_total = lax.ppermute(total, 'ctx', across)  17.3 us
    all_to_all x1, starting transfers between devices, body(): everywhere = lax.all_to_all(both, ('dp', 'ctx'), 0, 0, tiled=True)  13.8 us
    all_to_all x1, blocking collectives, body(): shares = lax.all_to_all(share, 'head', 0, 0, tiled=True)  11.1 us
    ppermute x3, starting transfers between devices, round_side(): return lax.ppermute(value, 'ctx', turn)  9.28 us
    all_to_all x2, starting transfers between devices, between(): lax.all_to_all(value, 'ctx', 0, 0, axis_index_groups=sides, tiled=True)  8.45 us
    pallas_call x1, Pallas kernels, body(): pl.pallas_call(attention, out_shape=(shape((1, TOK, 2 * WIDTH), BF16), sh...  8.31 us
    ppermute x1, waiting for transfers between devices, body(): lax.ppermute(jnp.where(at_start, own_cots, own_rows), ('dp', 'ctx'), stra...  4.47 us
    all_to_all x1, waiting for transfers between devices, body(): everywhere = lax.all_to_all(both, ('dp', 'ctx'), 0, 0, tiled=True)  4.43 us
  transfers between devices with their start and end apart: 13, of which 3 were waited for; matrix products, arithmetic and copies ran while one was open for 1% of the time, Pallas kernels for 16%

profile of v3, /device:TPU:1, one launch (start us, length us, event | category | flops | bytes accessed | tf_op | source)
XLA Modules:
  0.0 103.5 jit_solution(13461211664205876724)
XLA Ops:
  0.6 3.6 %local_states.1 = (bf16[4,272,256]{2,1,0:T(8,128)(2,1)}, bf16[128,1024]{1,0:T(8,128)(2,1)}, bf16[128,1024]{1,0:T(8,128)(2,1)}) custom-call(bf16[1,128,1024]{2,1,0:T(8,128)(2,1)} %x_ref.3, bf16[1,128,1024]{2,1,0:T(8,128)(2,1)} %dy_ref.3, bf16[1,2,128,128]{3,2,1,0:T(8,128)(2,1)} %bc_ref.3, f32[1,16,128]{2,1,0:T(8,128)} %step_ref, s32[1,128]{1,0:T(1,128)} %docs_ref.2, ...), custom_call_target="tpu_custom_call" | custom-call | tf_op jit(solution)/shard_map/local_states/pallas_call | solution.py:422
  4.2 0.0 copy-start.5
  4.2 0.0 copy-start.6
  4.2 0.0 copy-start.7
  4.2 0.0 copy-start.9
  4.3 0.0 copy-start
  4.3 0.0 copy-start.1
  4.3 5.0 %all-to-all-start = ((bf16[4,272,256]{2,1,0:T(8,128)(2,1)}), bf16[4,272,256]{2,1,0:T(8,128)(2,1)S(1)}, u32[]{:S(2)}, u32[]{:S(2)}) async-start(bf16[4,272,256]{2,1,0:T(8,128)(2,1)} %get-tuple-element.42), calls=%async_computation | async-start | bytes 1114112 | tf_op jit(solution)/shard_map/all_to_all | solution.py:420
  9.3 0.0 copy-done.5
  9.3 0.0 copy-done.6
  9.3 0.0 copy-done.7
  9.3 0.0 copy-done.9
  9.3 0.0 copy-start.2
  9.3 0.0 copy-start.8
  9.4 0.7 collective-permute-start.1
  10.0 0.0 copy-start.10
  10.0 0.0 copy-start.11
  10.0 1.3 %collective-permute-start.3 = (bf16[128,256]{1,0:T(8,128)(2,1)S(1)}, bf16[128,256]{1,0:T(8,128)(2,1)S(1)}, u32[]{:S(2)}, u32[]{:S(2)}) collective-permute-start(bf16[128,256]{1,0:T(8,128)(2,1)S(1)} %get-tuple-element.50), channel_id=1, source_target_pairs={{96,0},{104,8},{112,16},{120,24},{160,64},{168,72},{176,80},{184,8... | collective-permute-start | bytes 196616 | tf_op jit(solution)/shard_map/ppermute | solution.py:460
  11.3 0.0 copy-done
  11.4 0.0 copy-done.1
  11.4 0.0 copy-done.2
  11.4 0.0 copy-done.8
  11.4 0.0 copy-done.10
  11.4 0.0 copy-done.11
  11.4 3.0 %inside_shard.1 = (f32[128,1024]{1,0:T(8,128)S(1)}, f32[2,128,128]{2,1,0:T(8,128)S(1)}, f32[7,16,128]{2,1,0:T(8,128)S(1)}) custom-call(bf16[1,128,1024]{2,1,0:T(8,128)(2,1)S(1)} %copy-done, bf16[1,128,1024]{2,1,0:T(8,128)(2,1)S(1)} %copy-done.1, bf16[1,2,128,128]{3,2,1,0:T(8,128)(2,1)S(1)} %copy-done.2, f32[1,16,128]{2,1,0:T(8,128)S(1)} %copy-done.8, ...), custom_call_target="tpu_custom_call" | custom-call | flops 1024 | bytes 1024 | tf_op jit(solution)/shard_map/inside_shard/pallas_call | solution.py:463
  14.5 0.1 pad_add_fusion.half_ref.place_ref
  14.5 1.8 %all-to-all-done.ref = bf16[4,272,256]{2,1,0:T(8,128)(2,1)S(1)} async-done(((bf16[4,272,256]{2,1,0:T(8,128)(2,1)}), bf16[4,272,256]{2,1,0:T(8,128)(2,1)S(1)}, u32[]{:S(2)}, u32[]{:S(2)}) %all-to-all-start) | async-done | bytes 557088 | tf_op jit(solution)/shard_map/all_to_all | solution.py:420
  16.4 0.8 half_totals.1
  17.2 17.3 %collective-permute-start = (bf16[144,256]{1,0:T(8,128)(2,1)S(1)}, bf16[144,256]{1,0:T(8,128)(2,1)S(1)}, u32[]{:S(2)}, u32[]{:S(2)}) collective-permute-start(bf16[144,256]{1,0:T(8,128)(2,1)S(1)} %half_totals.1), channel_id=1, source_target_pairs={{0,32},{8,40},{16,48},{24,56},{32,0},{40,8},{48,16},{56,24},{1,33}... | collective-permute-start | bytes 221192 | tf_op jit(solution)/shard_map/ppermute | solution.py:486
  34.5 1.9 %collective-permute-start.6 = (bf16[144,256]{1,0:T(8,128)(2,1)S(1)}, bf16[144,256]{1,0:T(8,128)(2,1)S(1)}, u32[]{:S(2)}, u32[]{:S(2)}) collective-permute-start(bf16[144,256]{1,0:T(8,128)(2,1)S(1)} %get-tuple-element.52), channel_id=1, source_target_pairs={{0,32},{8,40},{16,48},{24,56},{32,0},{40,8},{48,16},{56,24},{1,33}... | collective-permute-start | bytes 221192 | tf_op jit(solution)/shard_map/ppermute | solution.py:488
  36.4 1.3 %collective-permute-start.5 = (bf16[128,256]{1,0:T(8,128)(2,1)S(1)}, bf16[128,256]{1,0:T(8,128)(2,1)S(1)}, u32[]{:S(2)}, u32[]{:S(2)}) collective-permute-start(bf16[128,256]{1,0:T(8,128)(2,1)S(1)} %broadcast_select_fusion), channel_id=1, source_target_pairs={{32,0},{40,8},{48,16},{56,24},{480,448},{488,456},{496,464},{504,4... | collective-permute-start | bytes 196616 | tf_op jit(solution)/shard_map/ppermute | solution.py:458
  37.7 0.0 collective-permute-done.1
  37.7 1.3 %collective-permute-start.2 = (bf16[128,256]{1,0:T(8,128)(2,1)S(1)}, bf16[128,256]{1,0:T(8,128)(2,1)S(1)}, u32[]{:S(2)}, u32[]{:S(2)}) collective-permute-start(bf16[128,256]{1,0:T(8,128)(2,1)S(1)} %collective-permute-done.1), channel_id=1, source_target_pairs={{64,0},{72,8},{80,16},{88,24},{128,64},{136,72},{144,80},{152,88},... | collective-permute-start | bytes 196616 | tf_op jit(solution)/shard_map/ppermute | solution.py:494
  39.0 0.0 collective-permute-done.3
  39.0 4.0 %collective-permute-start.4 = (bf16[128,256]{1,0:T(8,128)(2,1)S(1)}, bf16[128,256]{1,0:T(8,128)(2,1)S(1)}, u32[]{:S(2)}, u32[]{:S(2)}) collective-permute-start(bf16[128,256]{1,0:T(8,128)(2,1)S(1)} %collective-permute-done.3), channel_id=1, source_target_pairs={{0,64},{8,72},{16,80},{24,88},{64,128},{72,136},{80,144},{88,152},... | collective-permute-start | bytes 196616 | tf_op jit(solution)/shard_map/ppermute | solution.py:495
  43.0 0.0 collective-permute-done.other_ref
  43.1 1.6 %entering_states.1 = bf16[4,256,256]{2,1,0:T(8,128)(2,1)} custom-call(s32[2]{0:T(128)S(1)} %pad_add_fusion.half_ref.place_ref, bf16[4,272,256]{2,1,0:T(8,128)(2,1)S(1)} %all-to-all-done.ref, bf16[144,256]{1,0:T(8,128)(2,1)S(1)} %collective-permute-done.other_ref), custom_call_target="tpu_custom_call" | custom-call | tf_op jit(solution)/shard_map/entering_states/pallas_call | solution.py:497
  44.7 3.5 %all-to-all-start.1 = ((bf16[4,256,256]{2,1,0:T(8,128)(2,1)}), bf16[4,256,256]{2,1,0:T(8,128)(2,1)S(1)}, u32[]{:S(2)}, u32[]{:S(2)}) async-start(bf16[4,256,256]{2,1,0:T(8,128)(2,1)} %entering_states.1), calls=%async_computation.1 | async-start | bytes 1048576 | tf_op jit(solution)/shard_map/all_to_all | solution.py:420
  48.2 4.5 %collective-permute-done.5 = bf16[128,256]{1,0:T(8,128)(2,1)S(1)} collective-permute-done((bf16[128,256]{1,0:T(8,128)(2,1)S(1)}, bf16[128,256]{1,0:T(8,128)(2,1)S(1)}, u32[]{:S(2)}, u32[]{:S(2)}) %collective-permute-start.5) | collective-permute-done | bytes 65568 | tf_op jit(solution)/shard_map/ppermute | solution.py:458
  52.7 0.0 collective-permute-done.2
  52.7 0.0 collective-permute-done.4
  52.7 0.0 collective-permute-done.6
  52.7 0.0 copy-start.3
  52.7 0.0 copy-start.4
  52.8 4.2 %collective-permute-start.9 = (bf16[2,400,256]{2,1,0:T(8,128)(2,1)S(1)}, bf16[2,400,256]{2,1,0:T(8,128)(2,1)S(1)}, u32[]{:S(2)}, u32[]{:S(2)}) collective-permute-start(bf16[2,400,256]{2,1,0:T(8,128)(2,1)S(1)} %pad_maximum_fusion.refs_0_), channel_id=1, source_target_pairs={{0,24},{8,0},{16,8},{24,16},{32,56},{40,32},{48,40},{56,48},{1,25}... | collective-permute-start | bytes 1228808 | tf_op jit(solution)/shard_map/ppermute | solution.py:492
  57.0 2.3 %collective-permute-start.8 = (bf16[2,400,256]{2,1,0:T(8,128)(2,1)S(1)}, bf16[2,400,256]{2,1,0:T(8,128)(2,1)}, u32[]{:S(2)}, u32[]{:S(2)}) collective-permute-start(bf16[2,400,256]{2,1,0:T(8,128)(2,1)S(1)} %pad_maximum_fusion.refs_0_), channel_id=1, source_target_pairs={{0,16},{8,24},{16,0},{24,8},{32,48},{40,56},{48,32},{56,40},{1,17}... | collective-permute-start | bytes 1228808 | tf_op jit(solution)/shard_map/ppermute | solution.py:492
  59.3 2.8 %collective-permute-start.7 = (bf16[2,400,256]{2,1,0:T(8,128)(2,1)S(1)}, bf16[2,400,256]{2,1,0:T(8,128)(2,1)}, u32[]{:S(2)}, u32[]{:S(2)}) collective-permute-start(bf16[2,400,256]{2,1,0:T(8,128)(2,1)S(1)} %pad_maximum_fusion.refs_0_), channel_id=1, source_target_pairs={{0,8},{8,16},{16,24},{24,0},{32,40},{40,48},{48,56},{56,32},{1,9},... | collective-permute-start | bytes 1228808 | tf_op jit(solution)/shard_map/ppermute | solution.py:492
  62.1 0.0 all-to-all-done.1.in_ref
  62.1 0.0 copy-done.3
  62.1 0.0 copy-done.4
  62.1 2.4 %finish_ssm.1 = (bf16[1,128,1024]{2,1,0:T(8,128)(2,1)}, f32[1,16,128]{2,1,0:T(8,128)}, bf16[8,2,16,128]{3,2,1,0:T(8,128)(2,1)S(1)}, f32[64,2,128]{2,1,0:T(2,128)}) custom-call(bf16[4,256,256]{2,1,0:T(8,128)(2,1)S(1)} %all-to-all-done.1.in_ref, bf16[1,128,1024]{2,1,0:T(8,128)(2,1)S(1)} %copy-done, bf16[1,128,1024]{2,1,0:T(8,128)(2,1)S(1)} %copy-done.1, ...), custom_call_target="tpu_custom_call" | custom-call | tf_op jit(solution)/shard_map/finish_ssm/pallas_call | solution.py:518
  64.5 11.1 %all_to_all.20 = bf16[8,2,16,128]{3,2,1,0:T(8,128)(2,1)S(1)} all-to-all(bf16[8,2,16,128]{3,2,1,0:T(8,128)(2,1)S(1)} %get-tuple-element.63), channel_id=1, replica_groups=mesh['dp'=8,'ctx'=8,'head'=8] {'head'}, dimensions={0} | all-to-all | bytes 131072 | tf_op jit(solution)/shard_map/all_to_all | solution.py:531
  75.6 13.8 %all-to-all-start.3 = ((f32[64,2,128]{2,1,0:T(2,128)}), f32[64,2,128]{2,1,0:T(2,128)S(1)}, u32[]{:S(2)}, u32[]{:S(2)}) async-start(f32[64,2,128]{2,1,0:T(2,128)} %get-tuple-element.65), calls=%async_computation.3 | async-start | bytes 131072 | tf_op jit(solution)/shard_map/all_to_all | solution.py:533
  89.5 0.0 collective-permute-done.9.refs_3_
  89.5 0.0 collective-permute-done.8.refs_2_
  89.5 0.0 collective-permute-done.7.refs_1_
  89.5 8.3 %attention.1 = (bf16[1,128,256]{2,1,0:T(8,128)(2,1)}, bf16[1,2,128,128]{3,2,1,0:T(8,128)(2,1)}) custom-call(s32[2]{0:T(128)S(1)} %pad_add_fusion.half_ref.place_ref, bf16[2,400,256]{2,1,0:T(8,128)(2,1)S(1)} %pad_maximum_fusion.refs_0_, bf16[2,400,256]{2,1,0:T(8,128)(2,1)} %collective-permute-done.7.refs_1_, ...), custom_call_target="tpu_custom_call" | custom-call | flops 2147483648 | bytes 4194304 | tf_op jit(solution)/shard_map/attention/pallas_call | solution.py:536
  97.8 0.6 convert_reduce_fusion
  98.4 4.4 %all-to-all-done.3 = f32[64,2,128]{2,1,0:T(2,128)S(1)} async-done(((f32[64,2,128]{2,1,0:T(2,128)}), f32[64,2,128]{2,1,0:T(2,128)S(1)}, u32[]{:S(2)}, u32[]{:S(2)}) %all-to-all-start.3) | async-done | bytes 65568 | tf_op jit(solution)/shard_map/all_to_all | solution.py:533
  102.9 0.6 reduce_sum.19
  (5 shorter events, 0.1 us)
Async XLA Ops:
  4.2 5.1 %copy-start.5 = (bf16[1,128,256]{2,1,0:T(8,128)(2,1)S(1)}, bf16[1,128,256]{2,1,0:T(8,128)(2,1)}, u32[]{:S(2)}) copy-start(bf16[1,128,256]{2,1,0:T(8,128)(2,1)} %queries_ref.1) | copy-start | bytes 196612
  4.2 5.1 %copy-start.6 = (bf16[1,128,256]{2,1,0:T(8,128)(2,1)S(1)}, bf16[1,128,256]{2,1,0:T(8,128)(2,1)}, u32[]{:S(2)}) copy-start(bf16[1,128,256]{2,1,0:T(8,128)(2,1)} %grads_ref.1) | copy-start | bytes 196612
  4.2 5.0 %copy-start.7 = (bf16[1,2,128,128]{3,2,1,0:T(8,128)(2,1)S(1)}, bf16[1,2,128,128]{3,2,1,0:T(8,128)(2,1)}, u32[]{:S(2)}) copy-start(bf16[1,2,128,128]{3,2,1,0:T(8,128)(2,1)} %keyval_ref.1) | copy-start | bytes 196612
  4.2 5.0 %copy-start.9 = (s32[1,128]{1,0:T(1,128)S(1)}, s32[1,128]{1,0:T(1,128)}, u32[]{:S(2)}) copy-start(s32[1,128]{1,0:T(1,128)} %docs_ref.2) | copy-start | bytes 1540
  4.3 7.1 %copy-start = (bf16[1,128,1024]{2,1,0:T(8,128)(2,1)S(1)}, bf16[1,128,1024]{2,1,0:T(8,128)(2,1)}, u32[]{:S(2)}) copy-start(bf16[1,128,1024]{2,1,0:T(8,128)(2,1)} %x_ref.3) | copy-start | bytes 786436
  4.3 7.1 %copy-start.1 = (bf16[1,128,1024]{2,1,0:T(8,128)(2,1)S(1)}, bf16[1,128,1024]{2,1,0:T(8,128)(2,1)}, u32[]{:S(2)}) copy-start(bf16[1,128,1024]{2,1,0:T(8,128)(2,1)} %dy_ref.3) | copy-start | bytes 786436
  4.3 12.1 %all-to-all-start = ((bf16[4,272,256]{2,1,0:T(8,128)(2,1)}), bf16[4,272,256]{2,1,0:T(8,128)(2,1)S(1)}, u32[]{:S(2)}, u32[]{:S(2)}) async-start(bf16[4,272,256]{2,1,0:T(8,128)(2,1)} %get-tuple-element.42), calls=%async_computation | async-start | bytes 1114112 | tf_op jit(solution)/shard_map/all_to_all | solution.py:420
  9.3 2.1 %copy-start.2 = (bf16[1,2,128,128]{3,2,1,0:T(8,128)(2,1)S(1)}, bf16[1,2,128,128]{3,2,1,0:T(8,128)(2,1)}, u32[]{:S(2)}) copy-start(bf16[1,2,128,128]{3,2,1,0:T(8,128)(2,1)} %bc_ref.3) | copy-start | bytes 196612
  9.3 2.1 %copy-start.8 = (f32[1,16,128]{2,1,0:T(8,128)S(1)}, f32[1,16,128]{2,1,0:T(8,128)}, u32[]{:S(2)}) copy-start(f32[1,16,128]{2,1,0:T(8,128)} %step_ref) | copy-start | bytes 24580
  9.4 28.4 %collective-permute-start.1 = (bf16[128,256]{1,0:T(8,128)(2,1)S(1)}, bf16[128,256]{1,0:T(8,128)(2,1)S(1)}, u32[]{:S(2)}, u32[]{:S(2)}) collective-permute-start(bf16[128,256]{1,0:T(8,128)(2,1)S(1)} %get-tuple-element.49), channel_id=1, source_target_pairs={{32,64},{40,72},{48,80},{56,88},{96,128},{104,136},{112,144},{120,... | collective-permute-start | bytes 196616 | tf_op jit(solution)/shard_map/ppermute | solution.py:459
  10.0 1.4 %copy-start.10 = (f32[16]{0:T(128)S(1)}, f32[16]{0:T(128)}, u32[]{:S(2)}) copy-start(f32[16]{0:T(128)} %rate_ref.3) | copy-start | bytes 196
  10.0 1.4 %copy-start.11 = (f32[16]{0:T(128)S(1)}, f32[16]{0:T(128)}, u32[]{:S(2)}) copy-start(f32[16]{0:T(128)} %skip_ref.1) | copy-start | bytes 196
  10.0 29.0 %collective-permute-start.3 = (bf16[128,256]{1,0:T(8,128)(2,1)S(1)}, bf16[128,256]{1,0:T(8,128)(2,1)S(1)}, u32[]{:S(2)}, u32[]{:S(2)}) collective-permute-start(bf16[128,256]{1,0:T(8,128)(2,1)S(1)} %get-tuple-element.50), channel_id=1, source_target_pairs={{96,0},{104,8},{112,16},{120,24},{160,64},{168,72},{176,80},{184,8... | collective-permute-start | bytes 196616 | tf_op jit(solution)/shard_map/ppermute | solution.py:460
  17.2 25.8 %collective-permute-start = (bf16[144,256]{1,0:T(8,128)(2,1)S(1)}, bf16[144,256]{1,0:T(8,128)(2,1)S(1)}, u32[]{:S(2)}, u32[]{:S(2)}) collective-permute-start(bf16[144,256]{1,0:T(8,128)(2,1)S(1)} %half_totals.1), channel_id=1, source_target_pairs={{0,32},{8,40},{16,48},{24,56},{32,0},{40,8},{48,16},{56,24},{1,33}... | collective-permute-start | bytes 221192 | tf_op jit(solution)/shard_map/ppermute | solution.py:486
  34.5 18.2 %collective-permute-start.6 = (bf16[144,256]{1,0:T(8,128)(2,1)S(1)}, bf16[144,256]{1,0:T(8,128)(2,1)S(1)}, u32[]{:S(2)}, u32[]{:S(2)}) collective-permute-start(bf16[144,256]{1,0:T(8,128)(2,1)S(1)} %get-tuple-element.52), channel_id=1, source_target_pairs={{0,32},{8,40},{16,48},{24,56},{32,0},{40,8},{48,16},{56,24},{1,33}... | collective-permute-start | bytes 221192 | tf_op jit(solution)/shard_map/ppermute | solution.py:488
  36.4 16.2 %collective-permute-start.5 = (bf16[128,256]{1,0:T(8,128)(2,1)S(1)}, bf16[128,256]{1,0:T(8,128)(2,1)S(1)}, u32[]{:S(2)}, u32[]{:S(2)}) collective-permute-start(bf16[128,256]{1,0:T(8,128)(2,1)S(1)} %broadcast_select_fusion), channel_id=1, source_target_pairs={{32,0},{40,8},{48,16},{56,24},{480,448},{488,456},{496,464},{504,4... | collective-permute-start | bytes 196616 | tf_op jit(solution)/shard_map/ppermute | solution.py:458
  37.7 14.9 %collective-permute-start.2 = (bf16[128,256]{1,0:T(8,128)(2,1)S(1)}, bf16[128,256]{1,0:T(8,128)(2,1)S(1)}, u32[]{:S(2)}, u32[]{:S(2)}) collective-permute-start(bf16[128,256]{1,0:T(8,128)(2,1)S(1)} %collective-permute-done.1), channel_id=1, source_target_pairs={{64,0},{72,8},{80,16},{88,24},{128,64},{136,72},{144,80},{152,88},... | collective-permute-start | bytes 196616 | tf_op jit(solution)/shard_map/ppermute | solution.py:494
  39.0 13.6 %collective-permute-start.4 = (bf16[128,256]{1,0:T(8,128)(2,1)S(1)}, bf16[128,256]{1,0:T(8,128)(2,1)S(1)}, u32[]{:S(2)}, u32[]{:S(2)}) collective-permute-start(bf16[128,256]{1,0:T(8,128)(2,1)S(1)} %collective-permute-done.3), channel_id=1, source_target_pairs={{0,64},{8,72},{16,80},{24,88},{64,128},{72,136},{80,144},{88,152},... | collective-permute-start | bytes 196616 | tf_op jit(solution)/shard_map/ppermute | solution.py:495
  44.7 17.4 %all-to-all-start.1 = ((bf16[4,256,256]{2,1,0:T(8,128)(2,1)}), bf16[4,256,256]{2,1,0:T(8,128)(2,1)S(1)}, u32[]{:S(2)}, u32[]{:S(2)}) async-start(bf16[4,256,256]{2,1,0:T(8,128)(2,1)} %entering_states.1), calls=%async_computation.1 | async-start | bytes 1048576 | tf_op jit(solution)/shard_map/all_to_all | solution.py:420
  52.7 9.4 %copy-start.3 = (bf16[128,1024]{1,0:T(8,128)(2,1)S(1)}, bf16[128,1024]{1,0:T(8,128)(2,1)}, u32[]{:S(2)}) copy-start(bf16[128,1024]{1,0:T(8,128)(2,1)} %get-tuple-element.60.sin_ref) | copy-start | bytes 786436
  52.7 9.4 %copy-start.4 = (bf16[128,1024]{1,0:T(8,128)(2,1)S(1)}, bf16[128,1024]{1,0:T(8,128)(2,1)}, u32[]{:S(2)}) copy-start(bf16[128,1024]{1,0:T(8,128)(2,1)} %get-tuple-element.61.sgr_ref) | copy-start | bytes 786436
  52.8 36.7 %collective-permute-start.9 = (bf16[2,400,256]{2,1,0:T(8,128)(2,1)S(1)}, bf16[2,400,256]{2,1,0:T(8,128)(2,1)S(1)}, u32[]{:S(2)}, u32[]{:S(2)}) collective-permute-start(bf16[2,400,256]{2,1,0:T(8,128)(2,1)S(1)} %pad_maximum_fusion.refs_0_), channel_id=1, source_target_pairs={{0,24},{8,0},{16,8},{24,16},{32,56},{40,32},{48,40},{56,48},{1,25}... | collective-permute-start | bytes 1228808 | tf_op jit(solution)/shard_map/ppermute | solution.py:492
  57.0 32.5 %collective-permute-start.8 = (bf16[2,400,256]{2,1,0:T(8,128)(2,1)S(1)}, bf16[2,400,256]{2,1,0:T(8,128)(2,1)}, u32[]{:S(2)}, u32[]{:S(2)}) collective-permute-start(bf16[2,400,256]{2,1,0:T(8,128)(2,1)S(1)} %pad_maximum_fusion.refs_0_), channel_id=1, source_target_pairs={{0,16},{8,24},{16,0},{24,8},{32,48},{40,56},{48,32},{56,40},{1,17}... | collective-permute-start | bytes 1228808 | tf_op jit(solution)/shard_map/ppermute | solution.py:492
  59.3 30.2 %collective-permute-start.7 = (bf16[2,400,256]{2,1,0:T(8,128)(2,1)S(1)}, bf16[2,400,256]{2,1,0:T(8,128)(2,1)}, u32[]{:S(2)}, u32[]{:S(2)}) collective-permute-start(bf16[2,400,256]{2,1,0:T(8,128)(2,1)S(1)} %pad_maximum_fusion.refs_0_), channel_id=1, source_target_pairs={{0,8},{8,16},{16,24},{24,0},{32,40},{40,48},{48,56},{56,32},{1,9},... | collective-permute-start | bytes 1228808 | tf_op jit(solution)/shard_map/ppermute | solution.py:492
  75.6 27.2 %all-to-all-start.3 = ((f32[64,2,128]{2,1,0:T(2,128)}), f32[64,2,128]{2,1,0:T(2,128)S(1)}, u32[]{:S(2)}, u32[]{:S(2)}) async-start(f32[64,2,128]{2,1,0:T(2,128)} %get-tuple-element.65), calls=%async_computation.3 | async-start | bytes 131072 | tf_op jit(solution)/shard_map/all_to_all | solution.py:533

commit v4 on v3

--- a/solution.py
+++ b/solution.py
@@ -356,12 +356,11 @@
                 total_scr[1] += value_part
 
     shard(mine, True)
-    lax.fori_loop(
-        mine + 1,
-        jnp.minimum(mine + SIDE, 2 * SIDE - 1) + 1,
-        lambda r, _: (shard(r, False), 0)[1],
-        0,
-    )
+    last_doc = jnp.max(own_docs, axis=1, keepdims=True)
+    places = iota((1, 2 * SIDE * TOK), 1).astype(F32)
+    last_place = jnp.max(jnp.where(doc_scr[:1] == last_doc, places, 0.0)).astype(jnp.int32)
+    stop = jnp.minimum(jnp.minimum(last_place // TOK, mine + SIDE), 2 * SIDE - 1) + 1
+    lax.fori_loop(mine + 1, stop, lambda r, _: (shard(r, False), 0)[1], 0)
     dkv_ref[0] = total_scr[...].astype(BF16)
 
 
@@ -530,7 +529,12 @@
     )(entered, ssm_in, ssm_grad, bc_pair, near, shared_near, aux, scaled_in, scaled_grad)
     shares = lax.all_to_all(share, "head", 0, 0, tiled=True)
     both, shares = lax.optimization_barrier((both, shares))
-    everywhere = lax.all_to_all(both, ("dp", "ctx"), 0, 0, tiled=True)
+    order = [
+        at_place((k + half_ring) % (2 * half_ring), x) for k in range(2 * half_ring) for x in range(SIDE)
+    ]
+    everywhere = lax.all_to_all(
+        both, ("dp", "ctx"), 0, 0, axis_index_groups=[order], tiled=True
+    )
 
     shards, _ = lax.optimization_barrier((shards, both))
     query_grad, keyval_grad = pl.pallas_call(

time: 104 us -> 102 us (0.981)
  waiting for transfers between devices: 10.8 us -> 6.35 us
  starting transfers between devices: 59.3 us -> 62 us
    all_to_all x1, waiting for transfers between devices: 4.43 us -> 0.01 us  [body(): lax.all_to_all(both, ('dp', 'ctx'), 0, 0, axis_index_groups=[order], tile...]
    all_to_all x1, starting transfers between devices: 13.8 us -> 16.5 us  [body(): lax.all_to_all(both, ('dp', 'ctx'), 0, 0, axis_index_groups=[order], tile...]
  transfers between devices with their start and end apart: 13 -> 13, of which waited for: 3 -> 2; matrix products, arithmetic and copies ran while one was open for 1% -> 1% of each run, Pallas kernels for 16% -> 16%
where the time goes in v4:
time: 102 us
  starting transfers between devices  62 us (61%)
  Pallas kernels  19.9 us (20%)
  blocking collectives  11.1 us (11%)
  waiting for transfers between devices  6.35 us (6%)
  other arithmetic  1.42 us (1%)
  between operations  1.04 us (1%)
    ppermute x1, starting transfers between devices, body(): other_total = lax.ppermute(total, 'ctx', across)  17.3 us
    all_to_all x1, starting transfers between devices, body(): lax.all_to_all(both, ('dp', 'ctx'), 0, 0, axis_index_groups=[order], tile...  16.5 us
    all_to_all x1, blocking collectives, body(): shares = lax.all_to_all(share, 'head', 0, 0, tiled=True)  11.1 us
    ppermute x3, starting transfers between devices, round_side(): return lax.ppermute(value, 'ctx', turn)  9.28 us
    all_to_all x2, starting transfers between devices, between(): lax.all_to_all(value, 'ctx', 0, 0, axis_index_groups=sides, tiled=True)  8.45 us
    pallas_call x1, Pallas kernels, body(): pl.pallas_call(attention, out_shape=(shape((1, TOK, 2 * WIDTH), BF16), sh...  8.36 us
    ppermute x1, waiting for transfers between devices, body(): lax.ppermute(jnp.where(at_start, own_cots, own_rows), ('dp', 'ctx'), stra...  4.47 us
    ppermute x1, starting transfers between devices, body(): cots_above = lax.ppermute(near_cots, ('dp', 'ctx'), leg(1, 1))  3.99 us
  transfers between devices with their start and end apart: 13, of which 2 were waited for; matrix products, arithmetic and copies ran while one was open for 1% of the time, Pallas kernels for 16%

profile of v4, /device:TPU:1, one launch (start us, length us, event | category | flops | bytes accessed | tf_op | source)
XLA Modules:
  0.0 101.8 jit_solution(1473359059874643429)
XLA Ops:
  0.6 3.6 %local_states.1 = (bf16[4,272,256]{2,1,0:T(8,128)(2,1)}, bf16[128,1024]{1,0:T(8,128)(2,1)}, bf16[128,1024]{1,0:T(8,128)(2,1)}) custom-call(bf16[1,128,1024]{2,1,0:T(8,128)(2,1)} %x_ref.3, bf16[1,128,1024]{2,1,0:T(8,128)(2,1)} %dy_ref.3, bf16[1,2,128,128]{3,2,1,0:T(8,128)(2,1)} %bc_ref.3, f32[1,16,128]{2,1,0:T(8,128)} %step_ref, s32[1,128]{1,0:T(1,128)} %docs_ref.2, ...), custom_call_target="tpu_custom_call" | custom-call | tf_op jit(solution)/shard_map/local_states/pallas_call | solution.py:421
  4.2 0.0 copy-start.5
  4.2 0.0 copy-start.6
  4.2 0.0 copy-start.7
  4.2 0.0 copy-start.9
  4.3 0.0 copy-start
  4.3 0.0 copy-start.1
  4.3 5.0 %all-to-all-start = ((bf16[4,272,256]{2,1,0:T(8,128)(2,1)}), bf16[4,272,256]{2,1,0:T(8,128)(2,1)S(1)}, u32[]{:S(2)}, u32[]{:S(2)}) async-start(bf16[4,272,256]{2,1,0:T(8,128)(2,1)} %get-tuple-element.42), calls=%async_computation | async-start | bytes 1114112 | tf_op jit(solution)/shard_map/all_to_all | solution.py:419
  9.3 0.0 copy-done.5
  9.3 0.0 copy-done.6
  9.3 0.0 copy-done.7
  9.3 0.0 copy-done.9
  9.3 0.0 copy-start.2
  9.3 0.0 copy-start.8
  9.4 0.7 collective-permute-start.1
  10.0 0.0 copy-start.10
  10.0 0.0 copy-start.11
  10.0 1.3 %collective-permute-start.3 = (bf16[128,256]{1,0:T(8,128)(2,1)S(1)}, bf16[128,256]{1,0:T(8,128)(2,1)S(1)}, u32[]{:S(2)}, u32[]{:S(2)}) collective-permute-start(bf16[128,256]{1,0:T(8,128)(2,1)S(1)} %get-tuple-element.50), channel_id=1, source_target_pairs={{96,0},{104,8},{112,16},{120,24},{160,64},{168,72},{176,80},{184,8... | collective-permute-start | bytes 196616 | tf_op jit(solution)/shard_map/ppermute | solution.py:459
  11.3 0.0 copy-done
  11.4 0.0 copy-done.1
  11.4 0.0 copy-done.2
  11.4 0.0 copy-done.8
  11.4 0.0 copy-done.10
  11.4 0.0 copy-done.11
  11.4 3.0 %inside_shard.1 = (f32[128,1024]{1,0:T(8,128)S(1)}, f32[2,128,128]{2,1,0:T(8,128)S(1)}, f32[7,16,128]{2,1,0:T(8,128)S(1)}) custom-call(bf16[1,128,1024]{2,1,0:T(8,128)(2,1)S(1)} %copy-done, bf16[1,128,1024]{2,1,0:T(8,128)(2,1)S(1)} %copy-done.1, bf16[1,2,128,128]{3,2,1,0:T(8,128)(2,1)S(1)} %copy-done.2, f32[1,16,128]{2,1,0:T(8,128)S(1)} %copy-done.8, ...), custom_call_target="tpu_custom_call" | custom-call | flops 1024 | bytes 1024 | tf_op jit(solution)/shard_map/inside_shard/pallas_call | solution.py:462
  14.5 0.1 pad_add_fusion.half_ref.place_ref
  14.5 1.8 %all-to-all-done.ref = bf16[4,272,256]{2,1,0:T(8,128)(2,1)S(1)} async-done(((bf16[4,272,256]{2,1,0:T(8,128)(2,1)}), bf16[4,272,256]{2,1,0:T(8,128)(2,1)S(1)}, u32[]{:S(2)}, u32[]{:S(2)}) %all-to-all-start) | async-done | bytes 557088 | tf_op jit(solution)/shard_map/all_to_all | solution.py:419
  16.4 0.8 half_totals.1
  17.2 17.3 %collective-permute-start = (bf16[144,256]{1,0:T(8,128)(2,1)S(1)}, bf16[144,256]{1,0:T(8,128)(2,1)S(1)}, u32[]{:S(2)}, u32[]{:S(2)}) collective-permute-start(bf16[144,256]{1,0:T(8,128)(2,1)S(1)} %half_totals.1), channel_id=1, source_target_pairs={{0,32},{8,40},{16,48},{24,56},{32,0},{40,8},{48,16},{56,24},{1,33}... | collective-permute-start | bytes 221192 | tf_op jit(solution)/shard_map/ppermute | solution.py:485
  34.5 1.9 %collective-permute-start.6 = (bf16[144,256]{1,0:T(8,128)(2,1)S(1)}, bf16[144,256]{1,0:T(8,128)(2,1)S(1)}, u32[]{:S(2)}, u32[]{:S(2)}) collective-permute-start(bf16[144,256]{1,0:T(8,128)(2,1)S(1)} %get-tuple-element.52), channel_id=1, source_target_pairs={{0,32},{8,40},{16,48},{24,56},{32,0},{40,8},{48,16},{56,24},{1,33}... | collective-permute-start | bytes 221192 | tf_op jit(solution)/shard_map/ppermute | solution.py:487
  36.4 1.3 %collective-permute-start.5 = (bf16[128,256]{1,0:T(8,128)(2,1)S(1)}, bf16[128,256]{1,0:T(8,128)(2,1)S(1)}, u32[]{:S(2)}, u32[]{:S(2)}) collective-permute-start(bf16[128,256]{1,0:T(8,128)(2,1)S(1)} %broadcast_select_fusion), channel_id=1, source_target_pairs={{32,0},{40,8},{48,16},{56,24},{480,448},{488,456},{496,464},{504,4... | collective-permute-start | bytes 196616 | tf_op jit(solution)/shard_map/ppermute | solution.py:457
  37.7 0.0 collective-permute-done.1
  37.7 1.3 %collective-permute-start.2 = (bf16[128,256]{1,0:T(8,128)(2,1)S(1)}, bf16[128,256]{1,0:T(8,128)(2,1)S(1)}, u32[]{:S(2)}, u32[]{:S(2)}) collective-permute-start(bf16[128,256]{1,0:T(8,128)(2,1)S(1)} %collective-permute-done.1), channel_id=1, source_target_pairs={{64,0},{72,8},{80,16},{88,24},{128,64},{136,72},{144,80},{152,88},... | collective-permute-start | bytes 196616 | tf_op jit(solution)/shard_map/ppermute | solution.py:493
  39.0 0.0 collective-permute-done.3
  39.0 4.0 %collective-permute-start.4 = (bf16[128,256]{1,0:T(8,128)(2,1)S(1)}, bf16[128,256]{1,0:T(8,128)(2,1)S(1)}, u32[]{:S(2)}, u32[]{:S(2)}) collective-permute-start(bf16[128,256]{1,0:T(8,128)(2,1)S(1)} %collective-permute-done.3), channel_id=1, source_target_pairs={{0,64},{8,72},{16,80},{24,88},{64,128},{72,136},{80,144},{88,152},... | collective-permute-start | bytes 196616 | tf_op jit(solution)/shard_map/ppermute | solution.py:494
  43.0 0.0 collective-permute-done.other_ref
  43.1 1.6 %entering_states.1 = bf16[4,256,256]{2,1,0:T(8,128)(2,1)} custom-call(s32[2]{0:T(128)S(1)} %pad_add_fusion.half_ref.place_ref, bf16[4,272,256]{2,1,0:T(8,128)(2,1)S(1)} %all-to-all-done.ref, bf16[144,256]{1,0:T(8,128)(2,1)S(1)} %collective-permute-done.other_ref), custom_call_target="tpu_custom_call" | custom-call | tf_op jit(solution)/shard_map/entering_states/pallas_call | solution.py:496
  44.7 3.5 %all-to-all-start.1 = ((bf16[4,256,256]{2,1,0:T(8,128)(2,1)}), bf16[4,256,256]{2,1,0:T(8,128)(2,1)S(1)}, u32[]{:S(2)}, u32[]{:S(2)}) async-start(bf16[4,256,256]{2,1,0:T(8,128)(2,1)} %entering_states.1), calls=%async_computation.1 | async-start | bytes 1048576 | tf_op jit(solution)/shard_map/all_to_all | solution.py:419
  48.2 4.5 %collective-permute-done.5 = bf16[128,256]{1,0:T(8,128)(2,1)S(1)} collective-permute-done((bf16[128,256]{1,0:T(8,128)(2,1)S(1)}, bf16[128,256]{1,0:T(8,128)(2,1)S(1)}, u32[]{:S(2)}, u32[]{:S(2)}) %collective-permute-start.5) | collective-permute-done | bytes 65568 | tf_op jit(solution)/shard_map/ppermute | solution.py:457
  52.7 0.0 collective-permute-done.2
  52.7 0.0 collective-permute-done.4
  52.7 0.0 collective-permute-done.6
  52.7 0.0 copy-start.3
  52.7 0.0 copy-start.4
  52.8 4.2 %collective-permute-start.9 = (bf16[2,400,256]{2,1,0:T(8,128)(2,1)S(1)}, bf16[2,400,256]{2,1,0:T(8,128)(2,1)S(1)}, u32[]{:S(2)}, u32[]{:S(2)}) collective-permute-start(bf16[2,400,256]{2,1,0:T(8,128)(2,1)S(1)} %pad_maximum_fusion.refs_0_), channel_id=1, source_target_pairs={{0,24},{8,0},{16,8},{24,16},{32,56},{40,32},{48,40},{56,48},{1,25}... | collective-permute-start | bytes 1228808 | tf_op jit(solution)/shard_map/ppermute | solution.py:491
  57.0 2.3 %collective-permute-start.8 = (bf16[2,400,256]{2,1,0:T(8,128)(2,1)S(1)}, bf16[2,400,256]{2,1,0:T(8,128)(2,1)}, u32[]{:S(2)}, u32[]{:S(2)}) collective-permute-start(bf16[2,400,256]{2,1,0:T(8,128)(2,1)S(1)} %pad_maximum_fusion.refs_0_), channel_id=1, source_target_pairs={{0,16},{8,24},{16,0},{24,8},{32,48},{40,56},{48,32},{56,40},{1,17}... | collective-permute-start | bytes 1228808 | tf_op jit(solution)/shard_map/ppermute | solution.py:491
  59.3 2.8 %collective-permute-start.7 = (bf16[2,400,256]{2,1,0:T(8,128)(2,1)S(1)}, bf16[2,400,256]{2,1,0:T(8,128)(2,1)}, u32[]{:S(2)}, u32[]{:S(2)}) collective-permute-start(bf16[2,400,256]{2,1,0:T(8,128)(2,1)S(1)} %pad_maximum_fusion.refs_0_), channel_id=1, source_target_pairs={{0,8},{8,16},{16,24},{24,0},{32,40},{40,48},{48,56},{56,32},{1,9},... | collective-permute-start | bytes 1228808 | tf_op jit(solution)/shard_map/ppermute | solution.py:491
  62.1 0.0 all-to-all-done.1.in_ref
  62.1 0.0 copy-done.3
  62.1 0.0 copy-done.4
  62.1 2.4 %finish_ssm.1 = (bf16[1,128,1024]{2,1,0:T(8,128)(2,1)}, f32[1,16,128]{2,1,0:T(8,128)}, bf16[8,2,16,128]{3,2,1,0:T(8,128)(2,1)S(1)}, f32[64,2,128]{2,1,0:T(2,128)}) custom-call(bf16[4,256,256]{2,1,0:T(8,128)(2,1)S(1)} %all-to-all-done.1.in_ref, bf16[1,128,1024]{2,1,0:T(8,128)(2,1)S(1)} %copy-done, bf16[1,128,1024]{2,1,0:T(8,128)(2,1)S(1)} %copy-done.1, ...), custom_call_target="tpu_custom_call" | custom-call | tf_op jit(solution)/shard_map/finish_ssm/pallas_call | solution.py:517
  64.5 11.1 %all_to_all.20 = bf16[8,2,16,128]{3,2,1,0:T(8,128)(2,1)S(1)} all-to-all(bf16[8,2,16,128]{3,2,1,0:T(8,128)(2,1)S(1)} %get-tuple-element.63), channel_id=1, replica_groups=mesh['dp'=8,'ctx'=8,'head'=8] {'head'}, dimensions={0} | all-to-all | bytes 131072 | tf_op jit(solution)/shard_map/all_to_all | solution.py:530
  75.6 16.5 %all-to-all-start.3 = ((f32[64,2,128]{2,1,0:T(2,128)}), f32[64,2,128]{2,1,0:T(2,128)S(1)}, u32[]{:S(2)}, u32[]{:S(2)}) async-start(f32[64,2,128]{2,1,0:T(2,128)} %get-tuple-element.65), calls=%async_computation.3 | async-start | bytes 131072 | tf_op jit(solution)/shard_map/all_to_all | solution.py:535
  92.2 0.0 collective-permute-done.9.refs_3_
  92.2 0.0 collective-permute-done.8.refs_2_
  92.2 0.0 collective-permute-done.7.refs_1_
  92.2 8.4 %attention.1 = (bf16[1,128,256]{2,1,0:T(8,128)(2,1)}, bf16[1,2,128,128]{3,2,1,0:T(8,128)(2,1)}) custom-call(s32[2]{0:T(128)S(1)} %pad_add_fusion.half_ref.place_ref, bf16[2,400,256]{2,1,0:T(8,128)(2,1)S(1)} %pad_maximum_fusion.refs_0_, bf16[2,400,256]{2,1,0:T(8,128)(2,1)} %collective-permute-done.7.refs_1_, ...), custom_call_target="tpu_custom_call" | custom-call | flops 2147483648 | bytes 4194304 | tf_op jit(solution)/shard_map/attention/pallas_call | solution.py:540
  100.6 0.6 convert_reduce_fusion
  101.2 0.0 all-to-all-done.3
  101.2 0.6 reduce_sum.19
  (5 shorter events, 0.1 us)
Async XLA Ops:
  4.2 5.1 %copy-start.5 = (bf16[1,128,256]{2,1,0:T(8,128)(2,1)S(1)}, bf16[1,128,256]{2,1,0:T(8,128)(2,1)}, u32[]{:S(2)}) copy-start(bf16[1,128,256]{2,1,0:T(8,128)(2,1)} %queries_ref.1) | copy-start | bytes 196612
  4.2 5.1 %copy-start.6 = (bf16[1,128,256]{2,1,0:T(8,128)(2,1)S(1)}, bf16[1,128,256]{2,1,0:T(8,128)(2,1)}, u32[]{:S(2)}) copy-start(bf16[1,128,256]{2,1,0:T(8,128)(2,1)} %grads_ref.1) | copy-start | bytes 196612
  4.2 5.0 %copy-start.7 = (bf16[1,2,128,128]{3,2,1,0:T(8,128)(2,1)S(1)}, bf16[1,2,128,128]{3,2,1,0:T(8,128)(2,1)}, u32[]{:S(2)}) copy-start(bf16[1,2,128,128]{3,2,1,0:T(8,128)(2,1)} %keyval_ref.1) | copy-start | bytes 196612
  4.2 5.0 %copy-start.9 = (s32[1,128]{1,0:T(1,128)S(1)}, s32[1,128]{1,0:T(1,128)}, u32[]{:S(2)}) copy-start(s32[1,128]{1,0:T(1,128)} %docs_ref.2) | copy-start | bytes 1540
  4.3 7.1 %copy-start = (bf16[1,128,1024]{2,1,0:T(8,128)(2,1)S(1)}, bf16[1,128,1024]{2,1,0:T(8,128)(2,1)}, u32[]{:S(2)}) copy-start(bf16[1,128,1024]{2,1,0:T(8,128)(2,1)} %x_ref.3) | copy-start | bytes 786436
  4.3 7.1 %copy-start.1 = (bf16[1,128,1024]{2,1,0:T(8,128)(2,1)S(1)}, bf16[1,128,1024]{2,1,0:T(8,128)(2,1)}, u32[]{:S(2)}) copy-start(bf16[1,128,1024]{2,1,0:T(8,128)(2,1)} %dy_ref.3) | copy-start | bytes 786436
  4.3 12.1 %all-to-all-start = ((bf16[4,272,256]{2,1,0:T(8,128)(2,1)}), bf16[4,272,256]{2,1,0:T(8,128)(2,1)S(1)}, u32[]{:S(2)}, u32[]{:S(2)}) async-start(bf16[4,272,256]{2,1,0:T(8,128)(2,1)} %get-tuple-element.42), calls=%async_computation | async-start | bytes 1114112 | tf_op jit(solution)/shard_map/all_to_all | solution.py:419
  9.3 2.1 %copy-start.2 = (bf16[1,2,128,128]{3,2,1,0:T(8,128)(2,1)S(1)}, bf16[1,2,128,128]{3,2,1,0:T(8,128)(2,1)}, u32[]{:S(2)}) copy-start(bf16[1,2,128,128]{3,2,1,0:T(8,128)(2,1)} %bc_ref.3) | copy-start | bytes 196612
  9.3 2.1 %copy-start.8 = (f32[1,16,128]{2,1,0:T(8,128)S(1)}, f32[1,16,128]{2,1,0:T(8,128)}, u32[]{:S(2)}) copy-start(f32[1,16,128]{2,1,0:T(8,128)} %step_ref) | copy-start | bytes 24580
  9.4 28.4 %collective-permute-start.1 = (bf16[128,256]{1,0:T(8,128)(2,1)S(1)}, bf16[128,256]{1,0:T(8,128)(2,1)S(1)}, u32[]{:S(2)}, u32[]{:S(2)}) collective-permute-start(bf16[128,256]{1,0:T(8,128)(2,1)S(1)} %get-tuple-element.49), channel_id=1, source_target_pairs={{32,64},{40,72},{48,80},{56,88},{96,128},{104,136},{112,144},{120,... | collective-permute-start | bytes 196616 | tf_op jit(solution)/shard_map/ppermute | solution.py:458
  10.0 1.4 %copy-start.10 = (f32[16]{0:T(128)S(1)}, f32[16]{0:T(128)}, u32[]{:S(2)}) copy-start(f32[16]{0:T(128)} %rate_ref.3) | copy-start | bytes 196
  10.0 1.4 %copy-start.11 = (f32[16]{0:T(128)S(1)}, f32[16]{0:T(128)}, u32[]{:S(2)}) copy-start(f32[16]{0:T(128)} %skip_ref.1) | copy-start | bytes 196
  10.0 29.0 %collective-permute-start.3 = (bf16[128,256]{1,0:T(8,128)(2,1)S(1)}, bf16[128,256]{1,0:T(8,128)(2,1)S(1)}, u32[]{:S(2)}, u32[]{:S(2)}) collective-permute-start(bf16[128,256]{1,0:T(8,128)(2,1)S(1)} %get-tuple-element.50), channel_id=1, source_target_pairs={{96,0},{104,8},{112,16},{120,24},{160,64},{168,72},{176,80},{184,8... | collective-permute-start | bytes 196616 | tf_op jit(solution)/shard_map/ppermute | solution.py:459
  17.2 25.8 %collective-permute-start = (bf16[144,256]{1,0:T(8,128)(2,1)S(1)}, bf16[144,256]{1,0:T(8,128)(2,1)S(1)}, u32[]{:S(2)}, u32[]{:S(2)}) collective-permute-start(bf16[144,256]{1,0:T(8,128)(2,1)S(1)} %half_totals.1), channel_id=1, source_target_pairs={{0,32},{8,40},{16,48},{24,56},{32,0},{40,8},{48,16},{56,24},{1,33}... | collective-permute-start | bytes 221192 | tf_op jit(solution)/shard_map/ppermute | solution.py:485
  34.5 18.2 %collective-permute-start.6 = (bf16[144,256]{1,0:T(8,128)(2,1)S(1)}, bf16[144,256]{1,0:T(8,128)(2,1)S(1)}, u32[]{:S(2)}, u32[]{:S(2)}) collective-permute-start(bf16[144,256]{1,0:T(8,128)(2,1)S(1)} %get-tuple-element.52), channel_id=1, source_target_pairs={{0,32},{8,40},{16,48},{24,56},{32,0},{40,8},{48,16},{56,24},{1,33}... | collective-permute-start | bytes 221192 | tf_op jit(solution)/shard_map/ppermute | solution.py:487
  36.4 16.2 %collective-permute-start.5 = (bf16[128,256]{1,0:T(8,128)(2,1)S(1)}, bf16[128,256]{1,0:T(8,128)(2,1)S(1)}, u32[]{:S(2)}, u32[]{:S(2)}) collective-permute-start(bf16[128,256]{1,0:T(8,128)(2,1)S(1)} %broadcast_select_fusion), channel_id=1, source_target_pairs={{32,0},{40,8},{48,16},{56,24},{480,448},{488,456},{496,464},{504,4... | collective-permute-start | bytes 196616 | tf_op jit(solution)/shard_map/ppermute | solution.py:457
  37.7 14.9 %collective-permute-start.2 = (bf16[128,256]{1,0:T(8,128)(2,1)S(1)}, bf16[128,256]{1,0:T(8,128)(2,1)S(1)}, u32[]{:S(2)}, u32[]{:S(2)}) collective-permute-start(bf16[128,256]{1,0:T(8,128)(2,1)S(1)} %collective-permute-done.1), channel_id=1, source_target_pairs={{64,0},{72,8},{80,16},{88,24},{128,64},{136,72},{144,80},{152,88},... | collective-permute-start | bytes 196616 | tf_op jit(solution)/shard_map/ppermute | solution.py:493
  39.0 13.6 %collective-permute-start.4 = (bf16[128,256]{1,0:T(8,128)(2,1)S(1)}, bf16[128,256]{1,0:T(8,128)(2,1)S(1)}, u32[]{:S(2)}, u32[]{:S(2)}) collective-permute-start(bf16[128,256]{1,0:T(8,128)(2,1)S(1)} %collective-permute-done.3), channel_id=1, source_target_pairs={{0,64},{8,72},{16,80},{24,88},{64,128},{72,136},{80,144},{88,152},... | collective-permute-start | bytes 196616 | tf_op jit(solution)/shard_map/ppermute | solution.py:494
  44.7 17.4 %all-to-all-start.1 = ((bf16[4,256,256]{2,1,0:T(8,128)(2,1)}), bf16[4,256,256]{2,1,0:T(8,128)(2,1)S(1)}, u32[]{:S(2)}, u32[]{:S(2)}) async-start(bf16[4,256,256]{2,1,0:T(8,128)(2,1)} %entering_states.1), calls=%async_computation.1 | async-start | bytes 1048576 | tf_op jit(solution)/shard_map/all_to_all | solution.py:419
  52.7 9.4 %copy-start.3 = (bf16[128,1024]{1,0:T(8,128)(2,1)S(1)}, bf16[128,1024]{1,0:T(8,128)(2,1)}, u32[]{:S(2)}) copy-start(bf16[128,1024]{1,0:T(8,128)(2,1)} %get-tuple-element.60.sin_ref) | copy-start | bytes 786436
  52.7 9.4 %copy-start.4 = (bf16[128,1024]{1,0:T(8,128)(2,1)S(1)}, bf16[128,1024]{1,0:T(8,128)(2,1)}, u32[]{:S(2)}) copy-start(bf16[128,1024]{1,0:T(8,128)(2,1)} %get-tuple-element.61.sgr_ref) | copy-start | bytes 786436
  52.8 39.4 %collective-permute-start.9 = (bf16[2,400,256]{2,1,0:T(8,128)(2,1)S(1)}, bf16[2,400,256]{2,1,0:T(8,128)(2,1)S(1)}, u32[]{:S(2)}, u32[]{:S(2)}) collective-permute-start(bf16[2,400,256]{2,1,0:T(8,128)(2,1)S(1)} %pad_maximum_fusion.refs_0_), channel_id=1, source_target_pairs={{0,24},{8,0},{16,8},{24,16},{32,56},{40,32},{48,40},{56,48},{1,25}... | collective-permute-start | bytes 1228808 | tf_op jit(solution)/shard_map/ppermute | solution.py:491
  57.0 35.2 %collective-permute-start.8 = (bf16[2,400,256]{2,1,0:T(8,128)(2,1)S(1)}, bf16[2,400,256]{2,1,0:T(8,128)(2,1)}, u32[]{:S(2)}, u32[]{:S(2)}) collective-permute-start(bf16[2,400,256]{2,1,0:T(8,128)(2,1)S(1)} %pad_maximum_fusion.refs_0_), channel_id=1, source_target_pairs={{0,16},{8,24},{16,0},{24,8},{32,48},{40,56},{48,32},{56,40},{1,17}... | collective-permute-start | bytes 1228808 | tf_op jit(solution)/shard_map/ppermute | solution.py:491
  59.3 32.9 %collective-permute-start.7 = (bf16[2,400,256]{2,1,0:T(8,128)(2,1)S(1)}, bf16[2,400,256]{2,1,0:T(8,128)(2,1)}, u32[]{:S(2)}, u32[]{:S(2)}) collective-permute-start(bf16[2,400,256]{2,1,0:T(8,128)(2,1)S(1)} %pad_maximum_fusion.refs_0_), channel_id=1, source_target_pairs={{0,8},{8,16},{16,24},{24,0},{32,40},{40,48},{48,56},{56,32},{1,9},... | collective-permute-start | bytes 1228808 | tf_op jit(solution)/shard_map/ppermute | solution.py:491
  75.6 25.6 %all-to-all-start.3 = ((f32[64,2,128]{2,1,0:T(2,128)}), f32[64,2,128]{2,1,0:T(2,128)S(1)}, u32[]{:S(2)}, u32[]{:S(2)}) async-start(f32[64,2,128]{2,1,0:T(2,128)} %get-tuple-element.65), calls=%async_computation.3 | async-start | bytes 131072 | tf_op jit(solution)/shard_map/all_to_all | solution.py:535
